TPU v7x, 512 devices: a whole 4x8x8 slice. The times are simulated.
512 devices in a mesh: lat: 32 (over y, z_lo), lon: 16 (over x, z_hi, core).
Axes of the slice: x: 4, y: 8, z: 8 (z_hi: 2, z_lo: 4; z = z_hi * 4 + z_lo), core: 2. Of those that a mesh axis runs over, the one named last changes fastest.
Arguments:
- state_field: bfloat16 [384, 1024, 384], P('lat', 'lon'), may hold values from -6 to 6
- mix_weight: bfloat16 [384, 384, 384], P('lat', 'lon'), may hold values from -0.3125 to 0.3125
- upsample_weight: bfloat16 [384, 1024], replicated, may hold values from -0.3125 to 0.3125
- upsample_bias: float32 [64], replicated, may hold values from -3 to 3
- conv_weight: bfloat16 [9, 64, 64], replicated, may hold values from -0.25 to 0.25
- conv_bias: float32 [64], replicated, may hold values from -3 to 3
Outputs:
- fine_field: bfloat16 [64, 1536, 4096], P(None, 'lat', 'lon')
All inputs are finite; a program needn't handle non-finite values.
Results may differ from a plain program's by a relative error of at most 0.012.
Values may be sent and summed in bfloat16 or wider, within the bound.
No kernel may reach another device: no remote copies, remote signals or barrier semaphores. Data moves between devices by JAX's collectives and lax.ppermute only.
A program may use at most 128 MiB of HBM per device.

v0:
```python
import math

import jax
import jax.numpy as jnp
from jax import lax
from jax.sharding import PartitionSpec as P

degree_block = 16


def extended(cells, sides, width):
    for axis, dim in sides:
        count = lax.axis_size(axis)
        head = lax.slice_in_dim(cells, 0, width, axis=dim)
        tail = lax.slice_in_dim(cells, cells.shape[dim] - width, cells.shape[dim], axis=dim)
        cells = jnp.concatenate(
            [
                lax.ppermute(tail, axis, [(i, (i + 1) % count) for i in range(count)]),
                cells,
                lax.ppermute(head, axis, [((i + 1) % count, i) for i in range(count)]),
            ],
            axis=dim,
        )
    return cells


def start_logs(degrees):
    values = []
    running_total = 0.0
    for order_value in range(degrees):
        if order_value > 0:
            running_total = running_total + math.log(
                (2.0 * order_value - 1.0) / (2.0 * order_value)
            )
        values.append(0.5 * (math.log((2.0 * order_value + 1.0) / (4.0 * math.pi)) + running_total))
    return values


def legendre_setup(orders, lat_count, degrees):
    order_float = orders.astype(jnp.float32)[:, None]
    colatitude = (jnp.arange(lat_count, dtype=jnp.float32) + 0.5) * (math.pi / lat_count)
    cosine = jnp.cos(colatitude)[None, :]
    log_sine = jnp.log(jnp.sin(colatitude))[None, :]
    log_table = jnp.asarray(start_logs(degrees), jnp.float32)
    selector = orders[:, None] == jnp.arange(degrees, dtype=jnp.int32)[None, :]
    log_base = jnp.sum(jnp.where(selector, log_table[None, :], 0.0), axis=1)[:, None]
    log_start = log_base + order_float * log_sine
    diagonal_start = jnp.where(log_start > -80.0, jnp.exp(jnp.maximum(log_start, -80.0)), 0.0)
    return (order_float, cosine, diagonal_start)


def legendre_block(loop_carry_state, first_degree, order_float, cosine, diagonal_start):
    previous, earlier = loop_carry_state
    row_list = []
    for step_index in range(degree_block):
        degree = (first_degree + step_index).astype(jnp.float32)
        above_diag = degree > order_float
        spacing = jnp.where(above_diag, degree * degree - order_float * order_float, 1.0)
        alpha_coef = jnp.where(
            above_diag, jnp.sqrt(jnp.maximum(4.0 * degree * degree - 1.0, 1.0) / spacing), 0.0
        )
        past_next = degree > order_float + 1.0
        previous_degree = degree - 1.0
        numerator = jnp.maximum(previous_degree * previous_degree - order_float * order_float, 0.0)
        beta_coef = jnp.where(
            past_next,
            jnp.sqrt(numerator / jnp.maximum(4.0 * previous_degree * previous_degree - 1.0, 1.0)),
            0.0,
        )
        current = alpha_coef * (cosine * previous - beta_coef * earlier) + jnp.where(
            degree == order_float, diagonal_start, 0.0
        )
        row_list.append(current)
        earlier = previous
        previous = current
    return ((previous, earlier), jnp.stack(row_list))


def quadrature(lat_count):
    colatitude = (jnp.arange(lat_count, dtype=jnp.float32) + 0.5) * (math.pi / lat_count)
    return jnp.sin(colatitude) * (math.pi / lat_count)


def legendre_tables(orders, lat_count, degrees):
    order_float, cosine, diagonal_start = legendre_setup(orders, lat_count, degrees)
    zeros_grid = jnp.zeros((orders.shape[0], lat_count), jnp.float32)
    weights = quadrature(lat_count)[None, None, :]

    def advance(loop_carry_state, first_degree):
        loop_carry_state, basis = legendre_block(
            loop_carry_state, first_degree, order_float, cosine, diagonal_start
        )
        return (
            loop_carry_state,
            ((weights * basis).astype(jnp.bfloat16), basis.astype(jnp.bfloat16)),
        )

    firsts = jnp.arange(0, degrees, degree_block, dtype=jnp.int32)
    _, (weighted_stack, plain_stack) = lax.scan(advance, (zeros_grid, zeros_grid), firsts)
    table_shape = (degrees, orders.shape[0], lat_count)
    return (weighted_stack.reshape(table_shape), plain_stack.reshape(table_shape))


def fourier_tables(lon_count, wave_count):
    longitude = jnp.arange(lon_count, dtype=jnp.int32)
    wave_index = jnp.arange(wave_count, dtype=jnp.int32)
    phase_index = longitude[:, None] * wave_index[None, :] % lon_count
    angles = phase_index.astype(jnp.float32) * (2.0 * math.pi / lon_count)
    step_scale = 2.0 * math.pi / lon_count
    forward = jnp.concatenate(
        [jnp.cos(angles) * step_scale, -jnp.sin(angles) * step_scale], axis=1
    ).astype(jnp.bfloat16)
    doubling = jnp.where(wave_index == 0, 1.0, 2.0).astype(jnp.float32)[:, None]
    inverse = jnp.concatenate(
        [jnp.cos(angles).T * doubling, -jnp.sin(angles).T * doubling], axis=0
    ).astype(jnp.bfloat16)
    return (forward, inverse)


def upsample(hidden, upsample_weight, upsample_bias):
    channels, row_count, col_count = hidden.shape
    fine_channels = upsample_bias.shape[0]
    projected = lax.dot_general(
        upsample_weight,
        hidden.reshape(channels, row_count * col_count),
        (((0,), (0,)), ((), ())),
        preferred_element_type=jnp.float32,
    )
    projected = (
        projected.reshape(fine_channels, 4, 4, row_count, col_count)
        + upsample_bias[:, None, None, None, None]
    )
    fine_grid = jax.nn.gelu(projected).astype(jnp.bfloat16)
    return jnp.transpose(fine_grid, (0, 3, 1, 4, 2)).reshape(
        fine_channels, 4 * row_count, 4 * col_count
    )


def convolve(framed, conv_weight, conv_bias, fine_grid):
    fine_channels, row_count, col_count = fine_grid.shape
    accumulated = jnp.zeros((fine_channels, row_count * col_count), jnp.float32)
    for tap_index in range(9):
        tap_row = tap_index // 3
        tap_col = tap_index % 3
        shifted = framed[:, tap_row : tap_row + row_count, tap_col : tap_col + col_count].reshape(
            fine_channels, row_count * col_count
        )
        accumulated = accumulated + jnp.dot(
            conv_weight[tap_index], shifted, preferred_element_type=jnp.float32
        )
    total = (
        fine_grid.astype(jnp.float32)
        + accumulated.reshape(fine_channels, row_count, col_count)
        + conv_bias[:, None, None]
    )
    return total.astype(jnp.bfloat16)


def local(state_field, mix_weight, upsample_weight, upsample_bias, conv_weight, conv_bias):
    lat_parts = lax.axis_size("lat")
    lon_parts = lax.axis_size("lon")
    state_first = jnp.transpose(state_field, (2, 0, 1))
    channels, lat_rows, lon_cols = state_first.shape
    lat_count = lat_rows * lat_parts
    lon_count = lon_cols * lon_parts
    mode_count = 2 * lat_count
    per_lat = 2 * lat_rows
    forward, inverse = fourier_tables(lon_count, lat_count)
    row_layout = lax.all_to_all(state_first, "lon", split_axis=0, concat_axis=2, tiled=True)
    local_channels = row_layout.shape[0]
    spectra = jnp.dot(
        row_layout.reshape(local_channels * lat_rows, lon_count),
        forward,
        preferred_element_type=jnp.float32,
    )
    spectra = spectra.astype(jnp.bfloat16).reshape(local_channels, lat_rows, mode_count)
    column_entries = lax.all_to_all(spectra, "lat", split_axis=2, concat_axis=1, tiled=True)
    orders = (lax.axis_index("lat") * per_lat + jnp.arange(per_lat, dtype=jnp.int32)) % lat_count
    forward_legendre_basis, inverse_legendre_basis = legendre_tables(orders, lat_count, lat_count)
    coeffs = jnp.einsum(
        "wxy,jyx->wjy", column_entries, forward_legendre_basis, preferred_element_type=jnp.float32
    ).astype(jnp.bfloat16)
    degree_layout = lax.all_to_all(coeffs, "lat", split_axis=1, concat_axis=2, tiled=True)
    zero_carry = jnp.zeros((local_channels, lat_rows, mode_count), jnp.float32)
    shard_piece = lax.all_gather(degree_layout, "lon", axis=0, tiled=True)
    weight_part = lax.slice_in_dim(mix_weight, 0, shard_piece.shape[0], axis=2)
    mixed_modes = (
        zero_carry
        + jnp.einsum("loi,ilk->olk", weight_part, shard_piece, preferred_element_type=jnp.float32)
    ).astype(jnp.bfloat16)
    returned_output = lax.all_to_all(mixed_modes, "lat", split_axis=2, concat_axis=1, tiled=True)
    synthesized = jnp.einsum(
        "smi,mih->shi", returned_output, inverse_legendre_basis, preferred_element_type=jnp.float32
    ).astype(jnp.bfloat16)
    gathered = lax.all_to_all(synthesized, "lat", split_axis=1, concat_axis=2, tiled=True)
    spatial = jnp.dot(
        gathered.reshape(local_channels * lat_rows, mode_count),
        inverse,
        preferred_element_type=jnp.float32,
    )
    spatial = spatial.reshape(local_channels, lat_rows, lon_count)
    hidden_rows = (row_layout.astype(jnp.float32) + jax.nn.gelu(spatial)).astype(jnp.bfloat16)
    hidden = lax.all_to_all(hidden_rows, "lon", split_axis=2, concat_axis=0, tiled=True)
    fine_grid = upsample(hidden, upsample_weight, upsample_bias)
    framed = extended(fine_grid, (("lat", 1), ("lon", 2)), 1)
    frame_rows = framed.shape[1]
    lat_position = lax.axis_index("lat")
    edge_rows = jnp.arange(frame_rows, dtype=jnp.int32)
    blank_rows = (edge_rows == 0) & (lat_position == 0) | (edge_rows == frame_rows - 1) & (
        lat_position == lat_parts - 1
    )
    framed = jnp.where(blank_rows[None, :, None], jnp.zeros((), jnp.bfloat16), framed)
    return convolve(framed, conv_weight, conv_bias, fine_grid)


def solution(mesh):
    placed = (P("lat", "lon", None), P("lat", "lon", None), P(), P(), P(), P())
    return jax.shard_map(
        local, mesh=mesh, in_specs=placed, out_specs=P(None, "lat", "lon"), check_vma=False
    )
```

profile of v0, /device:TPU:8, one launch (start us, length us, event | category | flops | bytes accessed | tf_op | source)
XLA Modules:
  0.0 833.9 jit_solution(17161465069114613419)
XLA Ops:
  10.5 12.8 %all-to-all-start = ((bf16[16,2,9216]{2,1,0:T(2,128)(2,1)}), bf16[16,2,9216]{2,1,0:T(2,128)(2,1)S(1)}, u32[]{:S(2)}, u32[]{:S(2)}) async-start(bf16[16,2,9216]{2,1,0:T(2,128)(2,1)} %reshape.1879), calls=%async_computation | async-start | bytes 1179648 | tf_op jit(solution)/shard_map/all_to_all | solution.py:169
  23.6 7.3 multiply_convert_fusion.3
  30.9 8.0 all-to-all-done
  52.2 5.5 reshape.1881
  57.7 15.7 %all-to-all-start.1 = ((bf16[32,2,3456]{2,1,0:T(2,128)(2,1)}), bf16[32,2,3456]{2,1,0:T(2,128)(2,1)S(1)}, u32[]{:S(2)}, u32[]{:S(2)}) async-start(bf16[32,2,3456]{2,1,0:T(2,128)(2,1)} %reshape.1881), calls=%async_computation.1 | async-start | bytes 884736 | tf_op jit(solution)/shard_map/all_to_all | solution.py:177
  73.6 365.9 %while.23 = (s32[]{:T(128)}, f32[24,384]{1,0:T(8,128)S(1)}, f32[24,384]{1,0:T(8,128)S(1)}, bf16[24,16,24,384]{3,2,1,0:T(8,128)(2,1)}, bf16[24,16,24,384]{3,2,1,0...) while((s32[]{:T(128)}, f32[24,384]{1,0:T(8,128)S(1)}, ...), condition=%wide.region_2.3_spmd.clone.clone.clone.clone, body=%wide.region_1.2_spmd.clone.clone.clone.clone.sunk | while | flops 2868497 | bytes 3636694 | solution.py:99
  439.5 4.7 reshape.1882
  444.2 4.9 copy.119
  452.5 5.6 fusion.129
  465.2 26.0 %all_to_all.99 = bf16[32,2,3456]{2,1,0:T(2,128)(2,1)S(1)} all-to-all(bf16[32,2,3456]{2,1,0:T(2,128)(2,1)S(1)} %reshape.1883), channel_id=1, replica_groups=mesh['lat'=32,'lon'=16] {'lat'}, dimensions={0} | all-to-all | bytes 884736 | tf_op jit(solution)/shard_map/all_to_all | solution.py:183
  495.5 5.7 copy.124
  501.2 4.9 all_to_all.82
  506.1 94.9 %all-gather.2.cloned.1.call-done = bf16[384,12,768]{2,0,1:T(8,128)(2,1)} async-done(((bf16[24,12,768]{2,0,1:T(8,128)(2,1)}), bf16[384,12,768]{2,0,1:T(8,128)(2,1)}) %all-gather.2.cloned.1.call-update) | async-done | bytes 7077904 | tf_op jit(solution)/shard_map/all_gather | solution.py:185
  608.8 4.8 reshape.1885
  613.7 25.1 %all_to_all.100 = bf16[32,2,3456]{2,1,0:T(2,128)(2,1)S(1)} all-to-all(bf16[32,2,3456]{2,1,0:T(2,128)(2,1)S(1)} %reshape.1885), channel_id=1, replica_groups=mesh['lat'=32,'lon'=16] {'lat'}, dimensions={0} | all-to-all | bytes 884736 | tf_op jit(solution)/shard_map/all_to_all | solution.py:191
  638.8 4.6 reshape.1886
  643.4 4.9 copy.127
  658.8 5.2 reshape.1887
  663.9 5.4 all-to-all-start.4
  669.4 7.7 multiply_convert_fusion.2
  679.3 5.4 all-to-all-done.4
  684.7 4.7 reshape.1888
  700.7 4.7 copy.133
  705.4 5.5 reshape.1889
  710.9 24.2 %all_to_all.101 = bf16[16,2,9216]{2,1,0:T(2,128)(2,1)S(1)} all-to-all(bf16[16,2,9216]{2,1,0:T(2,128)(2,1)S(1)} %reshape.1889), channel_id=1, replica_groups=mesh['lat'=32,'lon'=16] {'lon'}, dimensions={0} | all-to-all | bytes 1179648 | tf_op jit(solution)/shard_map/all_to_all | solution.py:203
  735.1 5.7 reshape.1890
  740.8 5.5 copy.134
  756.6 6.8 fusion.91
  763.3 8.6 %copy.136 = bf16[64,12,4,64,4]{0,4,3,2,1:T(4,128)(2,1)S(1)} copy(bf16[64,12,4,64,4]{3,1,4,2,0:T(8,128)(2,1)} %fusion.91) | data formatting | bytes 3145728 | tf_op jit(solution)/shard_map/transpose | solution.py:134
  775.8 4.7 collective-permute-start.1
  784.4 9.9 %collective-permute-start.3 = (bf16[64,50,1]{0,2,1:T(2,128)(2,1)S(1)}, bf16[64,50,1]{0,2,1:T(2,128)(2,1)S(1)}, u32[]{:S(2)}, u32[]{:S(2)}) collective-permute-start(bf16[64,50,1]{0,2,1:T(2,128)(2,1)S(1)} %get-tuple-element.536), channel_id=1, source_target_pairs={{1,0},{2,1},{3,2},{4,3},{5,4},{6,5},{7,6},{8,7},{9,8},{10,9},{11,1... | collective-permute-start | bytes 19208 | tf_op jit(solution)/shard_map/ppermute | solution.py:20
  801.3 7.3 fusion.174
  (1143 shorter events, 201.0 us)
Async XLA Ops:
  6.5 740.7 %copy-start = (bf16[384,1024]{1,0:T(8,128)(2,1)S(1)}, bf16[384,1024]{1,0:T(8,128)(2,1)}, u32[]{:S(2)}) copy-start(bf16[384,1024]{1,0:T(8,128)(2,1)} %param.11) | copy-start | bytes 2359300
  6.5 16.9 %copy-start.10 = (f32[384]{0:T(512)S(1)}, f32[384]{0:T(512)}, u32[]{:S(2)}) copy-start(f32[384]{0:T(512)} %constant.265.clone) | copy-start | bytes 4612
  10.5 28.5 %all-to-all-start = ((bf16[16,2,9216]{2,1,0:T(2,128)(2,1)}), bf16[16,2,9216]{2,1,0:T(2,128)(2,1)S(1)}, u32[]{:S(2)}, u32[]{:S(2)}) async-start(bf16[16,2,9216]{2,1,0:T(2,128)(2,1)} %reshape.1879), calls=%async_computation | async-start | bytes 1179648 | tf_op jit(solution)/shard_map/all_to_all | solution.py:169
  39.9 4.5 copy-start.7
  57.7 381.9 %all-to-all-start.1 = ((bf16[32,2,3456]{2,1,0:T(2,128)(2,1)}), bf16[32,2,3456]{2,1,0:T(2,128)(2,1)S(1)}, u32[]{:S(2)}, u32[]{:S(2)}) async-start(bf16[32,2,3456]{2,1,0:T(2,128)(2,1)} %reshape.1881), calls=%async_computation.1 | async-start | bytes 884736 | tf_op jit(solution)/shard_map/all_to_all | solution.py:177
  73.4 527.6 %all-gather.2.cloned.1.call-start = ((), (), s32[]{:S(2)}) async-start(), calls=%async_computation.6 | async-start | bytes 7520256 | tf_op jit(solution)/shard_map/all_gather | solution.py:185
  495.5 105.5 %copy-start.8 = (bf16[12,24,384]{2,1,0:T(8,128)(2,1)S(1)}, bf16[12,24,384]{2,1,0:T(8,128)(2,1)}, u32[]{:S(2)}) copy-start(bf16[12,24,384]{2,1,0:T(8,128)(2,1)} %param.10) | copy-start | bytes 663556
  663.9 20.8 %all-to-all-start.4 = ((bf16[32,2,3456]{2,1,0:T(2,128)(2,1)}), bf16[32,2,3456]{2,1,0:T(2,128)(2,1)}, u32[]{:S(2)}, u32[]{:S(2)}) async-start(bf16[32,2,3456]{2,1,0:T(2,128)(2,1)} %reshape.1887), calls=%async_computation.4 | async-start | bytes 884736 | tf_op jit(solution)/shard_map/all_to_all | solution.py:195
  752.2 4.3 copy-start.11
  772.0 9.0 %collective-permute-start = (bf16[64,1,256]{0,2,1:T(8,128)(2,1)S(1)}, bf16[64,1,256]{0,2,1:T(8,128)(2,1)S(1)}, u32[]{:S(2)}, u32[]{:S(2)}) collective-permute-start(bf16[64,1,256]{0,2,1:T(8,128)(2,1)S(1)} %get-tuple-element.537), channel_id=1, source_target_pairs={{0,16},{16,32},{32,48},{48,64},{64,80},{80,96},{96,112},{112,128},... | collective-permute-start | bytes 98312 | tf_op jit(solution)/shard_map/ppermute | solution.py:18
  775.8 6.6 collective-permute-start.1
  782.5 15.0 %collective-permute-start.2 = (bf16[64,50,1]{0,2,1:T(2,128)(2,1)S(1)}, bf16[64,50,1]{0,2,1:T(2,128)(2,1)S(1)}, u32[]{:S(2)}, u32[]{:S(2)}) collective-permute-start(bf16[64,50,1]{0,2,1:T(2,128)(2,1)S(1)} %get-tuple-element.535), channel_id=1, source_target_pairs={{0,1},{1,2},{2,3},{3,4},{4,5},{5,6},{6,7},{7,8},{8,9},{9,10},{10,1... | collective-permute-start | bytes 19208 | tf_op jit(solution)/shard_map/ppermute | solution.py:18
  784.4 13.1 %collective-permute-start.3 = (bf16[64,50,1]{0,2,1:T(2,128)(2,1)S(1)}, bf16[64,50,1]{0,2,1:T(2,128)(2,1)S(1)}, u32[]{:S(2)}, u32[]{:S(2)}) collective-permute-start(bf16[64,50,1]{0,2,1:T(2,128)(2,1)S(1)} %get-tuple-element.536), channel_id=1, source_target_pairs={{1,0},{2,1},{3,2},{4,3},{5,4},{6,5},{7,6},{8,7},{9,8},{10,9},{11,1... | collective-permute-start | bytes 19208 | tf_op jit(solution)/shard_map/ppermute | solution.py:20
  801.2 7.4 copy-start.9
  808.6 3.3 copy-start.5
  811.9 1.9 copy-start.4
  813.8 1.9 copy-start.3
  815.6 1.9 copy-start.2
  823.6 1.4 copy-start.6
  823.6 1.4 copy-start.12
  823.6 3.0 copy-start.1
Sparse Core Ops, SparseCore 0:
  506.2 94.7 all-gather.1
where the time goes:
time: 846 us; the launch traced here: 834 us
  loops' own time  272 us (32%)
  local copies, waits for them, and re-layouts  167 us (20%)
  waiting for transfers between devices  110 us (13%)
  other arithmetic  106 us (13%)
  blocking collectives  75.2 us (9%)
  starting transfers between devices  54.6 us (6%)
  matrix products  35 us (4%)
  between operations  14.2 us (2%)
    another operation x1, loops' own time, legendre_tables(): lax.scan(advance, (zeros_grid, zeros_grid), firsts)  272 us
    all_gather x1, waiting for transfers between devices, local(): shard_piece = lax.all_gather(degree_layout, 'lon', axis=0, tiled=True)  94.9 us
    unnamed x40, local copies, waits for them, and re-layouts  57.9 us
    while x360, other arithmetic  34.4 us
    all_to_all x1, blocking collectives, local(): lax.all_to_all(coeffs, 'lat', split_axis=1, concat_axis=2, tiled=True)  26 us
    all_to_all x1, blocking collectives, local(): lax.all_to_all(mixed_modes, 'lat', split_axis=2, concat_axis=1, tiled=True)  25.1 us
    all_to_all x1, blocking collectives, local(): lax.all_to_all(hidden_rows, 'lon', split_axis=2, concat_axis=0, tiled=True)  24.2 us
    dynamic_update_slice x24, other arithmetic, legendre_tables(): lax.scan(advance, (zeros_grid, zeros_grid), firsts)  21.8 us
  transfers between devices with their start and end apart: 8, of which 5 were waited for; matrix products, arithmetic and copies ran while one was open for 14% of the time, Pallas kernels for 0%

commit v1 on v0

v1 whole, which is shorter than its diff:
```python
import math

import jax
import jax.numpy as jnp
from jax import lax
from jax.experimental import pallas as pl
from jax.experimental.pallas import tpu as pltpu
from jax.sharding import Mesh
from jax.sharding import PartitionSpec as P

f32 = jnp.float32
bf16 = jnp.bfloat16
MIB = 1 << 20


def call(kernel, out, *args, scratch=(), flops=0, smem=(), vmem=40):
    space = [
        pl.BlockSpec(memory_space=pltpu.SMEM if i in smem else pltpu.VMEM) for i in range(len(args))
    ]
    outs = out if isinstance(out, (tuple, list)) else (out,)
    moved = sum(x.size * x.dtype.itemsize for x in (*args, *outs))
    return pl.pallas_call(
        kernel,
        out_shape=out,
        in_specs=space,
        out_specs=jax.tree.map(lambda _: pl.BlockSpec(memory_space=pltpu.VMEM), out),
        scratch_shapes=list(scratch),
        compiler_params=pltpu.CompilerParams(vmem_limit_bytes=vmem * MIB),
        cost_estimate=pl.CostEstimate(flops=flops, bytes_accessed=moved, transcendentals=0),
    )(*args)


def shape(dims, dtype=bf16):
    return jax.ShapeDtypeStruct(dims, dtype)


def iota(dims, axis):
    return lax.broadcasted_iota(jnp.int32, dims, axis)


def widen():
    row, col = iota((384, 512), 0), iota((384, 512), 1)
    return jnp.where((col % 128 < 96) & (row == col // 128 * 96 + col % 128), 1.0, 0.0).astype(bf16)


def dot(a, b):
    return jnp.dot(a, b, preferred_element_type=f32)


def dot_nt(a, b):
    return lax.dot_general(a, b, (((1,), (1,)), ((), ())), preferred_element_type=f32)


def pack_kernel(x_ref, s_ref):
    spread = widen()
    for a in range(12):
        wide = dot(x_ref[a], spread).astype(bf16)
        for b in range(4):
            s_ref[
                pl.ds((a // 3 * 4 + b) * 64, 64), pl.ds(a % 3 * 128, 128)
            ] = wide[:, b * 128 : (b + 1) * 128]


def dft_tables_kernel(p_ref, q_ref, cb_ref, sb_ref, pt_ref, qt_ref, cbt_ref, sbt_ref, c_ref, g_ref):
    for b in range(8):
        c_ref[:, pl.ds(b * 128, 128)] = (
            p_ref[...] * cb_ref[:, b : b + 1] - q_ref[...] * sb_ref[:, b : b + 1]
        ).astype(bf16)
        g_ref[pl.ds(b * 128, 128), :] = (
            pt_ref[...] * cbt_ref[b : b + 1, :] - qt_ref[...] * sbt_ref[b : b + 1, :]
        ).astype(bf16)


def dft_kernel(c_ref, x_ref, w_ref, s_ref):
    for block in range(4):
        rows = pl.ds(block * 256, 256)
        s_ref[rows, :] = (dot(c_ref[rows, :], x_ref[...]) * w_ref[...]).astype(bf16)


def legendre_tables_kernel(order_ref, cosine_ref, start_ref, l_ref, t_ref, rows_ref):
    order = order_ref[...]
    squared = order * order
    rows_ref[...] = jnp.zeros(rows_ref.shape, f32)

    def step(l, carry):
        previous, earlier = carry
        degree = l.astype(f32)
        above = degree > order
        spacing = jnp.where(above, degree * degree - squared, 1.0)
        alpha = jnp.where(
            above, jnp.sqrt(jnp.maximum(4.0 * degree * degree - 1.0, 1.0) / spacing), 0.0
        )
        below = degree - 1.0
        beta = jnp.where(
            degree > order + 1.0,
            jnp.sqrt(
                jnp.maximum(below * below - squared, 0.0)
                / jnp.maximum(4.0 * below * below - 1.0, 1.0)
            ),
            0.0,
        )
        first = degree == order
        current = []
        for t in range(3):
            lanes = pl.ds(t * 128, 128)
            value = alpha * (cosine_ref[:, lanes] * previous[t] - beta * earlier[t]) + jnp.where(
                first, start_ref[:, lanes], 0.0
            )
            rows_ref[t, pl.ds(pl.multiple_of(l * 8, 8), 8), :] = value
            current.append(value)
        return (tuple(current), previous)

    zeros = (jnp.zeros((8, 128), f32),) * 3

    def block(i, carry):
        for u in range(8):
            carry = step(i * 8 + u, carry)
        return carry

    lax.fori_loop(0, 48, block, (zeros, zeros))
    for m3 in range(3):
        for t in range(3):
            parts = [rows_ref[t, pl.ds(r * 8 + m3, 128, stride=24), :] for r in range(3)]
            table = jnp.concatenate(parts, axis=0)
            l_ref[m3, :, pl.ds(t * 128, 128)] = table.astype(bf16)
            t_ref[m3, pl.ds(t * 128, 128), :] = table.T.astype(bf16)


def legendre_kernel(x_ref, l_ref, s_ref, in_ref, out_ref):
    for t in range(3):
        in_ref[t] = x_ref[:, t * 128 : (t + 1) * 128].astype(f32)
    out_ref[...] = jnp.zeros(out_ref.shape, f32)
    for m3 in range(3):
        halves = [
            jnp.concatenate(
                [in_ref[t, pl.ds(cs * 3 + m3, 128, stride=8), :] for t in range(3)], axis=0
            )
            for cs in range(2)
        ]
        result = dot(l_ref[m3], jnp.concatenate(halves, axis=1).astype(bf16))
        for t in range(3):
            for cs in range(2):
                out_ref[t, pl.ds(cs * 3 + m3, 128, stride=8), :] = result[
                    t * 128 : (t + 1) * 128, cs * 128 : (cs + 1) * 128
                ]
    for t in range(3):
        s_ref[:, pl.ds(t * 128, 128)] = out_ref[t].astype(bf16)


def mix_weight_kernel(first_ref, w_ref, o_ref):
    del first_ref
    part = w_ref[...].astype(f32).reshape(384, 384).astype(bf16)
    wide = dot(part, widen()).astype(bf16)
    o_ref[...] = jnp.zeros(o_ref.shape, bf16)
    for b in range(4):
        o_ref[0, pl.ds(b * 128, 96), :] = wide[b * 96 : (b + 1) * 96]


def spread_mix_weight(gathered, first):
    return pl.pallas_call(
        mix_weight_kernel,
        out_shape=shape((3, 512, 512)),
        grid_spec=pltpu.PrefetchScalarGridSpec(
            num_scalar_prefetch=1,
            grid=(3,),
            in_specs=[pl.BlockSpec((16, 1, 24, 384), lambda r, first: (0, first[0] + r, 0, 0))],
            out_specs=pl.BlockSpec((1, 512, 512), lambda r, first: (r, 0, 0)),
        ),
        compiler_params=pltpu.CompilerParams(vmem_limit_bytes=24 * MIB),
        cost_estimate=pl.CostEstimate(flops=10**9, bytes_accessed=3 * 10**6, transcendentals=0),
    )(first, gathered)


def mix_kernel(x_ref, w_ref, s_ref):
    for r in range(3):
        lanes = pl.ds(r * 128, 128)
        part = x_ref[:, lanes].astype(f32).reshape(32, 4, 8, 128)
        modes = jnp.concatenate([part[:, b].reshape(256, 128) for b in range(4)], axis=1)
        mixed = dot_nt(modes.astype(bf16), w_ref[r])
        back = [mixed[:, b * 128 : (b + 1) * 128].reshape(32, 1, 8, 128) for b in range(4)]
        s_ref[:, lanes] = jnp.concatenate(back, axis=1).reshape(1024, 128).astype(bf16)


def inverse_kernel(g_ref, x_ref, state_ref, s_ref, h_ref):
    for block in range(4):
        rows = pl.ds(block * 256, 256)
        spatial = dot(g_ref[rows, :], x_ref[...])
        hidden = (state_ref[rows, :].astype(f32) + jax.nn.gelu(spatial)).astype(bf16)
        h_ref[rows, :] = hidden.astype(f32)
        for part in range(4):
            s_ref[pl.ds((block * 4 + part) * 80, 64), :] = hidden[part * 64 : (part + 1) * 64]
    row = iota((16, 384), 0)
    for q in range(16):
        right = h_ref[pl.ds((q + 1) % 16 * 64, 1), :]
        left = h_ref[pl.ds((q * 64 + 1023) % 1024, 1), :]
        edge = jnp.where(row == 0, right, jnp.where(row == 15, left, 0.0))
        s_ref[pl.ds(q * 80 + 64, 16), :] = edge.astype(bf16)


def tail_weights_kernel(u_ref, w_ref, o_ref, c_ref):
    o_ref[...] = jnp.zeros(o_ref.shape, bf16)
    row, col = iota((1024, 256), 0), iota((1024, 256), 1)
    for q in range(4):
        pick = jnp.where(row == 16 * (col % 64) + 4 * (col // 64) + q, 1.0, 0.0).astype(bf16)
        part = dot(u_ref[...], pick).astype(bf16)
        for b in range(4):
            o_ref[pl.ds(b * 128, 96), pl.ds(q * 256, 256)] = part[b * 96 : (b + 1) * 96]
    for ds in range(3):
        for p in range(4):
            blocks = []
            for window in (0, 1, 2, 3, 4, -1):
                dr = window - p
                if -1 <= dr <= 1:
                    blocks.append(w_ref[3 * (dr + 1) + ds].astype(f32))
                else:
                    blocks.append(jnp.zeros((64, 64), f32))
            c_ref[ds, pl.ds(p * 64, 64), :] = jnp.concatenate(blocks, axis=1).astype(bf16)


def fine_kernel(x_ref, u_ref, bias_ref, o_ref, h_ref):
    for a in range(12):
        for b in range(4):
            h_ref[pl.ds(a * 80, 80), pl.ds(b * 128, 128)] = x_ref[
                pl.ds((a // 3 * 4 + b) * 80, 80), pl.ds(a % 3 * 128, 128)
            ]
    for q in range(4):
        lanes = pl.ds(q * 256, 256)
        for block in range(4):
            rows = pl.ds(block * 240, 240)
            value = dot(h_ref[rows, :], u_ref[:, lanes]) + bias_ref[:, lanes]
            o_ref[q, rows, :] = jax.nn.gelu(value).astype(bf16)


def conv_kernel(
    ends_ref, f_ref, up_ref, down_ref, u_ref, bias_ref, w_ref, cb_ref, o_ref,
    h_ref, e_ref, t_ref, s_ref, z_ref, g_ref,
):
    for b in range(4):
        lanes = pl.ds(b * 128, 128)
        h_ref[pl.ds(0, 80), lanes] = up_ref[pl.ds(b * 80, 80), :]
        h_ref[pl.ds(80, 80), lanes] = down_ref[pl.ds(b * 80, 80), :]
    first = iota((160, 256), 0) < 80
    keep = jnp.where(first, ends_ref[0], ends_ref[1]) > 0
    half = iota((80, 128), 1) < 64
    for q in range(4):
        lanes = pl.ds(q * 256, 256)
        value = jax.nn.gelu(dot(h_ref[...], u_ref[:, lanes]) + bias_ref[:, lanes])
        e_ref[...] = jnp.where(keep, value, 0.0).astype(bf16)
        for a in range(12):
            below = e_ref[pl.ds(80, 80), 0:128] if a == 11 else f_ref[q, pl.ds(a * 80 + 80, 80), 0:128]
            above = e_ref[pl.ds(0, 80), 128:256] if a == 0 else f_ref[q, pl.ds(a * 80 - 80, 80), 128:256]
            t_ref[q, pl.ds(a * 80, 80), :] = jnp.where(half, below, above)
    for side, q, amount in ((0, 3, 1), (1, 0, 79)):
        for a in range(12):
            rows = pl.ds(a * 80, 80)
            for t in range(3):
                part = t_ref[q, rows, :] if t == 2 else f_ref[q, rows, t * 128 : (t + 1) * 128]
                s_ref[side, rows, pl.ds(t * 128, 128)] = pltpu.roll(
                    part.astype(f32), amount, 0
                ).astype(bf16)
    for q in range(4):
        total = f_ref[q].astype(f32) + cb_ref[...]
        for ds in range(3):
            source = q + ds - 1
            if 0 <= source < 4:
                total = total + dot_nt(f_ref[source], w_ref[ds, :, 0:256])
                total = total + dot_nt(t_ref[source], w_ref[ds, :, 256:384])
            else:
                total = total + dot_nt(s_ref[0 if source < 0 else 1], w_ref[ds])
        z_ref[q] = total.astype(bf16)
    row, col = iota((256, 256), 0), iota((256, 256), 1)
    place = jnp.where(col == 4 * (row % 64) + row // 64, 1.0, 0.0).astype(bf16)
    for a in range(12):
        cells = jnp.concatenate([z_ref[q, pl.ds(a * 80, 64), :] for q in range(4)], axis=0)
        lines = lax.dot_general(cells, place, (((0,), (0,)), ((), ())), preferred_element_type=f32)
        for p in range(4):
            for t in range(2):
                g_ref[t, pl.ds(4 * a + p, 64, stride=48), :] = lines[
                    p * 64 : (p + 1) * 64, t * 128 : (t + 1) * 128
                ]
    for t in range(2):
        o_ref[:, :, pl.ds(t * 128, 128)] = g_ref[t].reshape(64, 48, 128).astype(bf16)


def start_logs(degrees):
    values = []
    total = 0.0
    for m in range(degrees):
        if m > 0:
            total = total + math.log((2.0 * m - 1.0) / (2.0 * m))
        values.append(0.5 * (math.log((2.0 * m + 1.0) / (4.0 * math.pi)) + total))
    return values


def legendre_tables(n):
    order = 3 * n + jnp.arange(8, dtype=jnp.int32)
    lane = jnp.arange(384, dtype=jnp.int32)
    colatitude = ((3 * (lane % 128) + lane // 128).astype(f32) + 0.5) * (math.pi / 384)
    cosine = jnp.broadcast_to(jnp.cos(colatitude)[None, :], (8, 384))
    log_sine = jnp.log(jnp.sin(colatitude))[None, :]
    logs = jnp.asarray(start_logs(384), f32)
    log_base = jnp.sum(jnp.where(order[:, None] == lane[None, :], logs[None, :], 0.0), axis=1)
    log_start = log_base[:, None] + order.astype(f32)[:, None] * log_sine
    start = jnp.where(log_start > -80.0, jnp.exp(jnp.maximum(log_start, -80.0)), 0.0)
    orders = jnp.broadcast_to(order.astype(f32)[:, None], (8, 128))
    return call(
        legendre_tables_kernel,
        (shape((3, 384, 384)), shape((3, 384, 384))),
        orders,
        cosine,
        start,
        scratch=[pltpu.VMEM((3, 3072, 128), f32)],
        flops=4 * 10**9,
    )


def dft_tables():
    step = 2.0 * math.pi / 1024

    def base(row_axis, dims):
        k, y = iota(dims, row_axis), iota(dims, 1 - row_axis)
        j = k % 8
        wave = 3 * (k // 8) + j % 3
        used = j < 6
        angle = ((wave * y + jnp.where(j < 3, 0, 256)) % 1024).astype(f32) * step
        scale = jnp.where(used, 1.0, 0.0)
        if row_axis == 1:
            scale = scale * jnp.where(wave == 0, 1.0, 2.0)
        turn = (wave * y % 8).astype(f32) * (math.pi / 4)
        return jnp.cos(angle) * scale, jnp.sin(angle) * scale, turn

    p, q, _ = base(0, (1024, 128))
    turn = base(0, (1024, 8))[2]
    pt, qt, _ = base(1, (128, 1024))
    turn_t = base(1, (8, 1024))[2]
    return call(
        dft_tables_kernel,
        (shape((1024, 1024)), shape((1024, 1024))),
        p, q, jnp.cos(turn), jnp.sin(turn), pt, qt, jnp.cos(turn_t), jnp.sin(turn_t),
        flops=4 * 10**9,
    )


def exchange(x, axes):
    return lax.all_to_all(x, axes, 0, 0, tiled=True)


def local(state_field, mix_weight, upsample_weight, upsample_bias, conv_weight, conv_bias):
    lat, qa, qb = lax.axis_index("lat"), lax.axis_index("qa"), lax.axis_index("qb")
    n = 4 * lat + qa
    gathered = lax.all_gather(mix_weight, ("qa", "qb"), axis=0)
    packed = call(pack_kernel, shape((1024, 384)), state_field, flops=10**9)
    state = exchange(packed, ("qa", "qb"))
    forward, inverse = dft_tables()
    colatitude = ((3 * n + jnp.arange(384, dtype=jnp.int32) // 128).astype(f32) + 0.5) * (
        math.pi / 384
    )
    scale = (jnp.sin(colatitude) * (math.pi / 384) * (2.0 * math.pi / 1024))[None, :]
    spectra = call(dft_kernel, shape((1024, 384)), forward, state, scale, flops=10**9)
    columns = exchange(spectra, ("lat", "qa"))
    basis, basis_t = legendre_tables(n)
    scratch = [pltpu.VMEM((3, 1024, 128), f32)] * 2
    coeffs = call(legendre_kernel, shape((1024, 384)), columns, basis, scratch=scratch, flops=10**9)
    degrees = exchange(coeffs, ("lat", "qb"))
    mixer = spread_mix_weight(gathered, (3 * qb).reshape(1).astype(jnp.int32))
    mixed = call(mix_kernel, shape((1024, 384)), degrees, mixer, flops=10**9)
    returned = exchange(mixed, ("lat", "qb"))
    synthesized = call(
        legendre_kernel, shape((1024, 384)), returned, basis_t, scratch=scratch, flops=10**9
    )
    modes = exchange(synthesized, ("lat", "qa"))
    hidden = call(
        inverse_kernel,
        shape((1280, 384)),
        inverse,
        modes,
        state,
        scratch=[pltpu.VMEM((1024, 384), f32)],
        flops=10**9,
    )
    cells = exchange(hidden, ("qa", "qb"))
    spread_up, spread_conv = call(
        tail_weights_kernel,
        (shape((512, 1024)), shape((3, 256, 384))),
        upsample_weight,
        conv_weight,
        flops=2 * 10**9,
    )
    first_row = cells[0:320, 0:128]
    last_row = cells[960:1280, 256:384]
    count = lax.axis_size("lat")
    up = lax.ppermute(last_row, "lat", [(i, i + 1) for i in range(count - 1)])
    down = lax.ppermute(first_row, "lat", [(i + 1, i) for i in range(count - 1)])
    bias = jnp.tile(upsample_bias, 16)[None, :]
    fine = call(
        fine_kernel,
        shape((4, 960, 256)),
        cells,
        spread_up,
        bias,
        scratch=[pltpu.VMEM((960, 512), bf16)],
        flops=10**10,
    )
    ends = jnp.stack([lat > 0, lat < count - 1]).astype(jnp.int32)
    return call(
        conv_kernel,
        shape((64, 48, 256)),
        ends,
        fine,
        up,
        down,
        spread_up,
        bias,
        spread_conv,
        jnp.tile(conv_bias, 4)[None, :],
        smem=(0,),
        scratch=[
            pltpu.VMEM((160, 512), bf16),
            pltpu.VMEM((160, 256), bf16),
            pltpu.VMEM((4, 960, 128), bf16),
            pltpu.VMEM((2, 960, 384), bf16),
            pltpu.VMEM((4, 960, 256), bf16),
            pltpu.VMEM((2, 3072, 128), f32),
        ],
        flops=10**10,
    )


def solution(mesh):
    fine_mesh = Mesh(mesh.devices.reshape(32, 4, 4), ("lat", "qa", "qb"))
    rows = P("lat", ("qa", "qb"), None)
    return jax.shard_map(
        local,
        mesh=fine_mesh,
        in_specs=(rows, rows, P(), P(), P(), P()),
        out_specs=P(None, "lat", ("qa", "qb")),
        check_vma=False,
    )
```

time: 846 us -> 276 us (0.33); the launches traced: 834 us -> 275 us
  loops' own time: 272 us -> 0 us
  local copies, waits for them, and re-layouts: 167 us -> 14.9 us
  other arithmetic: 106 us -> 7.44 us
  matrix products: 35 us -> 0 us
  Pallas kernels: 0 us -> 28.8 us
  waiting for transfers between devices: 110 us -> 85 us
  blocking collectives: 75.2 us -> 63.4 us
    another operation x1 -> x0, loops' own time: 272 us -> none  [legendre_tables(): lax.scan(advance, (zeros_grid, zeros_grid), firsts)]
    all_gather x1, waiting for transfers between devices: 94.9 us -> 0.02 us  [local(): gathered = lax.all_gather(mix_weight, ('qa', 'qb'), axis=0)]
    all_to_all x3 -> x4, waiting for transfers between devices: 13.4 us -> 84 us  [exchange(): return lax.all_to_all(x, axes, 0, 0, tiled=True)]
    unnamed x40 -> x34, local copies, waits for them, and re-layouts: 57.9 us -> 14.4 us
    all_to_all x10 -> x0, local copies, waits for them, and re-layouts: 39 us -> none  [the longest x2 10.5 us: local(): lax.all_to_all(coeffs, 'lat', split_axis=1, concat_axis=2, tiled=True)]
    dot_general x15 -> x0, matrix products: 35 us -> none  [the longest x9 12.9 us: convolve(): jnp.dot(conv_weight[tap_index], shifted, preferred_element_type=jnp.float32)]
    while x360 -> x0, other arithmetic: 34.4 us -> none
    pallas_call x0 -> x12, Pallas kernels: none -> 28.8 us  [the longest x11 27.5 us: call(): pl.pallas_call(kernel, out_shape=out, in_specs=space, out_specs=jax.tree....]
  transfers between devices with their start and end apart: 8 -> 7, of which waited for: 5 -> 5; matrix products, arithmetic and copies ran while one was open for 14% -> 3% of each run, Pallas kernels for 0% -> 6%
where the time goes in v1:
time: 276 us; the launch traced here: 275 us
  waiting for transfers between devices  85 us (31%)
  blocking collectives  63.4 us (23%)
  starting transfers between devices  61.8 us (22%)
  Pallas kernels  28.8 us (10%)
  local copies, waits for them, and re-layouts  14.9 us (5%)
  between operations  13.7 us (5%)
  other arithmetic  7.44 us (3%)
    all_to_all x4, waiting for transfers between devices, exchange(): return lax.all_to_all(x, axes, 0, 0, tiled=True)  84 us
    all_to_all x2, blocking collectives, exchange(): return lax.all_to_all(x, axes, 0, 0, tiled=True)  63.4 us
    all_to_all x4, starting transfers between devices, exchange(): return lax.all_to_all(x, axes, 0, 0, tiled=True)  53.2 us
    pallas_call x11, Pallas kernels, call(): pl.pallas_call(kernel, out_shape=out, in_specs=space, out_specs=jax.tree....  27.5 us
    unnamed x34, local copies, waits for them, and re-layouts  14.4 us
  transfers between devices with their start and end apart: 7, of which 5 were waited for; matrix products, arithmetic and copies ran while one was open for 3% of the time, Pallas kernels for 6%

profile of v1, /device:TPU:8, one launch (start us, length us, event | category | flops | bytes accessed | tf_op | source)
XLA Modules:
  0.0 275.0 jit_solution(1435841473614456219)
XLA Ops:
  8.3 1.9 shard_map.74
  10.2 12.8 %all-to-all-start = ((bf16[16,64,384]{2,1,0:T(8,128)(2,1)}), bf16[16,64,384]{2,1,0:T(8,128)(2,1)S(1)}, u32[]{:S(2)}, u32[]{:S(2)}) async-start(bf16[16,64,384]{2,1,0:T(8,128)(2,1)} %bitcast.2), calls=%async_computation | async-start | bytes 1572864 | tf_op jit(solution)/shard_map/all_to_all | solution.py:345
  23.6 2.7 select_multiply_fusion
  26.3 2.2 sine_multiply_fusion
  28.4 1.9 multiply_sine_fusion
  30.3 3.1 %shard_map.73 = (bf16[1024,1024]{1,0:T(8,128)(2,1)S(1)}, bf16[1024,1024]{1,0:T(8,128)(2,1)S(1)}) custom-call(f32[1024,128]{1,0:T(8,128)S(1)} %get-tuple-element.26.p_ref, f32[1024,128]{1,0:T(8,128)S(1)} %get-tuple-element.25.q_ref, f32[1024,8]{1,0:T(8,128)S(1)} %get-tuple-element.20.cb_ref, f32[1024,8]{1,0:T(8,128)S(1)} %get-tuple-element.19.sb_ref, ...), custom_call_target="tpu_custom_call" | custom-call | flops 4000000000 | bytes 6422528 | tf_op jit(solution)/shard_map/pallas_call | solution.py:22
  33.4 1.3 copy-done.8
  34.7 7.1 %all-to-all-done = bf16[16,64,384]{2,1,0:T(8,128)(2,1)S(1)} async-done(((bf16[16,64,384]{2,1,0:T(8,128)(2,1)}), bf16[16,64,384]{2,1,0:T(8,128)(2,1)S(1)}, u32[]{:S(2)}, u32[]{:S(2)}) %all-to-all-start) | async-done | bytes 786464 | tf_op jit(solution)/shard_map/all_to_all | solution.py:345
  41.8 1.6 copy-done.9
  43.4 1.2 shard_map.75
  45.5 23.8 %all-to-all-start.1 = ((bf16[128,8,384]{2,1,0:T(8,128)(2,1)}), bf16[128,8,384]{2,1,0:T(8,128)(2,1)}, u32[]{:S(2)}, u32[]{:S(2)}) async-start(bf16[128,8,384]{2,1,0:T(8,128)(2,1)} %bitcast.22), calls=%async_computation.1 | async-start | bytes 1572864 | tf_op jit(solution)/shard_map/all_to_all | solution.py:345
  69.8 4.1 %shard_map.76 = (bf16[3,384,384]{2,1,0:T(8,128)(2,1)S(1)}, bf16[3,384,384]{2,1,0:T(8,128)(2,1)S(1)}) custom-call(f32[8,128]{1,0:T(8,128)S(1)} %broadcast_in_dim.72.order_ref, f32[8,384]{1,0:T(8,128)S(1)} %broadcast_in_dim.73.cosine_ref, f32[8,384]{1,0:T(8,128)S(1)} %exponential_select_fusion.start_ref), custom_call_target="tpu_custom_call" | custom-call | flops 4000000000 | bytes 1798144 | tf_op jit(solution)/shard_map/pallas_call | solution.py:22
  75.7 31.5 %all-to-all-done.1 = bf16[128,8,384]{2,1,0:T(8,128)(2,1)} async-done(((bf16[128,8,384]{2,1,0:T(8,128)(2,1)}), bf16[128,8,384]{2,1,0:T(8,128)(2,1)}, u32[]{:S(2)}, u32[]{:S(2)}) %all-to-all-start.1) | async-done | bytes 786464 | tf_op jit(solution)/shard_map/all_to_all | solution.py:345
  107.2 1.2 copy-done.13
  108.4 1.9 shard_map.77
  111.2 10.4 %all-to-all-start.2 = ((bf16[128,8,384]{2,1,0:T(8,128)(2,1)}), bf16[128,8,384]{2,1,0:T(8,128)(2,1)}, u32[]{:S(2)}, u32[]{:S(2)}) async-start(bf16[128,8,384]{2,1,0:T(8,128)(2,1)} %bitcast.23), calls=%async_computation.2 | async-start | bytes 1572864 | tf_op jit(solution)/shard_map/all_to_all | solution.py:345
  121.7 2.0 copy-done
  123.7 1.3 shard_map.78.w_ref
  125.0 1.1 copy-done.1
  126.1 20.2 %all-to-all-done.2 = bf16[128,8,384]{2,1,0:T(8,128)(2,1)} async-done(((bf16[128,8,384]{2,1,0:T(8,128)(2,1)}), bf16[128,8,384]{2,1,0:T(8,128)(2,1)}, u32[]{:S(2)}, u32[]{:S(2)}) %all-to-all-start.2) | async-done | bytes 786464 | tf_op jit(solution)/shard_map/all_to_all | solution.py:345
  146.3 1.4 copy-done.2
  147.7 1.8 shard_map.79
  149.5 31.3 %all_to_all.66 = bf16[128,8,384]{2,1,0:T(8,128)(2,1)S(1)} all-to-all(bf16[128,8,384]{2,1,0:T(8,128)(2,1)S(1)} %bitcast.25), channel_id=1, replica_groups=mesh['lat'=32,'qa'=4,'qb'=4] {'lat','qb'}, dimensions={0} | all-to-all | bytes 1572864 | tf_op jit(solution)/shard_map/all_to_all | solution.py:345
  181.7 32.0 %all_to_all.67 = bf16[128,8,384]{2,1,0:T(8,128)(2,1)S(1)} all-to-all(bf16[128,8,384]{2,1,0:T(8,128)(2,1)S(1)} %bitcast.26), channel_id=1, replica_groups=mesh['lat'=32,'qa'=4,'qb'=4] {'lat','qa'}, dimensions={0} | all-to-all | bytes 1572864 | tf_op jit(solution)/shard_map/all_to_all | solution.py:345
  213.7 2.7 shard_map.81
  216.4 6.2 %all-to-all-start.5 = ((bf16[16,80,384]{2,1,0:T(8,128)(2,1)}), bf16[16,80,384]{2,1,0:T(8,128)(2,1)S(1)}, u32[]{:S(2)}, u32[]{:S(2)}) async-start(bf16[16,80,384]{2,1,0:T(8,128)(2,1)} %bitcast.14), calls=%async_computation.5 | async-start | bytes 1966080 | tf_op jit(solution)/shard_map/all_to_all | solution.py:345
  222.9 1.1 copy-done.5
  225.0 25.3 %all-to-all-done.5 = bf16[16,80,384]{2,1,0:T(8,128)(2,1)S(1)} async-done(((bf16[16,80,384]{2,1,0:T(8,128)(2,1)}), bf16[16,80,384]{2,1,0:T(8,128)(2,1)S(1)}, u32[]{:S(2)}, u32[]{:S(2)}) %all-to-all-start.5) | async-done | bytes 983072 | tf_op jit(solution)/shard_map/all_to_all | solution.py:345
  250.3 4.3 %collective-permute-start = (bf16[320,128]{1,0:T(8,128)(2,1)S(1)}, bf16[320,128]{1,0:T(8,128)(2,1)S(1)}, u32[]{:S(2)}, u32[]{:S(2)}) collective-permute-start(bf16[320,128]{1,0:T(8,128)(2,1)S(1)} %get-tuple-element.18), channel_id=1, source_target_pairs={{0,16},{16,32},{32,48},{48,64},{64,80},{80,96},{96,112},{112,128},... | collective-permute-start | bytes 245768 | tf_op jit(solution)/shard_map/ppermute | solution.py:392
  254.6 4.3 %collective-permute-start.1 = (bf16[320,128]{1,0:T(8,128)(2,1)S(1)}, bf16[320,128]{1,0:T(8,128)(2,1)S(1)}, u32[]{:S(2)}, u32[]{:S(2)}) collective-permute-start(bf16[320,128]{1,0:T(8,128)(2,1)S(1)} %get-tuple-element.17), channel_id=1, source_target_pairs={{16,0},{32,16},{48,32},{64,48},{80,64},{96,80},{112,96},{128,112},... | collective-permute-start | bytes 245768 | tf_op jit(solution)/shard_map/ppermute | solution.py:393
  258.9 1.9 shard_map.83.f_ref
  261.1 7.1 %shard_map.84 = bf16[64,48,256]{2,1,0:T(8,128)(2,1)} custom-call(s32[2]{0:T(128)S(1)} %add_convert_fusion.ends_ref, bf16[4,960,256]{2,1,0:T(8,128)(2,1)S(1)} %shard_map.83.f_ref, bf16[320,128]{1,0:T(8,128)(2,1)S(1)} %collective-permute-done.up_ref, bf16[320,128]{1,0:T(8,128)(2,1)S(1)} %collective-permute-done.1.down_ref, ...), custom_call_target="tpu_custom_call" | custom-call | flops 10000000000 | bytes 5346312 | tf_op jit(solution)/shard_map/pallas_call | solution.py:22
  (54 shorter events, 8.7 us)
Async XLA Ops:
  6.5 115.1 %all-gather.3.cloned.1.call-start = ((), (), s32[]{:S(2)}) async-start(), calls=%async_computation.6 | async-start | bytes 3760128 | tf_op jit(solution)/shard_map/all_gather | solution.py:351
  7.3 1.1 copy-start.6
  10.2 31.6 %all-to-all-start = ((bf16[16,64,384]{2,1,0:T(8,128)(2,1)}), bf16[16,64,384]{2,1,0:T(8,128)(2,1)S(1)}, u32[]{:S(2)}, u32[]{:S(2)}) async-start(bf16[16,64,384]{2,1,0:T(8,128)(2,1)} %bitcast.2), calls=%async_computation | async-start | bytes 1572864 | tf_op jit(solution)/shard_map/all_to_all | solution.py:345
  33.4 1.3 copy-start.8
  41.8 1.6 copy-start.9
  43.4 26.1 %copy-start.14 = (f32[384]{0:T(512)S(1)}, f32[384]{0:T(512)}, u32[]{:S(2)}) copy-start(f32[384]{0:T(512)} %constant.217.clone) | copy-start | bytes 4612
  44.6 0.9 copy-start.3
  45.5 61.6 %all-to-all-start.1 = ((bf16[128,8,384]{2,1,0:T(8,128)(2,1)}), bf16[128,8,384]{2,1,0:T(8,128)(2,1)}, u32[]{:S(2)}, u32[]{:S(2)}) async-start(bf16[128,8,384]{2,1,0:T(8,128)(2,1)} %bitcast.22), calls=%async_computation.1 | async-start | bytes 1572864 | tf_op jit(solution)/shard_map/all_to_all | solution.py:345
  73.8 0.9 copy-start.10
  74.8 0.9 copy-start.12
  107.2 1.2 copy-start.13
  110.3 0.9 copy-start.4
  111.2 35.1 %all-to-all-start.2 = ((bf16[128,8,384]{2,1,0:T(8,128)(2,1)}), bf16[128,8,384]{2,1,0:T(8,128)(2,1)}, u32[]{:S(2)}, u32[]{:S(2)}) async-start(bf16[128,8,384]{2,1,0:T(8,128)(2,1)} %bitcast.23), calls=%async_computation.2 | async-start | bytes 1572864 | tf_op jit(solution)/shard_map/all_to_all | solution.py:345
  121.7 2.0 copy-start
  125.0 1.1 copy-start.1
  146.3 1.4 copy-start.2
  147.7 33.2 %copy-start.11 = (bf16[3,384,384]{2,1,0:T(8,128)(2,1)S(1)}, bf16[3,384,384]{2,1,0:T(8,128)(2,1)}, u32[]{:S(2)}) copy-start(bf16[3,384,384]{2,1,0:T(8,128)(2,1)} %copy-done.10) | copy-start | bytes 2654212
  213.7 8.9 %copy-start.15 = (f32[64]{0:T(128)S(1)}, f32[64]{0:T(128)}, u32[]{:S(2)}) copy-start(f32[64]{0:T(128)} %param.10) | copy-start | bytes 772
  213.7 9.0 %copy-start.16 = (f32[64]{0:T(128)S(1)}, f32[64]{0:T(128)}, u32[]{:S(2)}) copy-start(f32[64]{0:T(128)} %param.12) | copy-start | bytes 772
  213.7 9.1 %copy-start.7 = (bf16[9,64,64]{2,1,0:T(8,128)(2,1)S(1)}, bf16[9,64,64]{2,1,0:T(8,128)(2,1)}, u32[]{:S(2)}) copy-start(bf16[9,64,64]{2,1,0:T(8,128)(2,1)} %w_ref.1) | copy-start | bytes 221188
  216.4 33.9 %all-to-all-start.5 = ((bf16[16,80,384]{2,1,0:T(8,128)(2,1)}), bf16[16,80,384]{2,1,0:T(8,128)(2,1)S(1)}, u32[]{:S(2)}, u32[]{:S(2)}) async-start(bf16[16,80,384]{2,1,0:T(8,128)(2,1)} %bitcast.14), calls=%async_computation.5 | async-start | bytes 1966080 | tf_op jit(solution)/shard_map/all_to_all | solution.py:345
  222.9 1.1 copy-start.5
  250.3 10.5 %collective-permute-start = (bf16[320,128]{1,0:T(8,128)(2,1)S(1)}, bf16[320,128]{1,0:T(8,128)(2,1)S(1)}, u32[]{:S(2)}, u32[]{:S(2)}) collective-permute-start(bf16[320,128]{1,0:T(8,128)(2,1)S(1)} %get-tuple-element.18), channel_id=1, source_target_pairs={{0,16},{16,32},{32,48},{48,64},{64,80},{80,96},{96,112},{112,128},... | collective-permute-start | bytes 245768 | tf_op jit(solution)/shard_map/ppermute | solution.py:392
  254.6 6.5 %collective-permute-start.1 = (bf16[320,128]{1,0:T(8,128)(2,1)S(1)}, bf16[320,128]{1,0:T(8,128)(2,1)S(1)}, u32[]{:S(2)}, u32[]{:S(2)}) collective-permute-start(bf16[320,128]{1,0:T(8,128)(2,1)S(1)} %get-tuple-element.17), channel_id=1, source_target_pairs={{16,0},{32,16},{48,32},{64,48},{80,64},{96,80},{112,96},{128,112},... | collective-permute-start | bytes 245768 | tf_op jit(solution)/shard_map/ppermute | solution.py:393
Sparse Core Ops, SparseCore 0:
  10.6 103.1 all-gather.2

commit v2 on v1

--- a/solution.py
+++ b/solution.py
@@ -51,14 +51,84 @@
     return lax.dot_general(a, b, (((1,), (1,)), ((), ())), preferred_element_type=f32)
 
 
+def lanes_of(x):
+    return iota(x.shape, 1)
+
+
+def close(first, middle, last):
+    lane = lanes_of(first)
+    return (
+        jnp.where(lane < 96, first, pltpu.roll(middle, 96, 1)),
+        jnp.where(lane < 96, last, pltpu.roll(middle, 64, 1)),
+    )
+
+
+def reopen(first, last, rest):
+    lane = lanes_of(first)
+    return jnp.where(
+        lane < 32, pltpu.roll(first, 32, 1), jnp.where(lane < 64, pltpu.roll(last, 64, 1), rest)
+    )
+
+
+def side_by_side(parts):
+    group = lanes_of(parts[0]) // 32
+    total = jnp.zeros(parts[0].shape, f32)
+    for i, part in enumerate(parts):
+        total = jnp.where(group == i, pltpu.roll(part, (32 * i + 64) % 128, 1), total)
+    return total
+
+
+def apart(x, i):
+    return pltpu.roll(x, (64 - 32 * i) % 128, 1)
+
+
+def close_cells(first, middle, last):
+    a, b = close(first, middle, last)
+    pieces = [middle[8 * g : 8 * g + 8] for g in range(8)]
+    return (
+        jnp.concatenate([a, side_by_side(pieces[:4])], axis=0),
+        jnp.concatenate([b, side_by_side(pieces[4:])], axis=0),
+    )
+
+
+def reopen_cells(first, last):
+    rest = [apart(first[64:72], i) for i in range(4)] + [apart(last[64:72], i) for i in range(4)]
+    return reopen(first[:64], last[:64], jnp.concatenate(rest, axis=0))
+
+
+def mode_row(j):
+    return pl.ds(j, 128, stride=8)
+
+
+def close_modes(y_ref, s_ref):
+    a, b = close(y_ref[0], y_ref[1], y_ref[2])
+    y_ref[0], y_ref[2] = a, b
+    y_ref[0, mode_row(6), :] = side_by_side([y_ref[1, mode_row(j), :] for j in range(4)])
+    y_ref[2, mode_row(6), :] = side_by_side([y_ref[1, mode_row(j), :] for j in range(4, 6)])
+    s_ref[:, 0:128] = y_ref[0].astype(bf16)
+    s_ref[:, 128:256] = y_ref[2].astype(bf16)
+
+
+def reopen_modes(x_ref, y_ref):
+    first, last = x_ref[:, 0:128].astype(f32), x_ref[:, 128:256].astype(f32)
+    y_ref[0], y_ref[2] = first, last
+    y_ref[1] = reopen(first, last, jnp.zeros(first.shape, f32))
+    rest = y_ref[0, mode_row(6), :], y_ref[2, mode_row(6), :]
+    upper = lanes_of(rest[0]) >= 64
+    for j in range(6):
+        y_ref[1, mode_row(j), :] = jnp.where(
+            upper, apart(rest[j // 4], j % 4), y_ref[1, mode_row(j), :]
+        )
+
+
 def pack_kernel(x_ref, s_ref):
     spread = widen()
-    for a in range(12):
-        wide = dot(x_ref[a], spread).astype(bf16)
+    for a in range(4):
+        wide = [dot(x_ref[3 * a + t], spread) for t in range(3)]
         for b in range(4):
-            s_ref[
-                pl.ds((a // 3 * 4 + b) * 64, 64), pl.ds(a % 3 * 128, 128)
-            ] = wide[:, b * 128 : (b + 1) * 128]
+            first, last = close_cells(*(w[:, b * 128 : (b + 1) * 128] for w in wide))
+            s_ref[a * 4 + b, :, 0:128] = first.astype(bf16)
+            s_ref[a * 4 + b, :, 128:256] = last.astype(bf16)
 
 
 def dft_tables_kernel(p_ref, q_ref, cb_ref, sb_ref, pt_ref, qt_ref, cbt_ref, sbt_ref, c_ref, g_ref):
@@ -71,10 +141,20 @@
         ).astype(bf16)
 
 
-def dft_kernel(c_ref, x_ref, w_ref, s_ref):
+def dft_kernel(c_ref, x_ref, w_ref, s_ref, state_ref, y_ref):
+    for q in range(16):
+        cells = x_ref[q].astype(f32)
+        first, last = cells[:, 0:128], cells[:, 128:256]
+        rows = pl.ds(q * 64, 64)
+        state_ref[rows, 0:128] = first[:64].astype(bf16)
+        state_ref[rows, 128:256] = reopen_cells(first, last).astype(bf16)
+        state_ref[rows, 256:384] = last[:64].astype(bf16)
     for block in range(4):
         rows = pl.ds(block * 256, 256)
-        s_ref[rows, :] = (dot(c_ref[rows, :], x_ref[...]) * w_ref[...]).astype(bf16)
+        result = dot(c_ref[rows, :], state_ref[...]) * w_ref[...]
+        for t in range(3):
+            y_ref[t, rows, :] = result[:, t * 128 : (t + 1) * 128]
+    close_modes(y_ref, s_ref)
 
 
 def legendre_tables_kernel(order_ref, cosine_ref, start_ref, l_ref, t_ref, rows_ref):
@@ -127,8 +207,7 @@
 
 
 def legendre_kernel(x_ref, l_ref, s_ref, in_ref, out_ref):
-    for t in range(3):
-        in_ref[t] = x_ref[:, t * 128 : (t + 1) * 128].astype(f32)
+    reopen_modes(x_ref, in_ref)
     out_ref[...] = jnp.zeros(out_ref.shape, f32)
     for m3 in range(3):
         halves = [
@@ -143,12 +222,10 @@
                 out_ref[t, pl.ds(cs * 3 + m3, 128, stride=8), :] = result[
                     t * 128 : (t + 1) * 128, cs * 128 : (cs + 1) * 128
                 ]
-    for t in range(3):
-        s_ref[:, pl.ds(t * 128, 128)] = out_ref[t].astype(bf16)
-
-
-def mix_weight_kernel(first_ref, w_ref, o_ref):
-    del first_ref
+    close_modes(out_ref, s_ref)
+
+
+def mix_weight_kernel(w_ref, o_ref):
     part = w_ref[...].astype(f32).reshape(384, 384).astype(bf16)
     wide = dot(part, widen()).astype(bf16)
     o_ref[...] = jnp.zeros(o_ref.shape, bf16)
@@ -156,45 +233,57 @@
         o_ref[0, pl.ds(b * 128, 96), :] = wide[b * 96 : (b + 1) * 96]
 
 
-def spread_mix_weight(gathered, first):
+def spread_mix_weight(gathered):
     return pl.pallas_call(
         mix_weight_kernel,
         out_shape=shape((3, 512, 512)),
-        grid_spec=pltpu.PrefetchScalarGridSpec(
-            num_scalar_prefetch=1,
-            grid=(3,),
-            in_specs=[pl.BlockSpec((16, 1, 24, 384), lambda r, first: (0, first[0] + r, 0, 0))],
-            out_specs=pl.BlockSpec((1, 512, 512), lambda r, first: (r, 0, 0)),
-        ),
+        grid=(3,),
+        in_specs=[pl.BlockSpec((16, 1, 24, 384), lambda r: (0, r, 0, 0))],
+        out_specs=pl.BlockSpec((1, 512, 512), lambda r: (r, 0, 0)),
         compiler_params=pltpu.CompilerParams(vmem_limit_bytes=24 * MIB),
         cost_estimate=pl.CostEstimate(flops=10**9, bytes_accessed=3 * 10**6, transcendentals=0),
-    )(first, gathered)
-
-
-def mix_kernel(x_ref, w_ref, s_ref):
+    )(gathered)
+
+
+def mix_kernel(x_ref, w_ref, s_ref, in_ref, out_ref):
+    reopen_modes(x_ref, in_ref)
     for r in range(3):
-        lanes = pl.ds(r * 128, 128)
-        part = x_ref[:, lanes].astype(f32).reshape(32, 4, 8, 128)
+        part = in_ref[r].reshape(32, 4, 8, 128)
         modes = jnp.concatenate([part[:, b].reshape(256, 128) for b in range(4)], axis=1)
         mixed = dot_nt(modes.astype(bf16), w_ref[r])
         back = [mixed[:, b * 128 : (b + 1) * 128].reshape(32, 1, 8, 128) for b in range(4)]
-        s_ref[:, lanes] = jnp.concatenate(back, axis=1).reshape(1024, 128).astype(bf16)
-
-
-def inverse_kernel(g_ref, x_ref, state_ref, s_ref, h_ref):
+        out_ref[r] = jnp.concatenate(back, axis=1).reshape(1024, 128)
+    close_modes(out_ref, s_ref)
+
+
+def inverse_kernel(g_ref, x_ref, state_ref, s_ref, y_ref, m_ref, h_ref):
+    reopen_modes(x_ref, y_ref)
+    for t in range(3):
+        m_ref[:, pl.ds(t * 128, 128)] = y_ref[t].astype(bf16)
     for block in range(4):
         rows = pl.ds(block * 256, 256)
-        spatial = dot(g_ref[rows, :], x_ref[...])
-        hidden = (state_ref[rows, :].astype(f32) + jax.nn.gelu(spatial)).astype(bf16)
-        h_ref[rows, :] = hidden.astype(f32)
-        for part in range(4):
-            s_ref[pl.ds((block * 4 + part) * 80, 64), :] = hidden[part * 64 : (part + 1) * 64]
-    row = iota((16, 384), 0)
+        spatial = dot(g_ref[rows, :], m_ref[...])
+        h_ref[rows, :] = state_ref[rows, :].astype(f32) + jax.nn.gelu(spatial)
+    row = iota((8, 128), 0)
     for q in range(16):
-        right = h_ref[pl.ds((q + 1) % 16 * 64, 1), :]
-        left = h_ref[pl.ds((q * 64 + 1023) % 1024, 1), :]
-        edge = jnp.where(row == 0, right, jnp.where(row == 15, left, 0.0))
-        s_ref[pl.ds(q * 80 + 64, 16), :] = edge.astype(bf16)
+        inner, halo = [], []
+        for t in range(3):
+            lanes = pl.ds(t * 128, 128)
+            inner.append(h_ref[pl.ds(q * 64, 64), lanes])
+            right = h_ref[pl.ds((q + 1) % 16 * 64, 1), lanes]
+            left = h_ref[pl.ds((q * 64 + 1023) % 1024, 1), lanes]
+            halo.append(jnp.where(row == 0, right, jnp.where(row == 1, left, 0.0)))
+        first, last = close_cells(*inner)
+        first_halo, last_halo = close(*halo)
+        rest = pltpu.roll(halo[1], 64, 1)
+        first_halo = jnp.where(row == 2, pltpu.roll(rest, 2, 0), first_halo)
+        last_halo = jnp.where(row == 2, pltpu.roll(rest, 1, 0), last_halo)
+        s_ref[q, :, 0:128] = jnp.concatenate([first, first_halo], axis=0).astype(bf16)
+        s_ref[q, :, 128:256] = jnp.concatenate([last, last_halo], axis=0).astype(bf16)
+
+
+def with_sides(inner, halo):
+    return jnp.concatenate([inner, halo, pltpu.roll(halo, 6, 0)], axis=0).astype(bf16)
 
 
 def tail_weights_kernel(u_ref, w_ref, o_ref, c_ref):
@@ -218,11 +307,24 @@
 
 
 def fine_kernel(x_ref, u_ref, bias_ref, o_ref, h_ref):
-    for a in range(12):
+    row = iota((8, 128), 0)
+    for a in range(4):
         for b in range(4):
-            h_ref[pl.ds(a * 80, 80), pl.ds(b * 128, 128)] = x_ref[
-                pl.ds((a // 3 * 4 + b) * 80, 80), pl.ds(a % 3 * 128, 128)
-            ]
+            cells = x_ref[a * 4 + b].astype(f32)
+            first, last = cells[:, 0:128], cells[:, 128:256]
+            first_halo, last_halo = first[72:80], last[72:80]
+            rest = jnp.where(
+                row == 0,
+                pltpu.roll(pltpu.roll(first_halo, 64, 1), 6, 0),
+                pltpu.roll(pltpu.roll(last_halo, 64, 1), 7, 0),
+            )
+            tiles = (
+                (first[:64], first_halo),
+                (reopen_cells(first, last), reopen(first_halo, last_halo, rest)),
+                (last[:64], last_halo),
+            )
+            for t, (inner, halo) in enumerate(tiles):
+                h_ref[pl.ds((a * 3 + t) * 80, 80), pl.ds(b * 128, 128)] = with_sides(inner, halo)
     for q in range(4):
         lanes = pl.ds(q * 256, 256)
         for block in range(4):
@@ -237,8 +339,9 @@
 ):
     for b in range(4):
         lanes = pl.ds(b * 128, 128)
-        h_ref[pl.ds(0, 80), lanes] = up_ref[pl.ds(b * 80, 80), :]
-        h_ref[pl.ds(80, 80), lanes] = down_ref[pl.ds(b * 80, 80), :]
+        for side, ref in enumerate((up_ref, down_ref)):
+            cells = ref[b].astype(f32)
+            h_ref[pl.ds(side * 80, 80), lanes] = with_sides(cells[:64], cells[72:80])
     first = iota((160, 256), 0) < 80
     keep = jnp.where(first, ends_ref[0], ends_ref[1]) > 0
     half = iota((80, 128), 1) < 64
@@ -346,36 +449,45 @@
 
 
 def local(state_field, mix_weight, upsample_weight, upsample_bias, conv_weight, conv_bias):
-    lat, qa, qb = lax.axis_index("lat"), lax.axis_index("qa"), lax.axis_index("qb")
-    n = 4 * lat + qa
-    gathered = lax.all_gather(mix_weight, ("qa", "qb"), axis=0)
-    packed = call(pack_kernel, shape((1024, 384)), state_field, flops=10**9)
-    state = exchange(packed, ("qa", "qb"))
+    lat = lax.axis_index("lat")
+    n = 4 * lat + lax.axis_index("qa")
+    own_degrees = exchange(mix_weight, "qb")
+    gathered = lax.all_gather(own_degrees, "qa", axis=0).reshape(16, 3, 24, 384)
+    packed = call(pack_kernel, shape((16, 72, 256)), state_field, flops=10**9)
+    arrived = exchange(packed, ("qa", "qb"))
     forward, inverse = dft_tables()
     colatitude = ((3 * n + jnp.arange(384, dtype=jnp.int32) // 128).astype(f32) + 0.5) * (
         math.pi / 384
     )
     scale = (jnp.sin(colatitude) * (math.pi / 384) * (2.0 * math.pi / 1024))[None, :]
-    spectra = call(dft_kernel, shape((1024, 384)), forward, state, scale, flops=10**9)
+    scratch = [pltpu.VMEM((3, 1024, 128), f32)] * 2
+    spectra, state = call(
+        dft_kernel,
+        (shape((1024, 256)), shape((1024, 384))),
+        forward,
+        arrived,
+        scale,
+        scratch=scratch[:1],
+        flops=10**9,
+    )
     columns = exchange(spectra, ("lat", "qa"))
     basis, basis_t = legendre_tables(n)
-    scratch = [pltpu.VMEM((3, 1024, 128), f32)] * 2
-    coeffs = call(legendre_kernel, shape((1024, 384)), columns, basis, scratch=scratch, flops=10**9)
+    coeffs = call(legendre_kernel, shape((1024, 256)), columns, basis, scratch=scratch, flops=10**9)
     degrees = exchange(coeffs, ("lat", "qb"))
-    mixer = spread_mix_weight(gathered, (3 * qb).reshape(1).astype(jnp.int32))
-    mixed = call(mix_kernel, shape((1024, 384)), degrees, mixer, flops=10**9)
+    mixer = spread_mix_weight(gathered)
+    mixed = call(mix_kernel, shape((1024, 256)), degrees, mixer, scratch=scratch, flops=10**9)
     returned = exchange(mixed, ("lat", "qb"))
     synthesized = call(
-        legendre_kernel, shape((1024, 384)), returned, basis_t, scratch=scratch, flops=10**9
+        legendre_kernel, shape((1024, 256)), returned, basis_t, scratch=scratch, flops=10**9
     )
     modes = exchange(synthesized, ("lat", "qa"))
     hidden = call(
         inverse_kernel,
-        shape((1280, 384)),
+        shape((16, 80, 256)),
         inverse,
         modes,
         state,
-        scratch=[pltpu.VMEM((1024, 384), f32)],
+        scratch=[scratch[0], pltpu.VMEM((1024, 384), bf16), pltpu.VMEM((1024, 384), f32)],
         flops=10**9,
     )
     cells = exchange(hidden, ("qa", "qb"))
@@ -386,8 +498,8 @@
         conv_weight,
         flops=2 * 10**9,
     )
-    first_row = cells[0:320, 0:128]
-    last_row = cells[960:1280, 256:384]
+    first_row = cells[0:4, :, 0:128]
+    last_row = cells[12:16, :, 128:256]
     count = lax.axis_size("lat")
     up = lax.ppermute(last_row, "lat", [(i, i + 1) for i in range(count - 1)])
     down = lax.ppermute(first_row, "lat", [(i + 1, i) for i in range(count - 1)])

time: 276 us -> 223 us (0.81)
  waiting for transfers between devices: 85 us -> 46.4 us
  between operations: 13.7 us -> 0.3 us
  blocking collectives: 63.4 us -> 71.4 us
  starting transfers between devices: 61.8 us -> 56.9 us
  local copies, waits for them, and re-layouts: 14.9 us -> 10.7 us
    all_to_all x4 -> x5, waiting for transfers between devices: 84 us -> 46 us  [exchange(): return lax.all_to_all(x, axes, 0, 0, tiled=True)]
    all_gather x0 -> x1, blocking collectives: none -> 14.4 us  [local(): gathered = lax.all_gather(own_degrees, 'qa', axis=0).reshape(16, 3, 24, 384)]
    all_to_all x2, blocking collectives: 63.4 us -> 57 us  [exchange(): return lax.all_to_all(x, axes, 0, 0, tiled=True)]
    all_to_all x4 -> x5, starting transfers between devices: 53.2 us -> 48.4 us  [exchange(): return lax.all_to_all(x, axes, 0, 0, tiled=True)]
    unnamed x34 -> x30, local copies, waits for them, and re-layouts: 14.4 us -> 10.2 us
  transfers between devices with their start and end apart: 7 -> 7, of which waited for: 5 -> 6; matrix products, arithmetic and copies ran while one was open for 3% -> 4% of each run, Pallas kernels for 6% -> 6%
where the time goes in v2:
time: 223 us; the launch traced here: 222 us
  blocking collectives  71.4 us (32%)
  starting transfers between devices  56.9 us (26%)
  waiting for transfers between devices  46.4 us (21%)
  Pallas kernels  27.9 us (13%)
  local copies, waits for them, and re-layouts  10.7 us (5%)
  other arithmetic  8.37 us (4%)
    all_to_all x2, blocking collectives, exchange(): return lax.all_to_all(x, axes, 0, 0, tiled=True)  57 us
    all_to_all x5, starting transfers between devices, exchange(): return lax.all_to_all(x, axes, 0, 0, tiled=True)  48.4 us
    all_to_all x5, waiting for transfers between devices, exchange(): return lax.all_to_all(x, axes, 0, 0, tiled=True)  46 us
    pallas_call x11, Pallas kernels, call(): pl.pallas_call(kernel, out_shape=out, in_specs=space, out_specs=jax.tree....  26.6 us
    all_gather x1, blocking collectives, local(): gathered = lax.all_gather(own_degrees, 'qa', axis=0).reshape(16, 3, 24, 384)  14.4 us
    unnamed x30, local copies, waits for them, and re-layouts  10.2 us
    mul x2, other arithmetic, base(): return (jnp.cos(angle) * scale, jnp.sin(angle) * scale, turn)  5.73 us
    ppermute x1, starting transfers between devices, local(): up = lax.ppermute(last_row, 'lat', [(i, i + 1) for i in range(count - 1)])  4.57 us
  transfers between devices with their start and end apart: 7, of which 6 were waited for; matrix products, arithmetic and copies ran while one was open for 4% of the time, Pallas kernels for 6%

profile of v2, /device:TPU:8, one launch (start us, length us, event | category | flops | bytes accessed | tf_op | source)
XLA Modules:
  0.0 221.9 jit_solution(9717450539114738773)
XLA Ops:
  1.1 1.8 shard_map.74
  2.9 12.8 %all-to-all-start = ((bf16[16,72,256]{2,1,0:T(8,128)(2,1)}), bf16[16,72,256]{2,1,0:T(8,128)(2,1)S(1)}, u32[]{:S(2)}, u32[]{:S(2)}) async-start(bf16[16,72,256]{2,1,0:T(8,128)(2,1)} %shard_map.74), calls=%async_computation | async-start | bytes 1179648 | tf_op jit(solution)/shard_map/all_to_all | solution.py:448
  15.9 3.1 %sine_multiply_fusion = (f32[128,1024]{1,0:T(8,128)S(1)}, f32[128,1024]{1,0:T(8,128)}) fusion(s32[1024]{0:T(1024)S(1)} %get-tuple-element.32, s32[1024]{0:T(1024)S(1)} %get-tuple-element.33, pred[1024]{0:T(1024)(128)(4,1)S(1)} %get-tuple-element.35, s32[1024]{0:T(1024)S(1)} %get-tuple-element.31, s32[1024]{0:T(1024)S(1)} %get-tuple-element.34, ...), kind=kLoop, calls=%fused_computation.32 | loop fusion | flops 4456448 | bytes 1067008 | tf_op jit(solution)/shard_map/mul | solution.py:433
  19.4 2.7 %select_multiply_fusion = (f32[1024,128]{1,0:T(8,128)S(1)}, f32[1024,128]{1,0:T(8,128)S(1)}) fusion(s32[1024]{0:T(1024)S(1)} %get-tuple-element.32, s32[1024]{0:T(1024)S(1)} %get-tuple-element.33, pred[1024]{0:T(1024)(128)(4,1)S(1)} %get-tuple-element.35, s32[1024]{0:T(1024)S(1)} %get-tuple-element.31, s32[1024]{0:T(1024)S(1)} %get-tuple-element.34, ...), kind=kLoop, calls=%fused_computation.20 | loop fusion | flops 4063232 | bytes 1067008 | tf_op jit(solution)/shard_map/mul | solution.py:433
  22.1 1.9 multiply_sine_fusion
  24.0 3.1 %shard_map.73 = (bf16[1024,1024]{1,0:T(8,128)(2,1)S(1)}, bf16[1024,1024]{1,0:T(8,128)(2,1)S(1)}) custom-call(f32[1024,128]{1,0:T(8,128)S(1)} %get-tuple-element.30.p_ref, f32[1024,128]{1,0:T(8,128)S(1)} %get-tuple-element.29.q_ref, f32[1024,8]{1,0:T(8,128)S(1)} %get-tuple-element.24.cb_ref, f32[1024,8]{1,0:T(8,128)S(1)} %get-tuple-element.23.sb_ref, ...), custom_call_target="tpu_custom_call" | custom-call | flops 4000000000 | bytes 6422528 | tf_op jit(solution)/shard_map/pallas_call | solution.py:22
  27.0 1.3 copy-done.6
  28.4 3.0 %all-to-all-done.x_ref = bf16[16,72,256]{2,1,0:T(8,128)(2,1)S(1)} async-done(((bf16[16,72,256]{2,1,0:T(8,128)(2,1)}), bf16[16,72,256]{2,1,0:T(8,128)(2,1)S(1)}, u32[]{:S(2)}, u32[]{:S(2)}) %all-to-all-start) | async-done | bytes 589856 | tf_op jit(solution)/shard_map/all_to_all | solution.py:448
  31.4 1.6 copy-done.7
  33.0 1.4 shard_map.75
  35.2 17.2 %all-to-all-start.1 = ((bf16[128,8,256]{2,1,0:T(8,128)(2,1)}), bf16[128,8,256]{2,1,0:T(8,128)(2,1)S(1)}, u32[]{:S(2)}, u32[]{:S(2)}) async-start(bf16[128,8,256]{2,1,0:T(8,128)(2,1)} %bitcast.14), calls=%async_computation.1 | async-start | bytes 1048576 | tf_op jit(solution)/shard_map/all_to_all | solution.py:448
  52.8 19.6 %all-to-all-done.1 = bf16[128,8,256]{2,1,0:T(8,128)(2,1)S(1)} async-done(((bf16[128,8,256]{2,1,0:T(8,128)(2,1)}), bf16[128,8,256]{2,1,0:T(8,128)(2,1)S(1)}, u32[]{:S(2)}, u32[]{:S(2)}) %all-to-all-start.1) | async-done | bytes 524320 | tf_op jit(solution)/shard_map/all_to_all | solution.py:448
  72.4 4.0 %all-to-all-start.3 = ((bf16[12,24,384]{2,1,0:T(8,128)(2,1)}), bf16[12,24,384]{2,1,0:T(8,128)(2,1)}, u32[]{:S(2)}, u32[]{:S(2)}) async-start(bf16[12,24,384]{2,1,0:T(8,128)(2,1)} %param.8), calls=%async_computation.3 | async-start | bytes 442368 | tf_op jit(solution)/shard_map/all_to_all | solution.py:448
  76.5 4.1 %shard_map.76 = (bf16[3,384,384]{2,1,0:T(8,128)(2,1)S(1)}, bf16[3,384,384]{2,1,0:T(8,128)(2,1)S(1)}) custom-call(f32[8,128]{1,0:T(8,128)S(1)} %broadcast_in_dim.72.order_ref, f32[8,384]{1,0:T(8,128)S(1)} %broadcast_in_dim.73.cosine_ref, f32[8,384]{1,0:T(8,128)S(1)} %exponential_select_fusion.start_ref), custom_call_target="tpu_custom_call" | custom-call | flops 4000000000 | bytes 1798144 | tf_op jit(solution)/shard_map/pallas_call | solution.py:22
  81.4 1.3 shard_map.77
  83.6 2.5 %all-to-all-done.3 = bf16[12,24,384]{2,1,0:T(8,128)(2,1)} async-done(((bf16[12,24,384]{2,1,0:T(8,128)(2,1)}), bf16[12,24,384]{2,1,0:T(8,128)(2,1)}, u32[]{:S(2)}, u32[]{:S(2)}) %all-to-all-start.3) | async-done | bytes 221216 | tf_op jit(solution)/shard_map/all_to_all | solution.py:448
  86.1 8.1 %all-to-all-start.2 = ((bf16[128,8,256]{2,1,0:T(8,128)(2,1)}), bf16[128,8,256]{2,1,0:T(8,128)(2,1)S(1)}, u32[]{:S(2)}, u32[]{:S(2)}) async-start(bf16[128,8,256]{2,1,0:T(8,128)(2,1)} %bitcast.15), calls=%async_computation.2 | async-start | bytes 1048576 | tf_op jit(solution)/shard_map/all_to_all | solution.py:448
  94.2 14.4 %all-gather = bf16[48,24,384]{2,1,0:T(8,128)(2,1)S(1)} all-gather(bf16[12,24,384]{2,1,0:T(8,128)(2,1)} %all-to-all-done.3), channel_id=2, replica_groups=mesh['lat'=32,'qa'=4,'qb'=4] {'qa'}, dimensions={0}, use_global_device_ids=true | all-gather | bytes 1105920 | tf_op jit(solution)/shard_map/all_gather | solution.py:455
  108.5 1.3 shard_map.78.w_ref
  109.9 1.1 copy-done.8
  111.0 2.9 %all-to-all-done.2 = bf16[128,8,256]{2,1,0:T(8,128)(2,1)S(1)} async-done(((bf16[128,8,256]{2,1,0:T(8,128)(2,1)}), bf16[128,8,256]{2,1,0:T(8,128)(2,1)S(1)}, u32[]{:S(2)}, u32[]{:S(2)}) %all-to-all-start.2) | async-done | bytes 524320 | tf_op jit(solution)/shard_map/all_to_all | solution.py:448
  113.9 1.4 copy-done.9
  116.3 30.3 %all_to_all.59 = bf16[128,8,256]{2,1,0:T(8,128)(2,1)S(1)} all-to-all(bf16[128,8,256]{2,1,0:T(8,128)(2,1)S(1)} %bitcast.18), channel_id=1, replica_groups=mesh['lat'=32,'qa'=4,'qb'=4] {'lat','qb'}, dimensions={0} | all-to-all | bytes 1048576 | tf_op jit(solution)/shard_map/all_to_all | solution.py:448
  146.6 1.3 shard_map.80
  147.9 26.7 %all_to_all.60 = bf16[128,8,256]{2,1,0:T(8,128)(2,1)S(1)} all-to-all(bf16[128,8,256]{2,1,0:T(8,128)(2,1)S(1)} %bitcast.19), channel_id=1, replica_groups=mesh['lat'=32,'qa'=4,'qb'=4] {'lat','qa'}, dimensions={0} | all-to-all | bytes 1048576 | tf_op jit(solution)/shard_map/all_to_all | solution.py:448
  174.6 2.5 %shard_map.81 = bf16[16,80,256]{2,1,0:T(8,128)(2,1)} custom-call(bf16[1024,1024]{1,0:T(8,128)(2,1)S(1)} %get-tuple-element.13.g_ref, bf16[1024,256]{1,0:T(8,128)(2,1)S(1)} %bitcast.11, bf16[1024,384]{1,0:T(8,128)(2,1)S(1)} %get-tuple-element.18.state_ref), custom_call_target="tpu_custom_call" | custom-call | flops 1000000000 | bytes 4063232 | tf_op jit(solution)/shard_map/pallas_call | solution.py:22
  177.2 6.2 %all-to-all-start.6 = ((bf16[16,80,256]{2,1,0:T(8,128)(2,1)}), bf16[16,80,256]{2,1,0:T(8,128)(2,1)S(1)}, u32[]{:S(2)}, u32[]{:S(2)}) async-start(bf16[16,80,256]{2,1,0:T(8,128)(2,1)} %shard_map.81), calls=%async_computation.6 | async-start | bytes 1310720 | tf_op jit(solution)/shard_map/all_to_all | solution.py:448
  185.8 18.1 %all-to-all-done.6.x_ref = bf16[16,80,256]{2,1,0:T(8,128)(2,1)S(1)} async-done(((bf16[16,80,256]{2,1,0:T(8,128)(2,1)}), bf16[16,80,256]{2,1,0:T(8,128)(2,1)S(1)}, u32[]{:S(2)}, u32[]{:S(2)}) %all-to-all-start.6) | async-done | bytes 655392 | tf_op jit(solution)/shard_map/all_to_all | solution.py:448
  203.9 4.6 %collective-permute-start = (bf16[4,80,128]{2,1,0:T(8,128)(2,1)S(1)}, bf16[4,80,128]{2,1,0:T(8,128)(2,1)S(1)}, u32[]{:S(2)}, u32[]{:S(2)}) collective-permute-start(bf16[4,80,128]{2,1,0:T(8,128)(2,1)S(1)} %get-tuple-element.22), channel_id=1, source_target_pairs={{0,16},{16,32},{32,48},{48,64},{64,80},{80,96},{96,112},{112,128},... | collective-permute-start | bytes 245768 | tf_op jit(solution)/shard_map/ppermute | solution.py:504
  208.5 4.0 %collective-permute-start.1 = (bf16[4,80,128]{2,1,0:T(8,128)(2,1)S(1)}, bf16[4,80,128]{2,1,0:T(8,128)(2,1)S(1)}, u32[]{:S(2)}, u32[]{:S(2)}) collective-permute-start(bf16[4,80,128]{2,1,0:T(8,128)(2,1)S(1)} %get-tuple-element.21), channel_id=1, source_target_pairs={{16,0},{32,16},{48,32},{64,48},{80,64},{96,80},{112,96},{128,112},... | collective-permute-start | bytes 245768 | tf_op jit(solution)/shard_map/ppermute | solution.py:505
  212.5 2.0 shard_map.83.f_ref
  214.8 7.1 %shard_map.84 = bf16[64,48,256]{2,1,0:T(8,128)(2,1)} custom-call(s32[2]{0:T(128)S(1)} %add_convert_fusion.ends_ref, bf16[4,960,256]{2,1,0:T(8,128)(2,1)S(1)} %shard_map.83.f_ref, bf16[4,80,128]{2,1,0:T(8,128)(2,1)S(1)} %collective-permute-done.up_ref, bf16[4,80,128]{2,1,0:T(8,128)(2,1)S(1)} %collective-permute-done.1.down_ref, ...), custom_call_target="tpu_custom_call" | custom-call | flops 10000000000 | bytes 5346312 | tf_op jit(solution)/shard_map/pallas_call | solution.py:22
  (50 shorter events, 8.3 us)
Async XLA Ops:
  0.0 1.1 copy-start.4
  2.9 28.5 %all-to-all-start = ((bf16[16,72,256]{2,1,0:T(8,128)(2,1)}), bf16[16,72,256]{2,1,0:T(8,128)(2,1)S(1)}, u32[]{:S(2)}, u32[]{:S(2)}) async-start(bf16[16,72,256]{2,1,0:T(8,128)(2,1)} %shard_map.74), calls=%async_computation | async-start | bytes 1179648 | tf_op jit(solution)/shard_map/all_to_all | solution.py:448
  19.1 4.8 %copy-start = (f32[128,1024]{1,0:T(8,128)S(1)}, f32[128,1024]{1,0:T(8,128)}, u32[]{:S(2)}) copy-start(f32[128,1024]{1,0:T(8,128)} %get-tuple-element.28.pt_ref) | copy-start | bytes 1572868
  27.0 1.4 copy-start.6
  31.4 1.6 copy-start.7
  33.0 19.5 %copy-start.12 = (f32[384]{0:T(512)S(1)}, f32[384]{0:T(512)}, u32[]{:S(2)}) copy-start(f32[384]{0:T(512)} %constant.215.clone) | copy-start | bytes 4612
  34.4 0.8 copy-start.1
  35.2 37.1 %all-to-all-start.1 = ((bf16[128,8,256]{2,1,0:T(8,128)(2,1)}), bf16[128,8,256]{2,1,0:T(8,128)(2,1)S(1)}, u32[]{:S(2)}, u32[]{:S(2)}) async-start(bf16[128,8,256]{2,1,0:T(8,128)(2,1)} %bitcast.14), calls=%async_computation.1 | async-start | bytes 1048576 | tf_op jit(solution)/shard_map/all_to_all | solution.py:448
  72.4 13.7 %all-to-all-start.3 = ((bf16[12,24,384]{2,1,0:T(8,128)(2,1)}), bf16[12,24,384]{2,1,0:T(8,128)(2,1)}, u32[]{:S(2)}, u32[]{:S(2)}) async-start(bf16[12,24,384]{2,1,0:T(8,128)(2,1)} %param.8), calls=%async_computation.3 | async-start | bytes 442368 | tf_op jit(solution)/shard_map/all_to_all | solution.py:448
  80.5 0.9 copy-start.10
  82.8 0.8 copy-start.2
  86.1 27.8 %all-to-all-start.2 = ((bf16[128,8,256]{2,1,0:T(8,128)(2,1)}), bf16[128,8,256]{2,1,0:T(8,128)(2,1)S(1)}, u32[]{:S(2)}, u32[]{:S(2)}) async-start(bf16[128,8,256]{2,1,0:T(8,128)(2,1)} %bitcast.15), calls=%async_computation.2 | async-start | bytes 1048576 | tf_op jit(solution)/shard_map/all_to_all | solution.py:448
  109.9 1.1 copy-start.8
  113.9 1.4 copy-start.9
  115.3 31.3 %copy-start.11 = (bf16[3,384,384]{2,1,0:T(8,128)(2,1)S(1)}, bf16[3,384,384]{2,1,0:T(8,128)(2,1)}, u32[]{:S(2)}) copy-start(bf16[3,384,384]{2,1,0:T(8,128)(2,1)} %copy-done.10) | copy-start | bytes 2654212
  174.6 8.8 %copy-start.13 = (f32[64]{0:T(128)S(1)}, f32[64]{0:T(128)}, u32[]{:S(2)}) copy-start(f32[64]{0:T(128)} %param.10) | copy-start | bytes 772
  174.6 8.9 %copy-start.14 = (f32[64]{0:T(128)S(1)}, f32[64]{0:T(128)}, u32[]{:S(2)}) copy-start(f32[64]{0:T(128)} %param.12) | copy-start | bytes 772
  174.6 9.0 %copy-start.5 = (bf16[9,64,64]{2,1,0:T(8,128)(2,1)S(1)}, bf16[9,64,64]{2,1,0:T(8,128)(2,1)}, u32[]{:S(2)}) copy-start(bf16[9,64,64]{2,1,0:T(8,128)(2,1)} %w_ref.1) | copy-start | bytes 221188
  177.2 26.7 %all-to-all-start.6 = ((bf16[16,80,256]{2,1,0:T(8,128)(2,1)}), bf16[16,80,256]{2,1,0:T(8,128)(2,1)S(1)}, u32[]{:S(2)}, u32[]{:S(2)}) async-start(bf16[16,80,256]{2,1,0:T(8,128)(2,1)} %shard_map.81), calls=%async_computation.6 | async-start | bytes 1310720 | tf_op jit(solution)/shard_map/all_to_all | solution.py:448
  183.7 1.1 copy-start.3
  203.9 10.5 %collective-permute-start = (bf16[4,80,128]{2,1,0:T(8,128)(2,1)S(1)}, bf16[4,80,128]{2,1,0:T(8,128)(2,1)S(1)}, u32[]{:S(2)}, u32[]{:S(2)}) collective-permute-start(bf16[4,80,128]{2,1,0:T(8,128)(2,1)S(1)} %get-tuple-element.22), channel_id=1, source_target_pairs={{0,16},{16,32},{32,48},{48,64},{64,80},{80,96},{96,112},{112,128},... | collective-permute-start | bytes 245768 | tf_op jit(solution)/shard_map/ppermute | solution.py:504
  208.5 6.3 %collective-permute-start.1 = (bf16[4,80,128]{2,1,0:T(8,128)(2,1)S(1)}, bf16[4,80,128]{2,1,0:T(8,128)(2,1)S(1)}, u32[]{:S(2)}, u32[]{:S(2)}) collective-permute-start(bf16[4,80,128]{2,1,0:T(8,128)(2,1)S(1)} %get-tuple-element.21), channel_id=1, source_target_pairs={{16,0},{32,16},{48,32},{64,48},{80,64},{96,80},{112,96},{128,112},... | collective-permute-start | bytes 245768 | tf_op jit(solution)/shard_map/ppermute | solution.py:505

commit v3 on v2

--- a/solution.py
+++ b/solution.py
@@ -121,14 +121,31 @@
         )
 
 
-def pack_kernel(x_ref, s_ref):
+def weight_tile(r, og, it):
+    index = r * 9 + og * 3 + it
+    return index // 7, index % 7
+
+
+def pack_kernel(x_ref, w_ref, s_ref):
     spread = widen()
+    blank = jnp.zeros((8, 128), f32)
     for a in range(4):
         wide = [dot(x_ref[3 * a + t], spread) for t in range(3)]
         for b in range(4):
             first, last = close_cells(*(w[:, b * 128 : (b + 1) * 128] for w in wide))
-            s_ref[a * 4 + b, :, 0:128] = first.astype(bf16)
-            s_ref[a * 4 + b, :, 128:256] = last.astype(bf16)
+            tiles = {}
+            for r in range(3):
+                weights = w_ref[3 * b + r].astype(f32)
+                for og in range(3):
+                    for it in range(3):
+                        tiles[weight_tile(r, og, it)] = weights[
+                            8 * og : 8 * og + 8, 128 * it : 128 * it + 128
+                        ]
+            for side, cells in enumerate((first, last)):
+                parts = [tiles.get((a, 2 * row + side), blank) for row in range(4)]
+                s_ref[a * 4 + b, :, pl.ds(side * 128, 128)] = jnp.concatenate(
+                    [cells, *parts], axis=0
+                ).astype(bf16)
 
 
 def dft_tables_kernel(p_ref, q_ref, cb_ref, sb_ref, pt_ref, qt_ref, cbt_ref, sbt_ref, c_ref, g_ref):
@@ -141,7 +158,7 @@
         ).astype(bf16)
 
 
-def dft_kernel(c_ref, x_ref, w_ref, s_ref, state_ref, y_ref):
+def dft_kernel(c_ref, x_ref, w_ref, s_ref, state_ref, part_ref, y_ref):
     for q in range(16):
         cells = x_ref[q].astype(f32)
         first, last = cells[:, 0:128], cells[:, 128:256]
@@ -149,6 +166,11 @@
         state_ref[rows, 0:128] = first[:64].astype(bf16)
         state_ref[rows, 128:256] = reopen_cells(first, last).astype(bf16)
         state_ref[rows, 256:384] = last[:64].astype(bf16)
+        parts = [
+            cells[72 + i // 2 * 8 : 80 + i // 2 * 8, i % 2 * 128 : i % 2 * 128 + 128]
+            for i in range(7)
+        ]
+        part_ref[q] = jnp.concatenate(parts, axis=0).astype(bf16)
     for block in range(4):
         rows = pl.ds(block * 256, 256)
         result = dot(c_ref[rows, :], state_ref[...]) * w_ref[...]
@@ -225,24 +247,20 @@
     close_modes(out_ref, s_ref)
 
 
-def mix_weight_kernel(w_ref, o_ref):
-    part = w_ref[...].astype(f32).reshape(384, 384).astype(bf16)
-    wide = dot(part, widen()).astype(bf16)
+def mix_weight_kernel(w_ref, o_ref, full_ref):
+    spread = widen()
     o_ref[...] = jnp.zeros(o_ref.shape, bf16)
-    for b in range(4):
-        o_ref[0, pl.ds(b * 128, 96), :] = wide[b * 96 : (b + 1) * 96]
-
-
-def spread_mix_weight(gathered):
-    return pl.pallas_call(
-        mix_weight_kernel,
-        out_shape=shape((3, 512, 512)),
-        grid=(3,),
-        in_specs=[pl.BlockSpec((16, 1, 24, 384), lambda r: (0, r, 0, 0))],
-        out_specs=pl.BlockSpec((1, 512, 512), lambda r: (r, 0, 0)),
-        compiler_params=pltpu.CompilerParams(vmem_limit_bytes=24 * MIB),
-        cost_estimate=pl.CostEstimate(flops=10**9, bytes_accessed=3 * 10**6, transcendentals=0),
-    )(gathered)
+    for r in range(3):
+        for og in range(3):
+            for it in range(3):
+                a, i = weight_tile(r, og, it)
+                full_ref[:, og, :, pl.ds(it * 128, 128)] = w_ref[a].astype(f32)[
+                    :, 8 * i : 8 * i + 8
+                ]
+        part = full_ref[...].reshape(384, 384).astype(bf16)
+        wide = dot(part, spread).astype(bf16)
+        for b in range(4):
+            o_ref[r, pl.ds(b * 128, 96), :] = wide[b * 96 : (b + 1) * 96]
 
 
 def mix_kernel(x_ref, w_ref, s_ref, in_ref, out_ref):
@@ -294,19 +312,19 @@
         part = dot(u_ref[...], pick).astype(bf16)
         for b in range(4):
             o_ref[pl.ds(b * 128, 96), pl.ds(q * 256, 256)] = part[b * 96 : (b + 1) * 96]
-    for ds in range(3):
-        for p in range(4):
-            blocks = []
+    for p in range(4):
+        blocks = []
+        for ds in range(3):
             for window in (0, 1, 2, 3, 4, -1):
                 dr = window - p
                 if -1 <= dr <= 1:
                     blocks.append(w_ref[3 * (dr + 1) + ds].astype(f32))
                 else:
                     blocks.append(jnp.zeros((64, 64), f32))
-            c_ref[ds, pl.ds(p * 64, 64), :] = jnp.concatenate(blocks, axis=1).astype(bf16)
-
-
-def fine_kernel(x_ref, u_ref, bias_ref, o_ref, h_ref):
+        c_ref[pl.ds(p * 64, 64), :] = jnp.concatenate(blocks, axis=1).astype(bf16)
+
+
+def fine_kernel(x_ref, u_ref, bias_ref, o_ref, side_ref, h_ref):
     row = iota((8, 128), 0)
     for a in range(4):
         for b in range(4):
@@ -330,11 +348,15 @@
         for block in range(4):
             rows = pl.ds(block * 240, 240)
             value = dot(h_ref[rows, :], u_ref[:, lanes]) + bias_ref[:, lanes]
-            o_ref[q, rows, :] = jax.nn.gelu(value).astype(bf16)
+            value = jax.nn.gelu(value).astype(bf16)
+            for i in range(3):
+                a = block * 3 + i
+                o_ref[q, pl.ds(a * 64, 64), :] = value[i * 80 : i * 80 + 64]
+                side_ref[q, pl.ds(a * 16, 16), :] = value[i * 80 + 64 : i * 80 + 80]
 
 
 def conv_kernel(
-    ends_ref, f_ref, up_ref, down_ref, u_ref, bias_ref, w_ref, cb_ref, o_ref,
+    ends_ref, f_ref, side_ref, up_ref, down_ref, u_ref, bias_ref, w_ref, cb_ref, o_ref,
     h_ref, e_ref, t_ref, s_ref, z_ref, g_ref,
 ):
     for b in range(4):
@@ -342,39 +364,51 @@
         for side, ref in enumerate((up_ref, down_ref)):
             cells = ref[b].astype(f32)
             h_ref[pl.ds(side * 80, 80), lanes] = with_sides(cells[:64], cells[72:80])
-    first = iota((160, 256), 0) < 80
-    keep = jnp.where(first, ends_ref[0], ends_ref[1]) > 0
-    half = iota((80, 128), 1) < 64
+    keep = jnp.where(iota((160, 256), 0) < 80, ends_ref[0], ends_ref[1]) > 0
+
+    def around(q, ref, a, size, start):
+        half = iota((size, 128), 1) < 64
+        below = e_ref[pl.ds(80 + start, size), 0:128]
+        above = e_ref[pl.ds(start, size), 128:256]
+        if a < 11:
+            below = ref[q, pl.ds((a + 1) * size, size), 0:128]
+        if a > 0:
+            above = ref[q, pl.ds((a - 1) * size, size), 128:256]
+        return jnp.where(half, below, above)
+
     for q in range(4):
         lanes = pl.ds(q * 256, 256)
         value = jax.nn.gelu(dot(h_ref[...], u_ref[:, lanes]) + bias_ref[:, lanes])
         e_ref[...] = jnp.where(keep, value, 0.0).astype(bf16)
         for a in range(12):
-            below = e_ref[pl.ds(80, 80), 0:128] if a == 11 else f_ref[q, pl.ds(a * 80 + 80, 80), 0:128]
-            above = e_ref[pl.ds(0, 80), 128:256] if a == 0 else f_ref[q, pl.ds(a * 80 - 80, 80), 128:256]
-            t_ref[q, pl.ds(a * 80, 80), :] = jnp.where(half, below, above)
-    for side, q, amount in ((0, 3, 1), (1, 0, 79)):
-        for a in range(12):
-            rows = pl.ds(a * 80, 80)
-            for t in range(3):
-                part = t_ref[q, rows, :] if t == 2 else f_ref[q, rows, t * 128 : (t + 1) * 128]
-                s_ref[side, rows, pl.ds(t * 128, 128)] = pltpu.roll(
-                    part.astype(f32), amount, 0
-                ).astype(bf16)
+            rows = pl.ds(a * 64, 64)
+            outer = around(q, f_ref, a, 64, 0)
+            t_ref[q, rows, :] = outer
+            if q in (0, 3):
+                side, amount = (0, 1) if q == 3 else (1, 79)
+                edges = pl.ds(a * 16, 16)
+                for t in range(3):
+                    if t < 2:
+                        inner = f_ref[q, rows, t * 128 : (t + 1) * 128]
+                        edge = side_ref[q, edges, t * 128 : (t + 1) * 128]
+                    else:
+                        inner, edge = outer, around(q, side_ref, a, 16, 64)
+                    column = jnp.concatenate([inner, edge], axis=0).astype(f32)
+                    column = pltpu.roll(column, amount, 0)[:64]
+                    s_ref[side, rows, pl.ds(t * 128, 128)] = column.astype(bf16)
     for q in range(4):
-        total = f_ref[q].astype(f32) + cb_ref[...]
-        for ds in range(3):
-            source = q + ds - 1
+        parts = []
+        for source in (q - 1, q, q + 1):
             if 0 <= source < 4:
-                total = total + dot_nt(f_ref[source], w_ref[ds, :, 0:256])
-                total = total + dot_nt(t_ref[source], w_ref[ds, :, 256:384])
+                parts += [f_ref[source], t_ref[source]]
             else:
-                total = total + dot_nt(s_ref[0 if source < 0 else 1], w_ref[ds])
-        z_ref[q] = total.astype(bf16)
+                parts.append(s_ref[0 if source < 0 else 1])
+        total = dot_nt(jnp.concatenate(parts, axis=1), w_ref[...])
+        z_ref[q] = (total + f_ref[q].astype(f32) + cb_ref[...]).astype(bf16)
     row, col = iota((256, 256), 0), iota((256, 256), 1)
     place = jnp.where(col == 4 * (row % 64) + row // 64, 1.0, 0.0).astype(bf16)
     for a in range(12):
-        cells = jnp.concatenate([z_ref[q, pl.ds(a * 80, 64), :] for q in range(4)], axis=0)
+        cells = jnp.concatenate([z_ref[q, pl.ds(a * 64, 64), :] for q in range(4)], axis=0)
         lines = lax.dot_general(cells, place, (((0,), (0,)), ((), ())), preferred_element_type=f32)
         for p in range(4):
             for t in range(2):
@@ -451,9 +485,7 @@
 def local(state_field, mix_weight, upsample_weight, upsample_bias, conv_weight, conv_bias):
     lat = lax.axis_index("lat")
     n = 4 * lat + lax.axis_index("qa")
-    own_degrees = exchange(mix_weight, "qb")
-    gathered = lax.all_gather(own_degrees, "qa", axis=0).reshape(16, 3, 24, 384)
-    packed = call(pack_kernel, shape((16, 72, 256)), state_field, flops=10**9)
+    packed = call(pack_kernel, shape((16, 104, 256)), state_field, mix_weight, flops=10**9)
     arrived = exchange(packed, ("qa", "qb"))
     forward, inverse = dft_tables()
     colatitude = ((3 * n + jnp.arange(384, dtype=jnp.int32) // 128).astype(f32) + 0.5) * (
@@ -461,9 +493,9 @@
     )
     scale = (jnp.sin(colatitude) * (math.pi / 384) * (2.0 * math.pi / 1024))[None, :]
     scratch = [pltpu.VMEM((3, 1024, 128), f32)] * 2
-    spectra, state = call(
+    spectra, state, own = call(
         dft_kernel,
-        (shape((1024, 256)), shape((1024, 384))),
+        (shape((1024, 256)), shape((1024, 384)), shape((16, 56, 128))),
         forward,
         arrived,
         scale,
@@ -473,8 +505,23 @@
     columns = exchange(spectra, ("lat", "qa"))
     basis, basis_t = legendre_tables(n)
     coeffs = call(legendre_kernel, shape((1024, 256)), columns, basis, scratch=scratch, flops=10**9)
+    spread_up, spread_conv = call(
+        tail_weights_kernel,
+        (shape((512, 1024)), shape((256, 1152))),
+        upsample_weight,
+        conv_weight,
+        flops=2 * 10**9,
+    )
+    coeffs, spread_up, spread_conv = lax.optimization_barrier((coeffs, spread_up, spread_conv))
     degrees = exchange(coeffs, ("lat", "qb"))
-    mixer = spread_mix_weight(gathered)
+    gathered = lax.all_gather(own, "qa", axis=0)
+    mixer = call(
+        mix_weight_kernel,
+        shape((3, 512, 512)),
+        gathered,
+        scratch=[pltpu.VMEM((16, 3, 8, 384), f32)],
+        flops=10**9,
+    )
     mixed = call(mix_kernel, shape((1024, 256)), degrees, mixer, scratch=scratch, flops=10**9)
     returned = exchange(mixed, ("lat", "qb"))
     synthesized = call(
@@ -491,22 +538,15 @@
         flops=10**9,
     )
     cells = exchange(hidden, ("qa", "qb"))
-    spread_up, spread_conv = call(
-        tail_weights_kernel,
-        (shape((512, 1024)), shape((3, 256, 384))),
-        upsample_weight,
-        conv_weight,
-        flops=2 * 10**9,
-    )
     first_row = cells[0:4, :, 0:128]
     last_row = cells[12:16, :, 128:256]
     count = lax.axis_size("lat")
     up = lax.ppermute(last_row, "lat", [(i, i + 1) for i in range(count - 1)])
     down = lax.ppermute(first_row, "lat", [(i + 1, i) for i in range(count - 1)])
     bias = jnp.tile(upsample_bias, 16)[None, :]
-    fine = call(
+    fine, sides = call(
         fine_kernel,
-        shape((4, 960, 256)),
+        (shape((4, 768, 256)), shape((4, 192, 256))),
         cells,
         spread_up,
         bias,
@@ -519,6 +559,7 @@
         shape((64, 48, 256)),
         ends,
         fine,
+        sides,
         up,
         down,
         spread_up,
@@ -529,9 +570,9 @@
         scratch=[
             pltpu.VMEM((160, 512), bf16),
             pltpu.VMEM((160, 256), bf16),
-            pltpu.VMEM((4, 960, 128), bf16),
-            pltpu.VMEM((2, 960, 384), bf16),
-            pltpu.VMEM((4, 960, 256), bf16),
+            pltpu.VMEM((4, 768, 128), bf16),
+            pltpu.VMEM((2, 768, 384), bf16),
+            pltpu.VMEM((4, 768, 256), bf16),
             pltpu.VMEM((2, 3072, 128), f32),
         ],
         flops=10**10,

time: 223 us -> 218 us (0.978)
  waiting for transfers between devices: 46.4 us -> 40.6 us
  local copies, waits for them, and re-layouts: 10.7 us -> 14.8 us
  starting transfers between devices: 56.9 us -> 54.4 us
    all_to_all x5 -> x4, waiting for transfers between devices: 46 us -> 40.3 us  [exchange(): return lax.all_to_all(x, axes, 0, 0, tiled=True)]
    unnamed x30 -> x42, local copies, waits for them, and re-layouts: 10.2 us -> 14.3 us
    all_to_all x5 -> x4, starting transfers between devices: 48.4 us -> 45.8 us  [exchange(): return lax.all_to_all(x, axes, 0, 0, tiled=True)]
    pallas_call x11 -> x12, Pallas kernels: 26.6 us -> 28.1 us  [call(): pl.pallas_call(kernel, out_shape=out, in_specs=space, out_specs=jax.tree....]
  transfers between devices with their start and end apart: 7 -> 6, of which waited for: 6 -> 5; matrix products, arithmetic and copies ran while one was open for 4% -> 4% of each run, Pallas kernels for 6% -> 5%
where the time goes in v3:
time: 218 us; the launch traced here: 217 us
  blocking collectives  71.4 us (33%)
  starting transfers between devices  54.4 us (25%)
  waiting for transfers between devices  40.6 us (19%)
  Pallas kernels  28.1 us (13%)
  local copies, waits for them, and re-layouts  14.8 us (7%)
  other arithmetic  7.44 us (3%)
    all_to_all x2, blocking collectives, exchange(): return lax.all_to_all(x, axes, 0, 0, tiled=True)  57.4 us
    all_to_all x4, starting transfers between devices, exchange(): return lax.all_to_all(x, axes, 0, 0, tiled=True)  45.8 us
    all_to_all x4, waiting for transfers between devices, exchange(): return lax.all_to_all(x, axes, 0, 0, tiled=True)  40.3 us
    pallas_call x12, Pallas kernels, call(): pl.pallas_call(kernel, out_shape=out, in_specs=space, out_specs=jax.tree....  28.1 us
    unnamed x42, local copies, waits for them, and re-layouts  14.3 us
    all_gather x1, blocking collectives, local(): gathered = lax.all_gather(own, 'qa', axis=0)  14 us
    mul x2, other arithmetic, base(): return (jnp.cos(angle) * scale, jnp.sin(angle) * scale, turn)  4.81 us
    ppermute x1, starting transfers between devices, local(): up = lax.ppermute(last_row, 'lat', [(i, i + 1) for i in range(count - 1)])  4.57 us
  transfers between devices with their start and end apart: 6, of which 5 were waited for; matrix products, arithmetic and copies ran while one was open for 4% of the time, Pallas kernels for 5%

profile of v3, /device:TPU:8, one launch (start us, length us, event | category | flops | bytes accessed | tf_op | source)
XLA Modules:
  0.0 217.1 jit_solution(439448135955715210)
XLA Ops:
  0.0 1.1 copy-done.3
  2.0 1.9 shard_map.74
  3.9 12.9 %all-to-all-start = ((bf16[16,104,256]{2,1,0:T(8,128)(2,1)}), bf16[16,104,256]{2,1,0:T(8,128)(2,1)S(1)}, u32[]{:S(2)}, u32[]{:S(2)}) async-start(bf16[16,104,256]{2,1,0:T(8,128)(2,1)} %shard_map.74), calls=%async_computation | async-start | bytes 1703936 | tf_op jit(solution)/shard_map/all_to_all | solution.py:482
  17.4 2.7 %select_multiply_fusion = (f32[1024,128]{1,0:T(8,128)S(1)}, f32[1024,128]{1,0:T(8,128)S(1)}) fusion(s32[1024]{0:T(1024)S(1)} %get-tuple-element.44, s32[1024]{0:T(1024)S(1)} %get-tuple-element.45, pred[1024]{0:T(1024)(128)(4,1)S(1)} %get-tuple-element.47, s32[1024]{0:T(1024)S(1)} %get-tuple-element.43, s32[1024]{0:T(1024)S(1)} %get-tuple-element.46, ...), kind=kLoop, calls=%fused_computation.20 | loop fusion | flops 4063232 | bytes 1067008 | tf_op jit(solution)/shard_map/mul | solution.py:467
  20.1 2.2 sine_multiply_fusion
  22.2 1.9 multiply_sine_fusion
  24.1 3.1 %shard_map.73 = (bf16[1024,1024]{1,0:T(8,128)(2,1)S(1)}, bf16[1024,1024]{1,0:T(8,128)(2,1)S(1)}) custom-call(f32[1024,128]{1,0:T(8,128)S(1)} %get-tuple-element.42.p_ref, f32[1024,128]{1,0:T(8,128)S(1)} %get-tuple-element.41.q_ref, f32[1024,8]{1,0:T(8,128)S(1)} %get-tuple-element.36.cb_ref, f32[1024,8]{1,0:T(8,128)S(1)} %get-tuple-element.35.sb_ref, ...), custom_call_target="tpu_custom_call" | custom-call | flops 4000000000 | bytes 6422528 | tf_op jit(solution)/shard_map/pallas_call | solution.py:22
  27.2 1.4 copy-done.6
  28.5 6.7 %all-to-all-done.x_ref = bf16[16,104,256]{2,1,0:T(8,128)(2,1)S(1)} async-done(((bf16[16,104,256]{2,1,0:T(8,128)(2,1)}), bf16[16,104,256]{2,1,0:T(8,128)(2,1)S(1)}, u32[]{:S(2)}, u32[]{:S(2)}) %all-to-all-start) | async-done | bytes 852000 | tf_op jit(solution)/shard_map/all_to_all | solution.py:482
  35.2 1.6 copy-done.7
  36.8 2.3 %shard_map.75 = (bf16[1024,256]{1,0:T(8,128)(2,1)}, bf16[1024,384]{1,0:T(8,128)(2,1)S(1)}, bf16[16,56,128]{2,1,0:T(8,128)(2,1)S(1)}) custom-call(bf16[1024,1024]{1,0:T(8,128)(2,1)S(1)} %copy-done.7, bf16[16,104,256]{2,1,0:T(8,128)(2,1)S(1)} %all-to-all-done.x_ref, f32[1,384]{1,0:T(1,128)S(1)} %fusion.61.w_ref), custom_call_target="tpu_custom_call" | custom-call | flops 1000000000 | bytes 4490752 | tf_op jit(solution)/shard_map/pallas_call | solution.py:22
  40.0 20.1 %all-to-all-start.1 = ((bf16[128,8,256]{2,1,0:T(8,128)(2,1)}), bf16[128,8,256]{2,1,0:T(8,128)(2,1)S(1)}, u32[]{:S(2)}, u32[]{:S(2)}) async-start(bf16[128,8,256]{2,1,0:T(8,128)(2,1)} %bitcast.2), calls=%async_computation.1 | async-start | bytes 1048576 | tf_op jit(solution)/shard_map/all_to_all | solution.py:482
  60.4 1.1 copy-done.2
  64.5 4.1 %shard_map.76 = (bf16[3,384,384]{2,1,0:T(8,128)(2,1)S(1)}, bf16[3,384,384]{2,1,0:T(8,128)(2,1)S(1)}) custom-call(f32[8,128]{1,0:T(8,128)S(1)} %broadcast_in_dim.72.order_ref, f32[8,384]{1,0:T(8,128)S(1)} %broadcast_in_dim.73.cosine_ref, f32[8,384]{1,0:T(8,128)S(1)} %exponential_select_fusion.start_ref), custom_call_target="tpu_custom_call" | custom-call | flops 4000000000 | bytes 1798144 | tf_op jit(solution)/shard_map/pallas_call | solution.py:22
  70.4 9.6 %all-to-all-done.1 = bf16[128,8,256]{2,1,0:T(8,128)(2,1)S(1)} async-done(((bf16[128,8,256]{2,1,0:T(8,128)(2,1)}), bf16[128,8,256]{2,1,0:T(8,128)(2,1)S(1)}, u32[]{:S(2)}, u32[]{:S(2)}) %all-to-all-start.1) | async-done | bytes 524320 | tf_op jit(solution)/shard_map/all_to_all | solution.py:482
  80.0 1.2 copy-done.13
  81.1 2.1 shard_map.77
  83.2 6.5 %all-to-all-start.2 = ((bf16[128,8,256]{2,1,0:T(8,128)(2,1)}), bf16[128,8,256]{2,1,0:T(8,128)(2,1)S(1)}, u32[]{:S(2)}, u32[]{:S(2)}) async-start(bf16[128,8,256]{2,1,0:T(8,128)(2,1)} %bitcast.4), calls=%async_computation.2 | async-start | bytes 1048576 | tf_op jit(solution)/shard_map/all_to_all | solution.py:482
  89.7 14.0 %all-gather = bf16[64,56,128]{2,1,0:T(8,128)(2,1)S(1)} all-gather(bf16[16,56,128]{2,1,0:T(8,128)(2,1)S(1)} %get-tuple-element.26), channel_id=2, replica_groups=mesh['lat'=32,'qa'=4,'qb'=4] {'qa'}, dimensions={0}, use_global_device_ids=true | all-gather | bytes 1146880 | tf_op jit(solution)/shard_map/all_gather | solution.py:517
  104.5 1.1 copy-done.8
  105.6 3.8 %all-to-all-done.2 = bf16[128,8,256]{2,1,0:T(8,128)(2,1)S(1)} async-done(((bf16[128,8,256]{2,1,0:T(8,128)(2,1)}), bf16[128,8,256]{2,1,0:T(8,128)(2,1)S(1)}, u32[]{:S(2)}, u32[]{:S(2)}) %all-to-all-start.2) | async-done | bytes 524320 | tf_op jit(solution)/shard_map/all_to_all | solution.py:482
  109.4 1.4 copy-done.9
  111.8 29.4 %all_to_all.54 = bf16[128,8,256]{2,1,0:T(8,128)(2,1)S(1)} all-to-all(bf16[128,8,256]{2,1,0:T(8,128)(2,1)S(1)} %bitcast.16), channel_id=1, replica_groups=mesh['lat'=32,'qa'=4,'qb'=4] {'lat','qb'}, dimensions={0} | all-to-all | bytes 1048576 | tf_op jit(solution)/shard_map/all_to_all | solution.py:482
  141.3 1.3 shard_map.81
  142.6 28.0 %all_to_all.55 = bf16[128,8,256]{2,1,0:T(8,128)(2,1)S(1)} all-to-all(bf16[128,8,256]{2,1,0:T(8,128)(2,1)S(1)} %bitcast.17), channel_id=1, replica_groups=mesh['lat'=32,'qa'=4,'qb'=4] {'lat','qa'}, dimensions={0} | all-to-all | bytes 1048576 | tf_op jit(solution)/shard_map/all_to_all | solution.py:482
  170.6 2.5 %shard_map.82 = bf16[16,80,256]{2,1,0:T(8,128)(2,1)} custom-call(bf16[1024,1024]{1,0:T(8,128)(2,1)S(1)} %get-tuple-element.19.g_ref, bf16[1024,256]{1,0:T(8,128)(2,1)S(1)} %bitcast.11, bf16[1024,384]{1,0:T(8,128)(2,1)S(1)} %copy-done.1), custom_call_target="tpu_custom_call" | custom-call | flops 1000000000 | bytes 4063232 | tf_op jit(solution)/shard_map/pallas_call | solution.py:22
  173.1 6.4 %all-to-all-start.5 = ((bf16[16,80,256]{2,1,0:T(8,128)(2,1)}), bf16[16,80,256]{2,1,0:T(8,128)(2,1)S(1)}, u32[]{:S(2)}, u32[]{:S(2)}) async-start(bf16[16,80,256]{2,1,0:T(8,128)(2,1)} %shard_map.82), calls=%async_computation.5 | async-start | bytes 1310720 | tf_op jit(solution)/shard_map/all_to_all | solution.py:482
  179.8 20.2 %all-to-all-done.5.x_ref = bf16[16,80,256]{2,1,0:T(8,128)(2,1)S(1)} async-done(((bf16[16,80,256]{2,1,0:T(8,128)(2,1)}), bf16[16,80,256]{2,1,0:T(8,128)(2,1)S(1)}, u32[]{:S(2)}, u32[]{:S(2)}) %all-to-all-start.5) | async-done | bytes 655392 | tf_op jit(solution)/shard_map/all_to_all | solution.py:482
  200.0 4.6 %collective-permute-start = (bf16[4,80,128]{2,1,0:T(8,128)(2,1)S(1)}, bf16[4,80,128]{2,1,0:T(8,128)(2,1)S(1)}, u32[]{:S(2)}, u32[]{:S(2)}) collective-permute-start(bf16[4,80,128]{2,1,0:T(8,128)(2,1)S(1)} %get-tuple-element.34), channel_id=1, source_target_pairs={{0,16},{16,32},{32,48},{48,64},{64,80},{80,96},{96,112},{112,128},... | collective-permute-start | bytes 245768 | tf_op jit(solution)/shard_map/ppermute | solution.py:544
  204.6 4.1 %collective-permute-start.1 = (bf16[4,80,128]{2,1,0:T(8,128)(2,1)S(1)}, bf16[4,80,128]{2,1,0:T(8,128)(2,1)S(1)}, u32[]{:S(2)}, u32[]{:S(2)}) collective-permute-start(bf16[4,80,128]{2,1,0:T(8,128)(2,1)S(1)} %get-tuple-element.33), channel_id=1, source_target_pairs={{16,0},{32,16},{48,32},{64,48},{80,64},{96,80},{112,96},{128,112},... | collective-permute-start | bytes 245768 | tf_op jit(solution)/shard_map/ppermute | solution.py:545
  208.7 2.0 shard_map.83
  211.1 6.0 %shard_map.84 = bf16[64,48,256]{2,1,0:T(8,128)(2,1)} custom-call(s32[2]{0:T(128)S(1)} %add_convert_fusion.ends_ref, bf16[4,768,256]{2,1,0:T(8,128)(2,1)S(1)} %get-tuple-element.30.f_ref, bf16[4,192,256]{2,1,0:T(8,128)(2,1)S(1)} %get-tuple-element.31.side_ref, bf16[4,80,128]{2,1,0:T(8,128)(2,1)S(1)} %collective-permute-done.up_ref, ...), custom_call_target="tpu_custom_call" | custom-call | flops 10000000000 | bytes 5346312 | tf_op jit(solution)/shard_map/pallas_call | solution.py:22
  (60 shorter events, 9.9 us)
Async XLA Ops:
  0.0 1.1 copy-start.3
  1.1 0.9 copy-start.4
  3.9 31.3 %all-to-all-start = ((bf16[16,104,256]{2,1,0:T(8,128)(2,1)}), bf16[16,104,256]{2,1,0:T(8,128)(2,1)S(1)}, u32[]{:S(2)}, u32[]{:S(2)}) async-start(bf16[16,104,256]{2,1,0:T(8,128)(2,1)} %shard_map.74), calls=%async_computation | async-start | bytes 1703936 | tf_op jit(solution)/shard_map/all_to_all | solution.py:482
  27.2 1.4 copy-start.6
  35.2 1.6 copy-start.7
  36.8 23.4 %copy-start.18 = (f32[384]{0:T(512)S(1)}, f32[384]{0:T(512)}, u32[]{:S(2)}) copy-start(f32[384]{0:T(512)} %constant.215.clone) | copy-start | bytes 4612
  36.8 23.6 %copy-start.5 = (bf16[9,64,64]{2,1,0:T(8,128)(2,1)S(1)}, bf16[9,64,64]{2,1,0:T(8,128)(2,1)}, u32[]{:S(2)}) copy-start(bf16[9,64,64]{2,1,0:T(8,128)(2,1)} %w_ref.3) | copy-start | bytes 221188
  39.1 0.9 copy-start
  40.0 40.0 %all-to-all-start.1 = ((bf16[128,8,256]{2,1,0:T(8,128)(2,1)}), bf16[128,8,256]{2,1,0:T(8,128)(2,1)S(1)}, u32[]{:S(2)}, u32[]{:S(2)}) async-start(bf16[128,8,256]{2,1,0:T(8,128)(2,1)} %bitcast.2), calls=%async_computation.1 | async-start | bytes 1048576 | tf_op jit(solution)/shard_map/all_to_all | solution.py:482
  60.4 1.1 copy-start.2
  62.5 1.0 copy-start.14
  63.5 0.8 copy-start.16
  68.5 0.9 copy-start.10
  69.5 0.9 copy-start.12
  80.0 1.2 copy-start.13
  83.2 26.2 %all-to-all-start.2 = ((bf16[128,8,256]{2,1,0:T(8,128)(2,1)}), bf16[128,8,256]{2,1,0:T(8,128)(2,1)S(1)}, u32[]{:S(2)}, u32[]{:S(2)}) async-start(bf16[128,8,256]{2,1,0:T(8,128)(2,1)} %bitcast.4), calls=%async_computation.2 | async-start | bytes 1048576 | tf_op jit(solution)/shard_map/all_to_all | solution.py:482
  104.5 1.1 copy-start.8
  109.4 1.4 copy-start.9
  110.8 30.5 %copy-start.11 = (bf16[3,384,384]{2,1,0:T(8,128)(2,1)S(1)}, bf16[3,384,384]{2,1,0:T(8,128)(2,1)}, u32[]{:S(2)}) copy-start(bf16[3,384,384]{2,1,0:T(8,128)(2,1)} %copy-done.10) | copy-start | bytes 2654212
  141.3 29.3 %copy-start.1 = (bf16[1024,384]{1,0:T(8,128)(2,1)S(1)}, bf16[1024,384]{1,0:T(8,128)(2,1)}, u32[]{:S(2)}) copy-start(bf16[1024,384]{1,0:T(8,128)(2,1)} %copy-done) | copy-start | bytes 2359300
  170.6 8.9 %copy-start.19 = (f32[64]{0:T(128)S(1)}, f32[64]{0:T(128)}, u32[]{:S(2)}) copy-start(f32[64]{0:T(128)} %param.10) | copy-start | bytes 772
  170.6 9.0 %copy-start.20 = (f32[64]{0:T(128)S(1)}, f32[64]{0:T(128)}, u32[]{:S(2)}) copy-start(f32[64]{0:T(128)} %param.12) | copy-start | bytes 772
  173.1 35.6 %copy-start.15 = (bf16[512,1024]{1,0:T(8,128)(2,1)S(1)}, bf16[512,1024]{1,0:T(8,128)(2,1)}, u32[]{:S(2)}) copy-start(bf16[512,1024]{1,0:T(8,128)(2,1)} %copy-done.14) | copy-start | bytes 3145732
  173.1 26.9 %all-to-all-start.5 = ((bf16[16,80,256]{2,1,0:T(8,128)(2,1)}), bf16[16,80,256]{2,1,0:T(8,128)(2,1)S(1)}, u32[]{:S(2)}, u32[]{:S(2)}) async-start(bf16[16,80,256]{2,1,0:T(8,128)(2,1)} %shard_map.82), calls=%async_computation.5 | async-start | bytes 1310720 | tf_op jit(solution)/shard_map/all_to_all | solution.py:482
  200.0 10.7 %collective-permute-start = (bf16[4,80,128]{2,1,0:T(8,128)(2,1)S(1)}, bf16[4,80,128]{2,1,0:T(8,128)(2,1)S(1)}, u32[]{:S(2)}, u32[]{:S(2)}) collective-permute-start(bf16[4,80,128]{2,1,0:T(8,128)(2,1)S(1)} %get-tuple-element.34), channel_id=1, source_target_pairs={{0,16},{16,32},{32,48},{48,64},{64,80},{80,96},{96,112},{112,128},... | collective-permute-start | bytes 245768 | tf_op jit(solution)/shard_map/ppermute | solution.py:544
  204.6 6.5 %copy-start.17 = (bf16[256,1152]{1,0:T(8,128)(2,1)S(1)}, bf16[256,1152]{1,0:T(8,128)(2,1)}, u32[]{:S(2)}) copy-start(bf16[256,1152]{1,0:T(8,128)(2,1)} %copy-done.16) | copy-start | bytes 1769476
  204.6 6.5 %collective-permute-start.1 = (bf16[4,80,128]{2,1,0:T(8,128)(2,1)S(1)}, bf16[4,80,128]{2,1,0:T(8,128)(2,1)S(1)}, u32[]{:S(2)}, u32[]{:S(2)}) collective-permute-start(bf16[4,80,128]{2,1,0:T(8,128)(2,1)S(1)} %get-tuple-element.33), channel_id=1, source_target_pairs={{16,0},{32,16},{48,32},{64,48},{80,64},{96,80},{112,96},{128,112},... | collective-permute-start | bytes 245768 | tf_op jit(solution)/shard_map/ppermute | solution.py:545

commit v4 on v3

--- a/solution.py
+++ b/solution.py
@@ -1,3 +1,4 @@
+import functools
 import math
 
 import jax
@@ -153,6 +154,7 @@
         c_ref[:, pl.ds(b * 128, 128)] = (
             p_ref[...] * cb_ref[:, b : b + 1] - q_ref[...] * sb_ref[:, b : b + 1]
         ).astype(bf16)
+    for b in range(4):
         g_ref[pl.ds(b * 128, 128), :] = (
             pt_ref[...] * cbt_ref[b : b + 1, :] - qt_ref[...] * sbt_ref[b : b + 1, :]
         ).astype(bf16)
@@ -171,15 +173,20 @@
             for i in range(7)
         ]
         part_ref[q] = jnp.concatenate(parts, axis=0).astype(bf16)
-    for block in range(4):
-        rows = pl.ds(block * 256, 256)
-        result = dot(c_ref[rows, :], state_ref[...]) * w_ref[...]
+    for t in range(3):
+        for j in (6, 7):
+            y_ref[t, mode_row(j), :] = jnp.zeros((128, 128), f32)
+    for block in range(3):
+        result = dot(c_ref[pl.ds(block * 256, 256), :], state_ref[...]) * w_ref[...]
         for t in range(3):
-            y_ref[t, rows, :] = result[:, t * 128 : (t + 1) * 128]
+            for i in range(2):
+                y_ref[t, mode_row(2 * block + i), :] = result[
+                    i * 128 : (i + 1) * 128, t * 128 : (t + 1) * 128
+                ]
     close_modes(y_ref, s_ref)
 
 
-def legendre_tables_kernel(order_ref, cosine_ref, start_ref, l_ref, t_ref, rows_ref):
+def legendre_tables_kernel(order_ref, cosine_ref, start_ref, l_ref, rows_ref):
     order = order_ref[...]
     squared = order * order
     rows_ref[...] = jnp.zeros(rows_ref.shape, f32)
@@ -225,10 +232,9 @@
             parts = [rows_ref[t, pl.ds(r * 8 + m3, 128, stride=24), :] for r in range(3)]
             table = jnp.concatenate(parts, axis=0)
             l_ref[m3, :, pl.ds(t * 128, 128)] = table.astype(bf16)
-            t_ref[m3, pl.ds(t * 128, 128), :] = table.T.astype(bf16)
-
-
-def legendre_kernel(x_ref, l_ref, s_ref, in_ref, out_ref):
+
+
+def legendre_kernel(side, x_ref, l_ref, s_ref, in_ref, out_ref):
     reopen_modes(x_ref, in_ref)
     out_ref[...] = jnp.zeros(out_ref.shape, f32)
     for m3 in range(3):
@@ -238,7 +244,12 @@
             )
             for cs in range(2)
         ]
-        result = dot(l_ref[m3], jnp.concatenate(halves, axis=1).astype(bf16))
+        result = lax.dot_general(
+            l_ref[m3],
+            jnp.concatenate(halves, axis=1).astype(bf16),
+            (((side,), (0,)), ((), ())),
+            preferred_element_type=f32,
+        )
         for t in range(3):
             for cs in range(2):
                 out_ref[t, pl.ds(cs * 3 + m3, 128, stride=8), :] = result[
@@ -276,12 +287,20 @@
 
 def inverse_kernel(g_ref, x_ref, state_ref, s_ref, y_ref, m_ref, h_ref):
     reopen_modes(x_ref, y_ref)
-    for t in range(3):
-        m_ref[:, pl.ds(t * 128, 128)] = y_ref[t].astype(bf16)
-    for block in range(4):
+    for parity in range(2):
+        for j in range(6):
+            first = (parity + j % 3) % 2 * 8 + j
+            rows = pl.ds(parity * 384 + j * 64, 64)
+            for t in range(3):
+                part = y_ref[t, pl.ds(first, 64, stride=16), :]
+                m_ref[rows, pl.ds(t * 128, 128)] = part.astype(bf16)
+    for block in range(2):
         rows = pl.ds(block * 256, 256)
-        spatial = dot(g_ref[rows, :], m_ref[...])
-        h_ref[rows, :] = state_ref[rows, :].astype(f32) + jax.nn.gelu(spatial)
+        even = dot(g_ref[rows, 0:384], m_ref[0:384, :])
+        odd = dot(g_ref[rows, 384:768], m_ref[384:768, :])
+        for half, spatial in enumerate((even + odd, even - odd)):
+            rows = pl.ds(half * 512 + block * 256, 256)
+            h_ref[rows, :] = state_ref[rows, :].astype(f32) + jax.nn.gelu(spatial)
     row = iota((8, 128), 0)
     for q in range(16):
         inner, halo = [], []
@@ -442,7 +461,7 @@
     orders = jnp.broadcast_to(order.astype(f32)[:, None], (8, 128))
     return call(
         legendre_tables_kernel,
-        (shape((3, 384, 384)), shape((3, 384, 384))),
+        shape((3, 384, 384)),
         orders,
         cosine,
         start,
@@ -454,26 +473,27 @@
 def dft_tables():
     step = 2.0 * math.pi / 1024
 
-    def base(row_axis, dims):
-        k, y = iota(dims, row_axis), iota(dims, 1 - row_axis)
-        j = k % 8
-        wave = 3 * (k // 8) + j % 3
-        used = j < 6
-        angle = ((wave * y + jnp.where(j < 3, 0, 256)) % 1024).astype(f32) * step
-        scale = jnp.where(used, 1.0, 0.0)
-        if row_axis == 1:
-            scale = scale * jnp.where(wave == 0, 1.0, 2.0)
-        turn = (wave * y % 8).astype(f32) * (math.pi / 4)
-        return jnp.cos(angle) * scale, jnp.sin(angle) * scale, turn
-
-    p, q, _ = base(0, (1024, 128))
-    turn = base(0, (1024, 8))[2]
-    pt, qt, _ = base(1, (128, 1024))
-    turn_t = base(1, (8, 1024))[2]
+    def waves(wave, sine, y, scale):
+        angle = ((wave * y + 256 * sine) % 1024).astype(f32) * step
+        return jnp.cos(angle) * scale, jnp.sin(angle) * scale
+
+    def turns(wave, block):
+        turn = (wave * block % 8).astype(f32) * (math.pi / 4)
+        return jnp.cos(turn), jnp.sin(turn)
+
+    row = jnp.arange(768, dtype=jnp.int32)[:, None]
+    wave, sine = 3 * (row % 128) + row // 128 % 3, row // 384
+    forward = (*waves(wave, sine, iota((1, 128), 1), 1.0), *turns(wave, iota((1, 8), 1)))
+    col = jnp.arange(768, dtype=jnp.int32)[None, :]
+    j = col % 384 // 64
+    wave = 3 * (2 * (col % 64) + (col // 384 + j % 3) % 2) + j % 3
+    scale = jnp.where(wave == 0, 1.0, 2.0)
+    inverse = (*waves(wave, j // 3, iota((128, 1), 0), scale), *turns(wave, iota((8, 1), 0)))
     return call(
         dft_tables_kernel,
-        (shape((1024, 1024)), shape((1024, 1024))),
-        p, q, jnp.cos(turn), jnp.sin(turn), pt, qt, jnp.cos(turn_t), jnp.sin(turn_t),
+        (shape((768, 1024)), shape((512, 768))),
+        *forward,
+        *inverse,
         flops=4 * 10**9,
     )
 
@@ -488,6 +508,8 @@
     packed = call(pack_kernel, shape((16, 104, 256)), state_field, mix_weight, flops=10**9)
     arrived = exchange(packed, ("qa", "qb"))
     forward, inverse = dft_tables()
+    basis = legendre_tables(n)
+    arrived, basis = lax.optimization_barrier((arrived, basis))
     colatitude = ((3 * n + jnp.arange(384, dtype=jnp.int32) // 128).astype(f32) + 0.5) * (
         math.pi / 384
     )
@@ -503,8 +525,12 @@
         flops=10**9,
     )
     columns = exchange(spectra, ("lat", "qa"))
-    basis, basis_t = legendre_tables(n)
-    coeffs = call(legendre_kernel, shape((1024, 256)), columns, basis, scratch=scratch, flops=10**9)
+
+    def transform(x, side):
+        kernel = functools.partial(legendre_kernel, side)
+        return call(kernel, shape((1024, 256)), x, basis, scratch=scratch, flops=10**9)
+
+    coeffs = transform(columns, 1)
     spread_up, spread_conv = call(
         tail_weights_kernel,
         (shape((512, 1024)), shape((256, 1152))),
@@ -512,9 +538,9 @@
         conv_weight,
         flops=2 * 10**9,
     )
-    coeffs, spread_up, spread_conv = lax.optimization_barrier((coeffs, spread_up, spread_conv))
+    gathered = lax.all_gather(own, "qa", axis=0)
+    coeffs, gathered = lax.optimization_barrier((coeffs, gathered))
     degrees = exchange(coeffs, ("lat", "qb"))
-    gathered = lax.all_gather(own, "qa", axis=0)
     mixer = call(
         mix_weight_kernel,
         shape((3, 512, 512)),
@@ -523,10 +549,9 @@
         flops=10**9,
     )
     mixed = call(mix_kernel, shape((1024, 256)), degrees, mixer, scratch=scratch, flops=10**9)
+    mixed, spread_up, spread_conv = lax.optimization_barrier((mixed, spread_up, spread_conv))
     returned = exchange(mixed, ("lat", "qb"))
-    synthesized = call(
-        legendre_kernel, shape((1024, 256)), returned, basis_t, scratch=scratch, flops=10**9
-    )
+    synthesized = transform(returned, 0)
     modes = exchange(synthesized, ("lat", "qa"))
     hidden = call(
         inverse_kernel,
@@ -534,7 +559,7 @@
         inverse,
         modes,
         state,
-        scratch=[scratch[0], pltpu.VMEM((1024, 384), bf16), pltpu.VMEM((1024, 384), f32)],
+        scratch=[scratch[0], pltpu.VMEM((768, 384), bf16), pltpu.VMEM((1024, 384), f32)],
         flops=10**9,
     )
     cells = exchange(hidden, ("qa", "qb"))

time: 218 us -> 213 us (0.977)
  local copies, waits for them, and re-layouts: 14.8 us -> 6.92 us
  starting transfers between devices: 54.4 us -> 58 us
  waiting for transfers between devices: 40.6 us -> 43.3 us
    unnamed x42 -> x36, local copies, waits for them, and re-layouts: 14.3 us -> 6.5 us
    all_gather x1, blocking collectives: 14 us -> 18.2 us  [local(): gathered = lax.all_gather(own, 'qa', axis=0)]
    all_to_all x2, blocking collectives: 57.4 us -> 53.4 us  [exchange(): return lax.all_to_all(x, axes, 0, 0, tiled=True)]
    all_to_all x4, starting transfers between devices: 45.8 us -> 49.3 us  [exchange(): return lax.all_to_all(x, axes, 0, 0, tiled=True)]
    mul x2 -> x1, other arithmetic: 4.81 us -> 1.58 us  [waves(): return (jnp.cos(angle) * scale, jnp.sin(angle) * scale)]
    all_to_all x4, waiting for transfers between devices: 40.3 us -> 42.9 us  [exchange(): return lax.all_to_all(x, axes, 0, 0, tiled=True)]
  transfers between devices with their start and end apart: 6 -> 6, of which waited for: 5 -> 5; matrix products, arithmetic and copies ran while one was open for 4% -> 3% of each run, Pallas kernels for 5% -> 5%
where the time goes in v4:
time: 213 us
  blocking collectives  71.6 us (34%)
  starting transfers between devices  58 us (27%)
  waiting for transfers between devices  43.3 us (20%)
  Pallas kernels  27.4 us (13%)
  local copies, waits for them, and re-layouts  6.92 us (3%)
  other arithmetic  5.37 us (3%)
    all_to_all x2, blocking collectives, exchange(): return lax.all_to_all(x, axes, 0, 0, tiled=True)  53.4 us
    all_to_all x4, starting transfers between devices, exchange(): return lax.all_to_all(x, axes, 0, 0, tiled=True)  49.3 us
    all_to_all x4, waiting for transfers between devices, exchange(): return lax.all_to_all(x, axes, 0, 0, tiled=True)  42.9 us
    pallas_call x12, Pallas kernels, call(): pl.pallas_call(kernel, out_shape=out, in_specs=space, out_specs=jax.tree....  27.4 us
    all_gather x1, blocking collectives, local(): gathered = lax.all_gather(own, 'qa', axis=0)  18.2 us
    unnamed x36, local copies, waits for them, and re-layouts  6.5 us
    ppermute x1, starting transfers between devices, local(): up = lax.ppermute(last_row, 'lat', [(i, i + 1) for i in range(count - 1)])  4.56 us
  transfers between devices with their start and end apart: 6, of which 5 were waited for; matrix products, arithmetic and copies ran while one was open for 3% of the time, Pallas kernels for 5%

profile of v4, /device:TPU:8, one launch (start us, length us, event | category | flops | bytes accessed | tf_op | source)
XLA Modules:
  0.0 212.8 jit_solution(3066137205736507168)
XLA Ops:
  0.0 1.1 copy-done.1
  1.1 0.9 copy-done.2
  2.0 1.9 shard_map.74
  3.9 13.0 %all-to-all-start = ((bf16[16,104,256]{2,1,0:T(8,128)(2,1)}), bf16[16,104,256]{2,1,0:T(8,128)(2,1)S(1)}, u32[]{:S(2)}, u32[]{:S(2)}) async-start(bf16[16,104,256]{2,1,0:T(8,128)(2,1)} %shard_map.74), calls=%async_computation | async-start | bytes 1703936 | tf_op jit(solution)/shard_map/all_to_all | solution.py:502
  17.8 1.6 fusion.6
  19.4 1.6 sine_multiply_fusion
  21.0 1.4 multiply_sine_fusion
  22.5 4.0 %shard_map.75.l_ref = bf16[3,384,384]{2,1,0:T(8,128)(2,1)S(1)} custom-call(f32[8,128]{1,0:T(8,128)S(1)} %broadcast_in_dim.28.order_ref, f32[8,384]{1,0:T(8,128)S(1)} %broadcast_in_dim.29.cosine_ref, f32[8,384]{1,0:T(8,128)S(1)} %exponential_select_fusion.start_ref), custom_call_target="tpu_custom_call" | custom-call | flops 4000000000 | bytes 913408 | tf_op jit(solution)/shard_map/pallas_call | solution.py:23
  26.6 0.9 copy-done.8
  27.5 2.0 shard_map.73
  30.3 5.0 %all-to-all-done.x_ref = bf16[16,104,256]{2,1,0:T(8,128)(2,1)S(1)} async-done(((bf16[16,104,256]{2,1,0:T(8,128)(2,1)}), bf16[16,104,256]{2,1,0:T(8,128)(2,1)S(1)}, u32[]{:S(2)}, u32[]{:S(2)}) %all-to-all-start) | async-done | bytes 852000 | tf_op jit(solution)/shard_map/all_to_all | solution.py:502
  35.3 2.4 %shard_map.76 = (bf16[1024,256]{1,0:T(8,128)(2,1)}, bf16[1024,384]{1,0:T(8,128)(2,1)S(1)}, bf16[16,56,128]{2,1,0:T(8,128)(2,1)S(1)}) custom-call(bf16[768,1024]{1,0:T(8,128)(2,1)S(1)} %get-tuple-element.22.c_ref, bf16[16,104,256]{2,1,0:T(8,128)(2,1)S(1)} %all-to-all-done.x_ref, f32[1,384]{1,0:T(1,128)S(1)} %fusion.71.w_ref), custom_call_target="tpu_custom_call" | custom-call | flops 1000000000 | bytes 3966464 | tf_op jit(solution)/shard_map/pallas_call | solution.py:23
  37.7 0.9 copy-done.6
  38.6 20.2 %all-to-all-start.1 = ((bf16[128,8,256]{2,1,0:T(8,128)(2,1)}), bf16[128,8,256]{2,1,0:T(8,128)(2,1)S(1)}, u32[]{:S(2)}, u32[]{:S(2)}) async-start(bf16[128,8,256]{2,1,0:T(8,128)(2,1)} %bitcast.2), calls=%async_computation.1 | async-start | bytes 1048576 | tf_op jit(solution)/shard_map/all_to_all | solution.py:502
  58.8 18.2 %all-gather = bf16[64,56,128]{2,1,0:T(8,128)(2,1)S(1)} all-gather(bf16[16,56,128]{2,1,0:T(8,128)(2,1)S(1)} %get-tuple-element.26), channel_id=2, replica_groups=mesh['lat'=32,'qa'=4,'qb'=4] {'qa'}, dimensions={0}, use_global_device_ids=true | all-gather | bytes 1146880 | tf_op jit(solution)/shard_map/all_gather | solution.py:541
  77.1 1.6 all-to-all-done.1
  78.7 2.1 shard_map.77
  80.8 9.7 %all-to-all-start.2 = ((bf16[128,8,256]{2,1,0:T(8,128)(2,1)}), bf16[128,8,256]{2,1,0:T(8,128)(2,1)S(1)}, u32[]{:S(2)}, u32[]{:S(2)}) async-start(bf16[128,8,256]{2,1,0:T(8,128)(2,1)} %bitcast.5), calls=%async_computation.2 | async-start | bytes 1048576 | tf_op jit(solution)/shard_map/all_to_all | solution.py:502
  90.6 1.0 shard_map.80
  91.6 1.0 copy-done.11
  94.2 16.1 %all-to-all-done.2 = bf16[128,8,256]{2,1,0:T(8,128)(2,1)S(1)} async-done(((bf16[128,8,256]{2,1,0:T(8,128)(2,1)}), bf16[128,8,256]{2,1,0:T(8,128)(2,1)S(1)}, u32[]{:S(2)}, u32[]{:S(2)}) %all-to-all-start.2) | async-done | bytes 524320 | tf_op jit(solution)/shard_map/all_to_all | solution.py:502
  110.3 1.0 shard_map.79
  111.3 25.7 %all_to_all.54 = bf16[128,8,256]{2,1,0:T(8,128)(2,1)S(1)} all-to-all(bf16[128,8,256]{2,1,0:T(8,128)(2,1)S(1)} %bitcast.15), channel_id=1, replica_groups=mesh['lat'=32,'qa'=4,'qb'=4] {'lat','qb'}, dimensions={0} | all-to-all | bytes 1048576 | tf_op jit(solution)/shard_map/all_to_all | solution.py:502
  137.0 1.6 shard_map.81
  138.6 27.6 %all_to_all.55 = bf16[128,8,256]{2,1,0:T(8,128)(2,1)S(1)} all-to-all(bf16[128,8,256]{2,1,0:T(8,128)(2,1)S(1)} %bitcast.17), channel_id=1, replica_groups=mesh['lat'=32,'qa'=4,'qb'=4] {'lat','qa'}, dimensions={0} | all-to-all | bytes 1048576 | tf_op jit(solution)/shard_map/all_to_all | solution.py:502
  166.2 2.6 %shard_map.82 = bf16[16,80,256]{2,1,0:T(8,128)(2,1)} custom-call(bf16[512,768]{1,0:T(8,128)(2,1)S(1)} %copy-done.5, bf16[1024,256]{1,0:T(8,128)(2,1)S(1)} %bitcast.14, bf16[1024,384]{1,0:T(8,128)(2,1)S(1)} %copy-done.7), custom_call_target="tpu_custom_call" | custom-call | flops 1000000000 | bytes 2752512 | tf_op jit(solution)/shard_map/pallas_call | solution.py:23
  168.8 6.4 %all-to-all-start.5 = ((bf16[16,80,256]{2,1,0:T(8,128)(2,1)}), bf16[16,80,256]{2,1,0:T(8,128)(2,1)S(1)}, u32[]{:S(2)}, u32[]{:S(2)}) async-start(bf16[16,80,256]{2,1,0:T(8,128)(2,1)} %shard_map.82), calls=%async_computation.5 | async-start | bytes 1310720 | tf_op jit(solution)/shard_map/all_to_all | solution.py:502
  175.5 20.2 %all-to-all-done.5.x_ref = bf16[16,80,256]{2,1,0:T(8,128)(2,1)S(1)} async-done(((bf16[16,80,256]{2,1,0:T(8,128)(2,1)}), bf16[16,80,256]{2,1,0:T(8,128)(2,1)S(1)}, u32[]{:S(2)}, u32[]{:S(2)}) %all-to-all-start.5) | async-done | bytes 655392 | tf_op jit(solution)/shard_map/all_to_all | solution.py:502
  195.7 4.6 %collective-permute-start = (bf16[4,80,128]{2,1,0:T(8,128)(2,1)S(1)}, bf16[4,80,128]{2,1,0:T(8,128)(2,1)S(1)}, u32[]{:S(2)}, u32[]{:S(2)}) collective-permute-start(bf16[4,80,128]{2,1,0:T(8,128)(2,1)S(1)} %get-tuple-element.38), channel_id=1, source_target_pairs={{0,16},{16,32},{32,48},{48,64},{64,80},{80,96},{96,112},{112,128},... | collective-permute-start | bytes 245768 | tf_op jit(solution)/shard_map/ppermute | solution.py:569
  200.3 4.1 %collective-permute-start.1 = (bf16[4,80,128]{2,1,0:T(8,128)(2,1)S(1)}, bf16[4,80,128]{2,1,0:T(8,128)(2,1)S(1)}, u32[]{:S(2)}, u32[]{:S(2)}) collective-permute-start(bf16[4,80,128]{2,1,0:T(8,128)(2,1)S(1)} %get-tuple-element.37), channel_id=1, source_target_pairs={{16,0},{32,16},{48,32},{64,48},{80,64},{96,80},{112,96},{128,112},... | collective-permute-start | bytes 245768 | tf_op jit(solution)/shard_map/ppermute | solution.py:570
  204.4 2.0 shard_map.83
  206.8 6.0 %shard_map.84 = bf16[64,48,256]{2,1,0:T(8,128)(2,1)} custom-call(s32[2]{0:T(128)S(1)} %add_convert_fusion.ends_ref, bf16[4,768,256]{2,1,0:T(8,128)(2,1)S(1)} %get-tuple-element.34.f_ref, bf16[4,192,256]{2,1,0:T(8,128)(2,1)S(1)} %get-tuple-element.35.side_ref, bf16[4,80,128]{2,1,0:T(8,128)(2,1)S(1)} %collective-permute-done.up_ref, ...), custom_call_target="tpu_custom_call" | custom-call | flops 10000000000 | bytes 5346312 | tf_op jit(solution)/shard_map/pallas_call | solution.py:23
  (54 shorter events, 4.0 us)
Async XLA Ops:
  0.0 1.1 copy-start.1
  1.1 0.9 copy-start.2
  3.9 13.5 %copy-start.15 = (f32[384]{0:T(512)S(1)}, f32[384]{0:T(512)}, u32[]{:S(2)}) copy-start(f32[384]{0:T(512)} %constant.216.clone) | copy-start | bytes 4612
  3.9 31.4 %all-to-all-start = ((bf16[16,104,256]{2,1,0:T(8,128)(2,1)}), bf16[16,104,256]{2,1,0:T(8,128)(2,1)S(1)}, u32[]{:S(2)}, u32[]{:S(2)}) async-start(bf16[16,104,256]{2,1,0:T(8,128)(2,1)} %shard_map.74), calls=%async_computation | async-start | bytes 1703936 | tf_op jit(solution)/shard_map/all_to_all | solution.py:502
  26.6 0.9 copy-start.8
  29.5 0.9 copy-start.4
  37.7 0.9 copy-start.6
  38.6 40.1 %copy-start.9 = (bf16[3,384,384]{2,1,0:T(8,128)(2,1)S(1)}, bf16[3,384,384]{2,1,0:T(8,128)(2,1)}, u32[]{:S(2)}) copy-start(bf16[3,384,384]{2,1,0:T(8,128)(2,1)} %copy-done.8) | copy-start | bytes 2654212
  38.6 40.1 %all-to-all-start.1 = ((bf16[128,8,256]{2,1,0:T(8,128)(2,1)}), bf16[128,8,256]{2,1,0:T(8,128)(2,1)S(1)}, u32[]{:S(2)}, u32[]{:S(2)}) async-start(bf16[128,8,256]{2,1,0:T(8,128)(2,1)} %bitcast.2), calls=%async_computation.1 | async-start | bytes 1048576 | tf_op jit(solution)/shard_map/all_to_all | solution.py:502
  78.7 11.9 %copy-start = (bf16[384,1024]{1,0:T(8,128)(2,1)S(1)}, bf16[384,1024]{1,0:T(8,128)(2,1)}, u32[]{:S(2)}) copy-start(bf16[384,1024]{1,0:T(8,128)(2,1)} %u_ref.1) | copy-start | bytes 2359300
  78.7 11.9 %copy-start.3 = (bf16[9,64,64]{2,1,0:T(8,128)(2,1)S(1)}, bf16[9,64,64]{2,1,0:T(8,128)(2,1)}, u32[]{:S(2)}) copy-start(bf16[9,64,64]{2,1,0:T(8,128)(2,1)} %w_ref.3) | copy-start | bytes 221188
  80.8 29.4 %all-to-all-start.2 = ((bf16[128,8,256]{2,1,0:T(8,128)(2,1)}), bf16[128,8,256]{2,1,0:T(8,128)(2,1)S(1)}, u32[]{:S(2)}, u32[]{:S(2)}) async-start(bf16[128,8,256]{2,1,0:T(8,128)(2,1)} %bitcast.5), calls=%async_computation.2 | async-start | bytes 1048576 | tf_op jit(solution)/shard_map/all_to_all | solution.py:502
  91.6 1.0 copy-start.11
  92.6 0.8 copy-start.13
  110.3 26.8 %copy-start.10 = (bf16[3,384,384]{2,1,0:T(8,128)(2,1)S(1)}, bf16[3,384,384]{2,1,0:T(8,128)(2,1)}, u32[]{:S(2)}) copy-start(bf16[3,384,384]{2,1,0:T(8,128)(2,1)} %copy-done.8) | copy-start | bytes 2654212
  137.0 29.2 %copy-start.5 = (bf16[512,768]{1,0:T(8,128)(2,1)S(1)}, bf16[512,768]{1,0:T(8,128)(2,1)}, u32[]{:S(2)}) copy-start(bf16[512,768]{1,0:T(8,128)(2,1)} %copy-done.4) | copy-start | bytes 2359300
  137.0 29.2 %copy-start.7 = (bf16[1024,384]{1,0:T(8,128)(2,1)S(1)}, bf16[1024,384]{1,0:T(8,128)(2,1)}, u32[]{:S(2)}) copy-start(bf16[1024,384]{1,0:T(8,128)(2,1)} %copy-done.6) | copy-start | bytes 2359300
  166.2 9.0 %copy-start.16 = (f32[64]{0:T(128)S(1)}, f32[64]{0:T(128)}, u32[]{:S(2)}) copy-start(f32[64]{0:T(128)} %param.10) | copy-start | bytes 772
  166.2 9.1 %copy-start.17 = (f32[64]{0:T(128)S(1)}, f32[64]{0:T(128)}, u32[]{:S(2)}) copy-start(f32[64]{0:T(128)} %param.12) | copy-start | bytes 772
  168.8 35.6 %copy-start.12 = (bf16[512,1024]{1,0:T(8,128)(2,1)S(1)}, bf16[512,1024]{1,0:T(8,128)(2,1)}, u32[]{:S(2)}) copy-start(bf16[512,1024]{1,0:T(8,128)(2,1)} %copy-done.11) | copy-start | bytes 3145732
  168.8 26.9 %all-to-all-start.5 = ((bf16[16,80,256]{2,1,0:T(8,128)(2,1)}), bf16[16,80,256]{2,1,0:T(8,128)(2,1)S(1)}, u32[]{:S(2)}, u32[]{:S(2)}) async-start(bf16[16,80,256]{2,1,0:T(8,128)(2,1)} %shard_map.82), calls=%async_computation.5 | async-start | bytes 1310720 | tf_op jit(solution)/shard_map/all_to_all | solution.py:502
  195.7 10.7 %collective-permute-start = (bf16[4,80,128]{2,1,0:T(8,128)(2,1)S(1)}, bf16[4,80,128]{2,1,0:T(8,128)(2,1)S(1)}, u32[]{:S(2)}, u32[]{:S(2)}) collective-permute-start(bf16[4,80,128]{2,1,0:T(8,128)(2,1)S(1)} %get-tuple-element.38), channel_id=1, source_target_pairs={{0,16},{16,32},{32,48},{48,64},{64,80},{80,96},{96,112},{112,128},... | collective-permute-start | bytes 245768 | tf_op jit(solution)/shard_map/ppermute | solution.py:569
  200.3 6.5 %copy-start.14 = (bf16[256,1152]{1,0:T(8,128)(2,1)S(1)}, bf16[256,1152]{1,0:T(8,128)(2,1)}, u32[]{:S(2)}) copy-start(bf16[256,1152]{1,0:T(8,128)(2,1)} %copy-done.13) | copy-start | bytes 1769476
  200.3 6.5 %collective-permute-start.1 = (bf16[4,80,128]{2,1,0:T(8,128)(2,1)S(1)}, bf16[4,80,128]{2,1,0:T(8,128)(2,1)S(1)}, u32[]{:S(2)}, u32[]{:S(2)}) collective-permute-start(bf16[4,80,128]{2,1,0:T(8,128)(2,1)S(1)} %get-tuple-element.37), channel_id=1, source_target_pairs={{16,0},{32,16},{48,32},{64,48},{80,64},{96,80},{112,96},{128,112},... | collective-permute-start | bytes 245768 | tf_op jit(solution)/shard_map/ppermute | solution.py:570

commit v5 on v4

--- a/solution.py
+++ b/solution.py
@@ -14,9 +14,12 @@
 MIB = 1 << 20
 
 
-def call(kernel, out, *args, scratch=(), flops=0, smem=(), vmem=40):
+def call(kernel, out, *args, scratch=(), flops=0, smem=(), far=(), vmem=40):
     space = [
-        pl.BlockSpec(memory_space=pltpu.SMEM if i in smem else pltpu.VMEM) for i in range(len(args))
+        pl.BlockSpec(
+            memory_space=pltpu.SMEM if i in smem else pltpu.HBM if i in far else pltpu.VMEM
+        )
+        for i in range(len(args))
     ]
     outs = out if isinstance(out, (tuple, list)) else (out,)
     moved = sum(x.size * x.dtype.itemsize for x in (*args, *outs))
@@ -24,7 +27,9 @@
         kernel,
         out_shape=out,
         in_specs=space,
-        out_specs=jax.tree.map(lambda _: pl.BlockSpec(memory_space=pltpu.VMEM), out),
+        out_specs=jax.tree.map(
+            lambda _: pl.BlockSpec(memory_space=pltpu.HBM if "out" in far else pltpu.VMEM), out
+        ),
         scratch_shapes=list(scratch),
         compiler_params=pltpu.CompilerParams(vmem_limit_bytes=vmem * MIB),
         cost_estimate=pl.CostEstimate(flops=flops, bytes_accessed=moved, transcendentals=0),
@@ -127,10 +132,19 @@
     return index // 7, index % 7
 
 
-def pack_kernel(x_ref, w_ref, s_ref):
+def pack_kernel(x_far, w_far, s_far, x_ref, w_ref, s_ref, in_sems, out_sems):
+    arriving = [pltpu.make_async_copy(w_far, w_ref, in_sems.at[4])]
+    for a in range(4):
+        rows = pl.ds(3 * a, 3)
+        arriving.append(pltpu.make_async_copy(x_far.at[rows], x_ref.at[rows], in_sems.at[a]))
+    for copy in arriving:
+        copy.start()
+    arriving[0].wait()
+    leaving = []
     spread = widen()
     blank = jnp.zeros((8, 128), f32)
     for a in range(4):
+        arriving[a + 1].wait()
         wide = [dot(x_ref[3 * a + t], spread) for t in range(3)]
         for b in range(4):
             first, last = close_cells(*(w[:, b * 128 : (b + 1) * 128] for w in wide))
@@ -147,6 +161,11 @@
                 s_ref[a * 4 + b, :, pl.ds(side * 128, 128)] = jnp.concatenate(
                     [cells, *parts], axis=0
                 ).astype(bf16)
+        done = pl.ds(a * 4, 4)
+        leaving.append(pltpu.make_async_copy(s_ref.at[done], s_far.at[done], out_sems.at[a]))
+        leaving[a].start()
+    for copy in leaving:
+        copy.wait()
 
 
 def dft_tables_kernel(p_ref, q_ref, cb_ref, sb_ref, pt_ref, qt_ref, cbt_ref, sbt_ref, c_ref, g_ref):
@@ -323,7 +342,7 @@
     return jnp.concatenate([inner, halo, pltpu.roll(halo, 6, 0)], axis=0).astype(bf16)
 
 
-def tail_weights_kernel(u_ref, w_ref, o_ref, c_ref):
+def tail_weights_kernel(u_ref, w_ref, o_ref, c_ref, y_ref):
     o_ref[...] = jnp.zeros(o_ref.shape, bf16)
     row, col = iota((1024, 256), 0), iota((1024, 256), 1)
     for q in range(4):
@@ -340,7 +359,14 @@
                     blocks.append(w_ref[3 * (dr + 1) + ds].astype(f32))
                 else:
                     blocks.append(jnp.zeros((64, 64), f32))
-        c_ref[pl.ds(p * 64, 64), :] = jnp.concatenate(blocks, axis=1).astype(bf16)
+        wide = jnp.concatenate(blocks, axis=1)
+        for t in range(9):
+            y_ref[t, pl.ds(p, 64, stride=4), :] = wide[:, t * 128 : (t + 1) * 128]
+    for t in range(9):
+        c_ref[:, pl.ds(t * 128, 128)] = y_ref[t].astype(bf16)
+    row, col = iota((256, 256), 0), iota((256, 256), 1)
+    same = (row // 4 == col % 64) & (row % 4 == col // 64)
+    c_ref[:, 1152:1408] = jnp.where(same, 1.0, 0.0).astype(bf16)
 
 
 def fine_kernel(x_ref, u_ref, bias_ref, o_ref, side_ref, h_ref):
@@ -422,20 +448,25 @@
                 parts += [f_ref[source], t_ref[source]]
             else:
                 parts.append(s_ref[0 if source < 0 else 1])
-        total = dot_nt(jnp.concatenate(parts, axis=1), w_ref[...])
-        z_ref[q] = (total + f_ref[q].astype(f32) + cb_ref[...]).astype(bf16)
+        total = dot_nt(jnp.concatenate([*parts, f_ref[q]], axis=1), w_ref[...])
+        z_ref[q] = (total + cb_ref[...]).astype(bf16)
     row, col = iota((256, 256), 0), iota((256, 256), 1)
     place = jnp.where(col == 4 * (row % 64) + row // 64, 1.0, 0.0).astype(bf16)
-    for a in range(12):
-        cells = jnp.concatenate([z_ref[q, pl.ds(a * 64, 64), :] for q in range(4)], axis=0)
-        lines = lax.dot_general(cells, place, (((0,), (0,)), ((), ())), preferred_element_type=f32)
-        for p in range(4):
-            for t in range(2):
-                g_ref[t, pl.ds(4 * a + p, 64, stride=48), :] = lines[
-                    p * 64 : (p + 1) * 64, t * 128 : (t + 1) * 128
-                ]
-    for t in range(2):
-        o_ref[:, :, pl.ds(t * 128, 128)] = g_ref[t].reshape(64, 48, 128).astype(bf16)
+    low = iota((32, 8, 256), 1) < 4
+    for h in range(6):
+        pair = []
+        for a in (2 * h, 2 * h + 1):
+            cells = jnp.concatenate([z_ref[q, pl.ds(a * 64, 64), :] for q in range(4)], axis=0)
+            lines = lax.dot_general(
+                cells, place, (((0,), (0,)), ((), ())), preferred_element_type=f32
+            )
+            pair.append(lines.reshape(32, 8, 256))
+        turned = [pltpu.roll(lines, 4, 1) for lines in pair]
+        first = jnp.where(low, pair[0], turned[1])
+        second = jnp.where(low, turned[0], pair[1])
+        both = jnp.stack([first, second], axis=1).reshape(64, 8, 256)
+        g_ref[:, pl.ds(8 * h, 8), :] = both
+    o_ref[...] = g_ref[...].astype(bf16)
 
 
 def start_logs(degrees):
@@ -505,7 +536,22 @@
 def local(state_field, mix_weight, upsample_weight, upsample_bias, conv_weight, conv_bias):
     lat = lax.axis_index("lat")
     n = 4 * lat + lax.axis_index("qa")
-    packed = call(pack_kernel, shape((16, 104, 256)), state_field, mix_weight, flops=10**9)
+    packed = call(
+        pack_kernel,
+        shape((16, 104, 256)),
+        state_field,
+        mix_weight,
+        far=(0, 1, "out"),
+        vmem=60,
+        scratch=[
+            pltpu.VMEM((12, 64, 384), bf16),
+            pltpu.VMEM((12, 24, 384), bf16),
+            pltpu.VMEM((16, 104, 256), bf16),
+            pltpu.SemaphoreType.DMA((5,)),
+            pltpu.SemaphoreType.DMA((4,)),
+        ],
+        flops=10**9,
+    )
     arrived = exchange(packed, ("qa", "qb"))
     forward, inverse = dft_tables()
     basis = legendre_tables(n)
@@ -533,9 +579,10 @@
     coeffs = transform(columns, 1)
     spread_up, spread_conv = call(
         tail_weights_kernel,
-        (shape((512, 1024)), shape((256, 1152))),
+        (shape((512, 1024)), shape((256, 1408))),
         upsample_weight,
         conv_weight,
+        scratch=[pltpu.VMEM((9, 256, 128), f32)],
         flops=2 * 10**9,
     )
     gathered = lax.all_gather(own, "qa", axis=0)
@@ -590,7 +637,7 @@
         spread_up,
         bias,
         spread_conv,
-        jnp.tile(conv_bias, 4)[None, :],
+        jnp.repeat(conv_bias, 4)[None, :],
         smem=(0,),
         scratch=[
             pltpu.VMEM((160, 512), bf16),
@@ -598,7 +645,7 @@
             pltpu.VMEM((4, 768, 128), bf16),
             pltpu.VMEM((2, 768, 384), bf16),
             pltpu.VMEM((4, 768, 256), bf16),
-            pltpu.VMEM((2, 3072, 128), f32),
+            pltpu.VMEM((64, 48, 256), f32),
         ],
         flops=10**10,
     )

time: 213 us -> 212 us (level)
    unnamed x36 -> x32, local copies, waits for them, and re-layouts: 6.5 us -> 4.54 us
where the time goes in v5:
time: 212 us; the launch traced here: 211 us
  blocking collectives  71.4 us (34%)
  starting transfers between devices  57.7 us (27%)
  waiting for transfers between devices  43.1 us (20%)
  Pallas kernels  28.1 us (13%)
  other arithmetic  5.37 us (3%)
  local copies, waits for them, and re-layouts  5.06 us (2%)
    all_to_all x2, blocking collectives, exchange(): return lax.all_to_all(x, axes, 0, 0, tiled=True)  53.3 us
    all_to_all x4, starting transfers between devices, exchange(): return lax.all_to_all(x, axes, 0, 0, tiled=True)  49 us
    all_to_all x4, waiting for transfers between devices, exchange(): return lax.all_to_all(x, axes, 0, 0, tiled=True)  42.7 us
    pallas_call x12, Pallas kernels, call(): pl.pallas_call(kernel, out_shape=out, in_specs=space, out_specs=jax.tree....  28.1 us
    all_gather x1, blocking collectives, local(): gathered = lax.all_gather(own, 'qa', axis=0)  18.2 us
    ppermute x1, starting transfers between devices, local(): up = lax.ppermute(last_row, 'lat', [(i, i + 1) for i in range(count - 1)])  4.57 us
    unnamed x32, local copies, waits for them, and re-layouts  4.54 us
  transfers between devices with their start and end apart: 6, of which 5 were waited for; matrix products, arithmetic and copies ran while one was open for 3% of the time, Pallas kernels for 5%

profile of v5, /device:TPU:8, one launch (start us, length us, event | category | flops | bytes accessed | tf_op | source)
XLA Modules:
  0.0 211.1 jit_solution(8601053095625385508)
XLA Ops:
  0.0 3.3 %shard_map.74 = bf16[16,104,256]{2,1,0:T(8,128)(2,1)} custom-call(bf16[12,64,384]{2,1,0:T(8,128)(2,1)} %x_far.1, bf16[12,24,384]{2,1,0:T(8,128)(2,1)} %w_far.1), custom_call_target="tpu_custom_call" | custom-call | flops 1000000000 | bytes 1662976 | tf_op jit(solution)/shard_map/pallas_call | solution.py:26
  3.3 12.8 %all-to-all-start = ((bf16[16,104,256]{2,1,0:T(8,128)(2,1)}), bf16[16,104,256]{2,1,0:T(8,128)(2,1)S(1)}, u32[]{:S(2)}, u32[]{:S(2)}) async-start(bf16[16,104,256]{2,1,0:T(8,128)(2,1)} %shard_map.74), calls=%async_computation | async-start | bytes 1703936 | tf_op jit(solution)/shard_map/all_to_all | solution.py:533
  17.1 1.6 fusion.6
  18.7 1.6 sine_multiply_fusion
  20.3 1.4 multiply_sine_fusion
  21.8 4.0 %shard_map.75.l_ref = bf16[3,384,384]{2,1,0:T(8,128)(2,1)S(1)} custom-call(f32[8,128]{1,0:T(8,128)S(1)} %broadcast_in_dim.30.order_ref, f32[8,384]{1,0:T(8,128)S(1)} %broadcast_in_dim.31.cosine_ref, f32[8,384]{1,0:T(8,128)S(1)} %exponential_select_fusion.start_ref), custom_call_target="tpu_custom_call" | custom-call | flops 4000000000 | bytes 913408 | tf_op jit(solution)/shard_map/pallas_call | solution.py:26
  25.8 0.9 copy-done.6
  26.7 2.0 shard_map.73
  28.7 0.9 copy-done.2
  29.6 5.0 %all-to-all-done.x_ref = bf16[16,104,256]{2,1,0:T(8,128)(2,1)S(1)} async-done(((bf16[16,104,256]{2,1,0:T(8,128)(2,1)}), bf16[16,104,256]{2,1,0:T(8,128)(2,1)S(1)}, u32[]{:S(2)}, u32[]{:S(2)}) %all-to-all-start) | async-done | bytes 852000 | tf_op jit(solution)/shard_map/all_to_all | solution.py:533
  34.6 2.4 %shard_map.76 = (bf16[1024,256]{1,0:T(8,128)(2,1)}, bf16[1024,384]{1,0:T(8,128)(2,1)S(1)}, bf16[16,56,128]{2,1,0:T(8,128)(2,1)S(1)}) custom-call(bf16[768,1024]{1,0:T(8,128)(2,1)S(1)} %get-tuple-element.22.c_ref, bf16[16,104,256]{2,1,0:T(8,128)(2,1)S(1)} %all-to-all-done.x_ref, f32[1,384]{1,0:T(1,128)S(1)} %fusion.71.w_ref), custom_call_target="tpu_custom_call" | custom-call | flops 1000000000 | bytes 3966464 | tf_op jit(solution)/shard_map/pallas_call | solution.py:26
  37.0 0.9 copy-done.4
  37.9 20.2 %all-to-all-start.1 = ((bf16[128,8,256]{2,1,0:T(8,128)(2,1)}), bf16[128,8,256]{2,1,0:T(8,128)(2,1)S(1)}, u32[]{:S(2)}, u32[]{:S(2)}) async-start(bf16[128,8,256]{2,1,0:T(8,128)(2,1)} %bitcast.2), calls=%async_computation.1 | async-start | bytes 1048576 | tf_op jit(solution)/shard_map/all_to_all | solution.py:533
  58.1 18.2 %all-gather = bf16[64,56,128]{2,1,0:T(8,128)(2,1)S(1)} all-gather(bf16[16,56,128]{2,1,0:T(8,128)(2,1)S(1)} %get-tuple-element.26), channel_id=2, replica_groups=mesh['lat'=32,'qa'=4,'qb'=4] {'qa'}, dimensions={0}, use_global_device_ids=true | all-gather | bytes 1146880 | tf_op jit(solution)/shard_map/all_gather | solution.py:588
  76.3 1.7 all-to-all-done.1
  78.0 2.1 shard_map.77
  80.1 9.6 %all-to-all-start.2 = ((bf16[128,8,256]{2,1,0:T(8,128)(2,1)}), bf16[128,8,256]{2,1,0:T(8,128)(2,1)S(1)}, u32[]{:S(2)}, u32[]{:S(2)}) async-start(bf16[128,8,256]{2,1,0:T(8,128)(2,1)} %bitcast.5), calls=%async_computation.2 | async-start | bytes 1048576 | tf_op jit(solution)/shard_map/all_to_all | solution.py:533
  89.7 1.1 shard_map.80
  90.8 1.0 copy-done.9
  91.7 0.9 copy-done.11
  93.4 15.9 %all-to-all-done.2 = bf16[128,8,256]{2,1,0:T(8,128)(2,1)S(1)} async-done(((bf16[128,8,256]{2,1,0:T(8,128)(2,1)}), bf16[128,8,256]{2,1,0:T(8,128)(2,1)S(1)}, u32[]{:S(2)}, u32[]{:S(2)}) %all-to-all-start.2) | async-done | bytes 524320 | tf_op jit(solution)/shard_map/all_to_all | solution.py:533
  109.3 1.0 shard_map.79
  110.4 25.7 %all_to_all.54 = bf16[128,8,256]{2,1,0:T(8,128)(2,1)S(1)} all-to-all(bf16[128,8,256]{2,1,0:T(8,128)(2,1)S(1)} %bitcast.15), channel_id=1, replica_groups=mesh['lat'=32,'qa'=4,'qb'=4] {'lat','qb'}, dimensions={0} | all-to-all | bytes 1048576 | tf_op jit(solution)/shard_map/all_to_all | solution.py:533
  136.1 1.6 shard_map.81
  137.7 27.5 %all_to_all.55 = bf16[128,8,256]{2,1,0:T(8,128)(2,1)S(1)} all-to-all(bf16[128,8,256]{2,1,0:T(8,128)(2,1)S(1)} %bitcast.17), channel_id=1, replica_groups=mesh['lat'=32,'qa'=4,'qb'=4] {'lat','qa'}, dimensions={0} | all-to-all | bytes 1048576 | tf_op jit(solution)/shard_map/all_to_all | solution.py:533
  165.2 2.6 %shard_map.82 = bf16[16,80,256]{2,1,0:T(8,128)(2,1)} custom-call(bf16[512,768]{1,0:T(8,128)(2,1)S(1)} %copy-done.3, bf16[1024,256]{1,0:T(8,128)(2,1)S(1)} %bitcast.14, bf16[1024,384]{1,0:T(8,128)(2,1)S(1)} %copy-done.5), custom_call_target="tpu_custom_call" | custom-call | flops 1000000000 | bytes 2752512 | tf_op jit(solution)/shard_map/pallas_call | solution.py:26
  167.8 6.4 %all-to-all-start.5 = ((bf16[16,80,256]{2,1,0:T(8,128)(2,1)}), bf16[16,80,256]{2,1,0:T(8,128)(2,1)S(1)}, u32[]{:S(2)}, u32[]{:S(2)}) async-start(bf16[16,80,256]{2,1,0:T(8,128)(2,1)} %shard_map.82), calls=%async_computation.5 | async-start | bytes 1310720 | tf_op jit(solution)/shard_map/all_to_all | solution.py:533
  174.5 20.1 %all-to-all-done.5.x_ref = bf16[16,80,256]{2,1,0:T(8,128)(2,1)S(1)} async-done(((bf16[16,80,256]{2,1,0:T(8,128)(2,1)}), bf16[16,80,256]{2,1,0:T(8,128)(2,1)S(1)}, u32[]{:S(2)}, u32[]{:S(2)}) %all-to-all-start.5) | async-done | bytes 655392 | tf_op jit(solution)/shard_map/all_to_all | solution.py:533
  194.7 4.6 %collective-permute-start = (bf16[4,80,128]{2,1,0:T(8,128)(2,1)S(1)}, bf16[4,80,128]{2,1,0:T(8,128)(2,1)S(1)}, u32[]{:S(2)}, u32[]{:S(2)}) collective-permute-start(bf16[4,80,128]{2,1,0:T(8,128)(2,1)S(1)} %get-tuple-element.38), channel_id=1, source_target_pairs={{0,16},{16,32},{32,48},{48,64},{64,80},{80,96},{96,112},{112,128},... | collective-permute-start | bytes 245768 | tf_op jit(solution)/shard_map/ppermute | solution.py:616
  199.3 4.1 %collective-permute-start.1 = (bf16[4,80,128]{2,1,0:T(8,128)(2,1)S(1)}, bf16[4,80,128]{2,1,0:T(8,128)(2,1)S(1)}, u32[]{:S(2)}, u32[]{:S(2)}) collective-permute-start(bf16[4,80,128]{2,1,0:T(8,128)(2,1)S(1)} %get-tuple-element.37), channel_id=1, source_target_pairs={{16,0},{32,16},{48,32},{64,48},{80,64},{96,80},{112,96},{128,112},... | collective-permute-start | bytes 245768 | tf_op jit(solution)/shard_map/ppermute | solution.py:617
  203.4 2.0 shard_map.83
  205.8 5.3 %shard_map.84 = bf16[64,48,256]{2,1,0:T(8,128)(2,1)} custom-call(s32[2]{0:T(128)S(1)} %add_convert_fusion.ends_ref, bf16[4,768,256]{2,1,0:T(8,128)(2,1)S(1)} %get-tuple-element.34.f_ref, bf16[4,192,256]{2,1,0:T(8,128)(2,1)S(1)} %get-tuple-element.35.side_ref, bf16[4,80,128]{2,1,0:T(8,128)(2,1)S(1)} %collective-permute-done.up_ref, ...), custom_call_target="tpu_custom_call" | custom-call | flops 10000000000 | bytes 5477384 | tf_op jit(solution)/shard_map/pallas_call | solution.py:26
  (50 shorter events, 2.5 us)
Async XLA Ops:
  3.3 13.4 %copy-start.13 = (f32[384]{0:T(512)S(1)}, f32[384]{0:T(512)}, u32[]{:S(2)}) copy-start(f32[384]{0:T(512)} %constant.216.clone) | copy-start | bytes 4612
  3.3 31.3 %all-to-all-start = ((bf16[16,104,256]{2,1,0:T(8,128)(2,1)}), bf16[16,104,256]{2,1,0:T(8,128)(2,1)S(1)}, u32[]{:S(2)}, u32[]{:S(2)}) async-start(bf16[16,104,256]{2,1,0:T(8,128)(2,1)} %shard_map.74), calls=%async_computation | async-start | bytes 1703936 | tf_op jit(solution)/shard_map/all_to_all | solution.py:533
  25.8 0.9 copy-start.6
  28.7 0.9 copy-start.2
  37.0 0.9 copy-start.4
  37.9 40.1 %copy-start.7 = (bf16[3,384,384]{2,1,0:T(8,128)(2,1)S(1)}, bf16[3,384,384]{2,1,0:T(8,128)(2,1)}, u32[]{:S(2)}) copy-start(bf16[3,384,384]{2,1,0:T(8,128)(2,1)} %copy-done.6) | copy-start | bytes 2654212
  37.9 40.1 %all-to-all-start.1 = ((bf16[128,8,256]{2,1,0:T(8,128)(2,1)}), bf16[128,8,256]{2,1,0:T(8,128)(2,1)S(1)}, u32[]{:S(2)}, u32[]{:S(2)}) async-start(bf16[128,8,256]{2,1,0:T(8,128)(2,1)} %bitcast.2), calls=%async_computation.1 | async-start | bytes 1048576 | tf_op jit(solution)/shard_map/all_to_all | solution.py:533
  78.0 11.7 %copy-start = (bf16[384,1024]{1,0:T(8,128)(2,1)S(1)}, bf16[384,1024]{1,0:T(8,128)(2,1)}, u32[]{:S(2)}) copy-start(bf16[384,1024]{1,0:T(8,128)(2,1)} %u_ref.1) | copy-start | bytes 2359300
  78.0 11.7 %copy-start.1 = (bf16[9,64,64]{2,1,0:T(8,128)(2,1)S(1)}, bf16[9,64,64]{2,1,0:T(8,128)(2,1)}, u32[]{:S(2)}) copy-start(bf16[9,64,64]{2,1,0:T(8,128)(2,1)} %w_ref.1) | copy-start | bytes 221188
  80.1 29.3 %all-to-all-start.2 = ((bf16[128,8,256]{2,1,0:T(8,128)(2,1)}), bf16[128,8,256]{2,1,0:T(8,128)(2,1)S(1)}, u32[]{:S(2)}, u32[]{:S(2)}) async-start(bf16[128,8,256]{2,1,0:T(8,128)(2,1)} %bitcast.5), calls=%async_computation.2 | async-start | bytes 1048576 | tf_op jit(solution)/shard_map/all_to_all | solution.py:533
  90.8 1.0 copy-start.9
  91.7 0.9 copy-start.11
  109.3 26.8 %copy-start.8 = (bf16[3,384,384]{2,1,0:T(8,128)(2,1)S(1)}, bf16[3,384,384]{2,1,0:T(8,128)(2,1)}, u32[]{:S(2)}) copy-start(bf16[3,384,384]{2,1,0:T(8,128)(2,1)} %copy-done.6) | copy-start | bytes 2654212
  136.1 29.1 %copy-start.3 = (bf16[512,768]{1,0:T(8,128)(2,1)S(1)}, bf16[512,768]{1,0:T(8,128)(2,1)}, u32[]{:S(2)}) copy-start(bf16[512,768]{1,0:T(8,128)(2,1)} %copy-done.2) | copy-start | bytes 2359300
  136.1 29.1 %copy-start.5 = (bf16[1024,384]{1,0:T(8,128)(2,1)S(1)}, bf16[1024,384]{1,0:T(8,128)(2,1)}, u32[]{:S(2)}) copy-start(bf16[1024,384]{1,0:T(8,128)(2,1)} %copy-done.4) | copy-start | bytes 2359300
  165.2 9.0 %copy-start.15 = (f32[64]{0:T(128)S(1)}, f32[64]{0:T(128)}, u32[]{:S(2)}) copy-start(f32[64]{0:T(128)} %param.10) | copy-start | bytes 772
  165.2 9.1 %copy-start.14 = (f32[64]{0:T(128)S(1)}, f32[64]{0:T(128)}, u32[]{:S(2)}) copy-start(f32[64]{0:T(128)} %param.12) | copy-start | bytes 772
  167.8 35.6 %copy-start.10 = (bf16[512,1024]{1,0:T(8,128)(2,1)S(1)}, bf16[512,1024]{1,0:T(8,128)(2,1)}, u32[]{:S(2)}) copy-start(bf16[512,1024]{1,0:T(8,128)(2,1)} %copy-done.9) | copy-start | bytes 3145732
  167.8 26.9 %all-to-all-start.5 = ((bf16[16,80,256]{2,1,0:T(8,128)(2,1)}), bf16[16,80,256]{2,1,0:T(8,128)(2,1)S(1)}, u32[]{:S(2)}, u32[]{:S(2)}) async-start(bf16[16,80,256]{2,1,0:T(8,128)(2,1)} %shard_map.82), calls=%async_computation.5 | async-start | bytes 1310720 | tf_op jit(solution)/shard_map/all_to_all | solution.py:533
  194.7 10.7 %collective-permute-start = (bf16[4,80,128]{2,1,0:T(8,128)(2,1)S(1)}, bf16[4,80,128]{2,1,0:T(8,128)(2,1)S(1)}, u32[]{:S(2)}, u32[]{:S(2)}) collective-permute-start(bf16[4,80,128]{2,1,0:T(8,128)(2,1)S(1)} %get-tuple-element.38), channel_id=1, source_target_pairs={{0,16},{16,32},{32,48},{48,64},{64,80},{80,96},{96,112},{112,128},... | collective-permute-start | bytes 245768 | tf_op jit(solution)/shard_map/ppermute | solution.py:616
  199.3 6.5 %copy-start.12 = (bf16[256,1408]{1,0:T(8,128)(2,1)S(1)}, bf16[256,1408]{1,0:T(8,128)(2,1)}, u32[]{:S(2)}) copy-start(bf16[256,1408]{1,0:T(8,128)(2,1)} %copy-done.11) | copy-start | bytes 2162692
  199.3 6.5 %collective-permute-start.1 = (bf16[4,80,128]{2,1,0:T(8,128)(2,1)S(1)}, bf16[4,80,128]{2,1,0:T(8,128)(2,1)S(1)}, u32[]{:S(2)}, u32[]{:S(2)}) collective-permute-start(bf16[4,80,128]{2,1,0:T(8,128)(2,1)S(1)} %get-tuple-element.37), channel_id=1, source_target_pairs={{16,0},{32,16},{48,32},{64,48},{80,64},{96,80},{112,96},{128,112},... | collective-permute-start | bytes 245768 | tf_op jit(solution)/shard_map/ppermute | solution.py:617

commit v6 on v5

--- a/solution.py
+++ b/solution.py
@@ -156,11 +156,8 @@
                         tiles[weight_tile(r, og, it)] = weights[
                             8 * og : 8 * og + 8, 128 * it : 128 * it + 128
                         ]
-            for side, cells in enumerate((first, last)):
-                parts = [tiles.get((a, 2 * row + side), blank) for row in range(4)]
-                s_ref[a * 4 + b, :, pl.ds(side * 128, 128)] = jnp.concatenate(
-                    [cells, *parts], axis=0
-                ).astype(bf16)
+            parts = [tiles.get((a, i), blank) for i in range(7)]
+            s_ref[a * 4 + b] = jnp.concatenate([first, last, *parts], axis=0).astype(bf16)
         done = pl.ds(a * 4, 4)
         leaving.append(pltpu.make_async_copy(s_ref.at[done], s_far.at[done], out_sems.at[a]))
         leaving[a].start()
@@ -179,19 +176,17 @@
         ).astype(bf16)
 
 
-def dft_kernel(c_ref, x_ref, w_ref, s_ref, state_ref, part_ref, y_ref):
+def dft_kernel(c_ref, x_ref, w_ref, s_ref, state_ref, *rest):
+    *part_refs, y_ref = rest
     for q in range(16):
         cells = x_ref[q].astype(f32)
-        first, last = cells[:, 0:128], cells[:, 128:256]
+        first, last = cells[0:72], cells[72:144]
         rows = pl.ds(q * 64, 64)
         state_ref[rows, 0:128] = first[:64].astype(bf16)
         state_ref[rows, 128:256] = reopen_cells(first, last).astype(bf16)
         state_ref[rows, 256:384] = last[:64].astype(bf16)
-        parts = [
-            cells[72 + i // 2 * 8 : 80 + i // 2 * 8, i % 2 * 128 : i % 2 * 128 + 128]
-            for i in range(7)
-        ]
-        part_ref[q] = jnp.concatenate(parts, axis=0).astype(bf16)
+        for part, ref in enumerate(part_refs):
+            ref[q] = cells[144 + 32 * part : min(176 + 32 * part, 200)].astype(bf16)
     for t in range(3):
         for j in (6, 7):
             y_ref[t, mode_row(j), :] = jnp.zeros((128, 128), f32)
@@ -277,16 +272,15 @@
     close_modes(out_ref, s_ref)
 
 
-def mix_weight_kernel(w_ref, o_ref, full_ref):
+def mix_weight_kernel(w_ref, v_ref, o_ref, full_ref):
     spread = widen()
     o_ref[...] = jnp.zeros(o_ref.shape, bf16)
     for r in range(3):
         for og in range(3):
             for it in range(3):
                 a, i = weight_tile(r, og, it)
-                full_ref[:, og, :, pl.ds(it * 128, 128)] = w_ref[a].astype(f32)[
-                    :, 8 * i : 8 * i + 8
-                ]
+                part = (w_ref, v_ref)[i // 4][a].astype(f32)
+                full_ref[:, og, :, pl.ds(it * 128, 128)] = part[:, i % 4 * 8 : i % 4 * 8 + 8]
         part = full_ref[...].reshape(384, 384).astype(bf16)
         wide = dot(part, spread).astype(bf16)
         for b in range(4):
@@ -538,7 +532,7 @@
     n = 4 * lat + lax.axis_index("qa")
     packed = call(
         pack_kernel,
-        shape((16, 104, 256)),
+        shape((16, 200, 128)),
         state_field,
         mix_weight,
         far=(0, 1, "out"),
@@ -546,7 +540,7 @@
         scratch=[
             pltpu.VMEM((12, 64, 384), bf16),
             pltpu.VMEM((12, 24, 384), bf16),
-            pltpu.VMEM((16, 104, 256), bf16),
+            pltpu.VMEM((16, 200, 128), bf16),
             pltpu.SemaphoreType.DMA((5,)),
             pltpu.SemaphoreType.DMA((4,)),
         ],
@@ -561,9 +555,9 @@
     )
     scale = (jnp.sin(colatitude) * (math.pi / 384) * (2.0 * math.pi / 1024))[None, :]
     scratch = [pltpu.VMEM((3, 1024, 128), f32)] * 2
-    spectra, state, own = call(
+    spectra, state, *own = call(
         dft_kernel,
-        (shape((1024, 256)), shape((1024, 384)), shape((16, 56, 128))),
+        (shape((1024, 256)), shape((1024, 384)), shape((16, 32, 128)), shape((16, 24, 128))),
         forward,
         arrived,
         scale,
@@ -585,13 +579,14 @@
         scratch=[pltpu.VMEM((9, 256, 128), f32)],
         flops=2 * 10**9,
     )
-    gathered = lax.all_gather(own, "qa", axis=0)
-    coeffs, gathered = lax.optimization_barrier((coeffs, gathered))
+    gathered = lax.all_gather(own[0], "qa", axis=0)
+    coeffs, gathered, rest = lax.optimization_barrier((coeffs, gathered, own[1]))
     degrees = exchange(coeffs, ("lat", "qb"))
     mixer = call(
         mix_weight_kernel,
         shape((3, 512, 512)),
         gathered,
+        lax.all_gather(rest, "qa", axis=0),
         scratch=[pltpu.VMEM((16, 3, 8, 384), f32)],
         flops=10**9,
     )

time: 212 us -> 213 us (level)
  blocking collectives: 71.4 us -> 85.7 us
  waiting for transfers between devices: 43.1 us -> 34 us
  starting transfers between devices: 57.7 us -> 54.2 us
    all_to_all x4, waiting for transfers between devices: 42.7 us -> 33.7 us  [exchange(): return lax.all_to_all(x, axes, 0, 0, tiled=True)]
    all_gather x1 -> x2, blocking collectives: 18.2 us -> 26.9 us  [the longest x1 14.1 us: local(): gathered = lax.all_gather(own[0], 'qa', axis=0)]
    all_to_all x2, blocking collectives: 53.3 us -> 58.8 us  [exchange(): return lax.all_to_all(x, axes, 0, 0, tiled=True)]
    all_to_all x4, starting transfers between devices: 49 us -> 45.5 us  [exchange(): return lax.all_to_all(x, axes, 0, 0, tiled=True)]
    unnamed x32 -> x30, local copies, waits for them, and re-layouts: 4.54 us -> 4.63 us
where the time goes in v6:
time: 213 us
  blocking collectives  85.7 us (40%)
  starting transfers between devices  54.2 us (25%)
  waiting for transfers between devices  34 us (16%)
  Pallas kernels  28.1 us (13%)
  other arithmetic  5.37 us (3%)
  local copies, waits for them, and re-layouts  5.15 us (2%)
    all_to_all x2, blocking collectives, exchange(): return lax.all_to_all(x, axes, 0, 0, tiled=True)  58.8 us
    all_to_all x4, starting transfers between devices, exchange(): return lax.all_to_all(x, axes, 0, 0, tiled=True)  45.5 us
    all_to_all x4, waiting for transfers between devices, exchange(): return lax.all_to_all(x, axes, 0, 0, tiled=True)  33.7 us
    pallas_call x12, Pallas kernels, call(): pl.pallas_call(kernel, out_shape=out, in_specs=space, out_specs=jax.tree....  28.1 us
    all_gather x1, blocking collectives, local(): gathered = lax.all_gather(own[0], 'qa', axis=0)  14.1 us
    all_gather x1, blocking collectives, local(): lax.all_gather(rest, 'qa', axis=0)  12.8 us
    unnamed x30, local copies, waits for them, and re-layouts  4.63 us
    ppermute x1, starting transfers between devices, local(): up = lax.ppermute(last_row, 'lat', [(i, i + 1) for i in range(count - 1)])  4.57 us
  transfers between devices with their start and end apart: 6, of which 5 were waited for; matrix products, arithmetic and copies ran while one was open for 3% of the time, Pallas kernels for 5%

profile of v6, /device:TPU:8, one launch (start us, length us, event | category | flops | bytes accessed | tf_op | source)
XLA Modules:
  0.0 212.9 jit_solution(8361509693618991950)
XLA Ops:
  0.0 3.3 %shard_map.74 = bf16[16,200,128]{2,1,0:T(8,128)(2,1)} custom-call(bf16[12,64,384]{2,1,0:T(8,128)(2,1)} %x_far.1, bf16[12,24,384]{2,1,0:T(8,128)(2,1)} %w_far.1), custom_call_target="tpu_custom_call" | custom-call | flops 1000000000 | bytes 1630208 | tf_op jit(solution)/shard_map/pallas_call | solution.py:26
  3.3 12.9 %all-to-all-start = ((bf16[16,200,128]{2,1,0:T(8,128)(2,1)}), bf16[16,200,128]{2,1,0:T(8,128)(2,1)S(1)}, u32[]{:S(2)}, u32[]{:S(2)}) async-start(bf16[16,200,128]{2,1,0:T(8,128)(2,1)} %shard_map.74), calls=%async_computation | async-start | bytes 1638400 | tf_op jit(solution)/shard_map/all_to_all | solution.py:527
  17.1 1.6 fusion.6
  18.7 1.6 sine_multiply_fusion
  20.3 1.4 multiply_sine_fusion
  21.8 4.0 %shard_map.75.l_ref = bf16[3,384,384]{2,1,0:T(8,128)(2,1)S(1)} custom-call(f32[8,128]{1,0:T(8,128)S(1)} %broadcast_in_dim.30.order_ref, f32[8,384]{1,0:T(8,128)S(1)} %broadcast_in_dim.31.cosine_ref, f32[8,384]{1,0:T(8,128)S(1)} %exponential_select_fusion.start_ref), custom_call_target="tpu_custom_call" | custom-call | flops 4000000000 | bytes 913408 | tf_op jit(solution)/shard_map/pallas_call | solution.py:26
  25.8 0.9 copy-done.6
  26.8 2.0 shard_map.73
  28.7 0.9 copy-done.2
  29.7 4.6 %all-to-all-done.x_ref = bf16[16,200,128]{2,1,0:T(8,128)(2,1)S(1)} async-done(((bf16[16,200,128]{2,1,0:T(8,128)(2,1)}), bf16[16,200,128]{2,1,0:T(8,128)(2,1)S(1)}, u32[]{:S(2)}, u32[]{:S(2)}) %all-to-all-start) | async-done | bytes 819232 | tf_op jit(solution)/shard_map/all_to_all | solution.py:527
  34.3 2.4 %shard_map.76 = (bf16[1024,256]{1,0:T(8,128)(2,1)}, bf16[1024,384]{1,0:T(8,128)(2,1)S(1)}, bf16[16,32,128]{2,1,0:T(8,128)(2,1)S(1)}, bf16[16,24,128]{2,1,0:T(8,128)(2,1)S(1)}) custom-call(bf16[768,1024]{1,0:T(8,128)(2,1)S(1)} %get-tuple-element.24.c_ref, bf16[16,200,128]{2,1,0:T(8,128)(2,1)S(1)} %all-to-all-done.x_ref, f32[1,384]{1,0:T(1,128)S(1)} %fusion.71.w_ref), custom_call_target="tpu_custom_call" | custom-call | flops 1000000000 | bytes 3933696 | tf_op jit(solution)/shard_map/pallas_call | solution.py:26
  36.7 0.9 copy-done.4
  37.6 19.8 %all-to-all-start.1 = ((bf16[128,8,256]{2,1,0:T(8,128)(2,1)}), bf16[128,8,256]{2,1,0:T(8,128)(2,1)S(1)}, u32[]{:S(2)}, u32[]{:S(2)}) async-start(bf16[128,8,256]{2,1,0:T(8,128)(2,1)} %bitcast.2), calls=%async_computation.1 | async-start | bytes 1048576 | tf_op jit(solution)/shard_map/all_to_all | solution.py:527
  57.4 14.1 %all-gather = bf16[64,32,128]{2,1,0:T(8,128)(2,1)S(1)} all-gather(bf16[16,32,128]{2,1,0:T(8,128)(2,1)S(1)} %get-tuple-element.28), channel_id=2, replica_groups=mesh['lat'=32,'qa'=4,'qb'=4] {'qa'}, dimensions={0}, use_global_device_ids=true | all-gather | bytes 655360 | tf_op jit(solution)/shard_map/all_gather | solution.py:582
  71.5 5.8 %all-to-all-done.1 = bf16[128,8,256]{2,1,0:T(8,128)(2,1)S(1)} async-done(((bf16[128,8,256]{2,1,0:T(8,128)(2,1)}), bf16[128,8,256]{2,1,0:T(8,128)(2,1)S(1)}, u32[]{:S(2)}, u32[]{:S(2)}) %all-to-all-start.1) | async-done | bytes 524320 | tf_op jit(solution)/shard_map/all_to_all | solution.py:527
  77.3 2.1 shard_map.77
  79.4 6.5 %all-to-all-start.2 = ((bf16[128,8,256]{2,1,0:T(8,128)(2,1)}), bf16[128,8,256]{2,1,0:T(8,128)(2,1)S(1)}, u32[]{:S(2)}, u32[]{:S(2)}) async-start(bf16[128,8,256]{2,1,0:T(8,128)(2,1)} %bitcast.5), calls=%async_computation.2 | async-start | bytes 1048576 | tf_op jit(solution)/shard_map/all_to_all | solution.py:527
  85.9 1.1 shard_map.80
  87.0 1.0 copy-done.8
  88.9 12.8 %all-gather.1 = bf16[64,24,128]{2,1,0:T(8,128)(2,1)S(1)} all-gather(bf16[16,24,128]{2,1,0:T(8,128)(2,1)S(1)} %get-tuple-element.32), channel_id=3, replica_groups=mesh['lat'=32,'qa'=4,'qb'=4] {'qa'}, dimensions={0}, use_global_device_ids=true | all-gather | bytes 491520 | tf_op jit(solution)/shard_map/all_gather | solution.py:589
  102.5 3.1 %all-to-all-done.2 = bf16[128,8,256]{2,1,0:T(8,128)(2,1)S(1)} async-done(((bf16[128,8,256]{2,1,0:T(8,128)(2,1)}), bf16[128,8,256]{2,1,0:T(8,128)(2,1)S(1)}, u32[]{:S(2)}, u32[]{:S(2)}) %all-to-all-start.2) | async-done | bytes 524320 | tf_op jit(solution)/shard_map/all_to_all | solution.py:527
  105.6 1.0 shard_map.79
  106.6 30.1 %all_to_all.54 = bf16[128,8,256]{2,1,0:T(8,128)(2,1)S(1)} all-to-all(bf16[128,8,256]{2,1,0:T(8,128)(2,1)S(1)} %bitcast.16), channel_id=1, replica_groups=mesh['lat'=32,'qa'=4,'qb'=4] {'lat','qb'}, dimensions={0} | all-to-all | bytes 1048576 | tf_op jit(solution)/shard_map/all_to_all | solution.py:527
  136.7 1.6 shard_map.81
  138.3 28.7 %all_to_all.55 = bf16[128,8,256]{2,1,0:T(8,128)(2,1)S(1)} all-to-all(bf16[128,8,256]{2,1,0:T(8,128)(2,1)S(1)} %bitcast.18), channel_id=1, replica_groups=mesh['lat'=32,'qa'=4,'qb'=4] {'lat','qa'}, dimensions={0} | all-to-all | bytes 1048576 | tf_op jit(solution)/shard_map/all_to_all | solution.py:527
  167.0 2.6 %shard_map.82 = bf16[16,80,256]{2,1,0:T(8,128)(2,1)} custom-call(bf16[512,768]{1,0:T(8,128)(2,1)S(1)} %copy-done.3, bf16[1024,256]{1,0:T(8,128)(2,1)S(1)} %bitcast.15, bf16[1024,384]{1,0:T(8,128)(2,1)S(1)} %copy-done.5), custom_call_target="tpu_custom_call" | custom-call | flops 1000000000 | bytes 2752512 | tf_op jit(solution)/shard_map/pallas_call | solution.py:26
  169.6 6.4 %all-to-all-start.5 = ((bf16[16,80,256]{2,1,0:T(8,128)(2,1)}), bf16[16,80,256]{2,1,0:T(8,128)(2,1)S(1)}, u32[]{:S(2)}, u32[]{:S(2)}) async-start(bf16[16,80,256]{2,1,0:T(8,128)(2,1)} %shard_map.82), calls=%async_computation.5 | async-start | bytes 1310720 | tf_op jit(solution)/shard_map/all_to_all | solution.py:527
  176.4 20.1 %all-to-all-done.5.x_ref = bf16[16,80,256]{2,1,0:T(8,128)(2,1)S(1)} async-done(((bf16[16,80,256]{2,1,0:T(8,128)(2,1)}), bf16[16,80,256]{2,1,0:T(8,128)(2,1)S(1)}, u32[]{:S(2)}, u32[]{:S(2)}) %all-to-all-start.5) | async-done | bytes 655392 | tf_op jit(solution)/shard_map/all_to_all | solution.py:527
  196.5 4.6 %collective-permute-start = (bf16[4,80,128]{2,1,0:T(8,128)(2,1)S(1)}, bf16[4,80,128]{2,1,0:T(8,128)(2,1)S(1)}, u32[]{:S(2)}, u32[]{:S(2)}) collective-permute-start(bf16[4,80,128]{2,1,0:T(8,128)(2,1)S(1)} %get-tuple-element.42), channel_id=1, source_target_pairs={{0,16},{16,32},{32,48},{48,64},{64,80},{80,96},{96,112},{112,128},... | collective-permute-start | bytes 245768 | tf_op jit(solution)/shard_map/ppermute | solution.py:611
  201.1 4.1 %collective-permute-start.1 = (bf16[4,80,128]{2,1,0:T(8,128)(2,1)S(1)}, bf16[4,80,128]{2,1,0:T(8,128)(2,1)S(1)}, u32[]{:S(2)}, u32[]{:S(2)}) collective-permute-start(bf16[4,80,128]{2,1,0:T(8,128)(2,1)S(1)} %get-tuple-element.41), channel_id=1, source_target_pairs={{16,0},{32,16},{48,32},{64,48},{80,64},{96,80},{112,96},{128,112},... | collective-permute-start | bytes 245768 | tf_op jit(solution)/shard_map/ppermute | solution.py:612
  205.2 2.0 shard_map.83
  207.6 5.3 %shard_map.84 = bf16[64,48,256]{2,1,0:T(8,128)(2,1)} custom-call(s32[2]{0:T(128)S(1)} %add_convert_fusion.ends_ref, bf16[4,768,256]{2,1,0:T(8,128)(2,1)S(1)} %get-tuple-element.38.f_ref, bf16[4,192,256]{2,1,0:T(8,128)(2,1)S(1)} %get-tuple-element.39.side_ref, bf16[4,80,128]{2,1,0:T(8,128)(2,1)S(1)} %collective-permute-done.up_ref, ...), custom_call_target="tpu_custom_call" | custom-call | flops 10000000000 | bytes 5477384 | tf_op jit(solution)/shard_map/pallas_call | solution.py:26
  (49 shorter events, 3.3 us)
Async XLA Ops:
  3.3 13.3 %copy-start.12 = (f32[384]{0:T(512)S(1)}, f32[384]{0:T(512)}, u32[]{:S(2)}) copy-start(f32[384]{0:T(512)} %constant.216.clone) | copy-start | bytes 4612
  3.3 30.9 %all-to-all-start = ((bf16[16,200,128]{2,1,0:T(8,128)(2,1)}), bf16[16,200,128]{2,1,0:T(8,128)(2,1)S(1)}, u32[]{:S(2)}, u32[]{:S(2)}) async-start(bf16[16,200,128]{2,1,0:T(8,128)(2,1)} %shard_map.74), calls=%async_computation | async-start | bytes 1638400 | tf_op jit(solution)/shard_map/all_to_all | solution.py:527
  25.8 0.9 copy-start.6
  28.7 0.9 copy-start.2
  36.7 0.9 copy-start.4
  37.6 39.7 %copy-start.7 = (bf16[3,384,384]{2,1,0:T(8,128)(2,1)S(1)}, bf16[3,384,384]{2,1,0:T(8,128)(2,1)}, u32[]{:S(2)}) copy-start(bf16[3,384,384]{2,1,0:T(8,128)(2,1)} %copy-done.6) | copy-start | bytes 2654212
  37.6 39.7 %all-to-all-start.1 = ((bf16[128,8,256]{2,1,0:T(8,128)(2,1)}), bf16[128,8,256]{2,1,0:T(8,128)(2,1)S(1)}, u32[]{:S(2)}, u32[]{:S(2)}) async-start(bf16[128,8,256]{2,1,0:T(8,128)(2,1)} %bitcast.2), calls=%async_computation.1 | async-start | bytes 1048576 | tf_op jit(solution)/shard_map/all_to_all | solution.py:527
  77.3 8.6 %copy-start = (bf16[384,1024]{1,0:T(8,128)(2,1)S(1)}, bf16[384,1024]{1,0:T(8,128)(2,1)}, u32[]{:S(2)}) copy-start(bf16[384,1024]{1,0:T(8,128)(2,1)} %u_ref.1) | copy-start | bytes 2359300
  77.3 8.6 %copy-start.1 = (bf16[9,64,64]{2,1,0:T(8,128)(2,1)S(1)}, bf16[9,64,64]{2,1,0:T(8,128)(2,1)}, u32[]{:S(2)}) copy-start(bf16[9,64,64]{2,1,0:T(8,128)(2,1)} %w_ref.1) | copy-start | bytes 221188
  79.4 26.2 %all-to-all-start.2 = ((bf16[128,8,256]{2,1,0:T(8,128)(2,1)}), bf16[128,8,256]{2,1,0:T(8,128)(2,1)S(1)}, u32[]{:S(2)}, u32[]{:S(2)}) async-start(bf16[128,8,256]{2,1,0:T(8,128)(2,1)} %bitcast.5), calls=%async_computation.2 | async-start | bytes 1048576 | tf_op jit(solution)/shard_map/all_to_all | solution.py:527
  87.0 1.0 copy-start.8
  88.0 0.9 copy-start.10
  136.7 30.3 %copy-start.3 = (bf16[512,768]{1,0:T(8,128)(2,1)S(1)}, bf16[512,768]{1,0:T(8,128)(2,1)}, u32[]{:S(2)}) copy-start(bf16[512,768]{1,0:T(8,128)(2,1)} %copy-done.2) | copy-start | bytes 2359300
  136.7 30.3 %copy-start.5 = (bf16[1024,384]{1,0:T(8,128)(2,1)S(1)}, bf16[1024,384]{1,0:T(8,128)(2,1)}, u32[]{:S(2)}) copy-start(bf16[1024,384]{1,0:T(8,128)(2,1)} %copy-done.4) | copy-start | bytes 2359300
  167.0 9.0 %copy-start.14 = (f32[64]{0:T(128)S(1)}, f32[64]{0:T(128)}, u32[]{:S(2)}) copy-start(f32[64]{0:T(128)} %param.10) | copy-start | bytes 772
  167.0 9.1 %copy-start.13 = (f32[64]{0:T(128)S(1)}, f32[64]{0:T(128)}, u32[]{:S(2)}) copy-start(f32[64]{0:T(128)} %param.12) | copy-start | bytes 772
  169.6 35.6 %copy-start.9 = (bf16[512,1024]{1,0:T(8,128)(2,1)S(1)}, bf16[512,1024]{1,0:T(8,128)(2,1)}, u32[]{:S(2)}) copy-start(bf16[512,1024]{1,0:T(8,128)(2,1)} %copy-done.8) | copy-start | bytes 3145732
  169.6 26.9 %all-to-all-start.5 = ((bf16[16,80,256]{2,1,0:T(8,128)(2,1)}), bf16[16,80,256]{2,1,0:T(8,128)(2,1)S(1)}, u32[]{:S(2)}, u32[]{:S(2)}) async-start(bf16[16,80,256]{2,1,0:T(8,128)(2,1)} %shard_map.82), calls=%async_computation.5 | async-start | bytes 1310720 | tf_op jit(solution)/shard_map/all_to_all | solution.py:527
  196.5 10.7 %collective-permute-start = (bf16[4,80,128]{2,1,0:T(8,128)(2,1)S(1)}, bf16[4,80,128]{2,1,0:T(8,128)(2,1)S(1)}, u32[]{:S(2)}, u32[]{:S(2)}) collective-permute-start(bf16[4,80,128]{2,1,0:T(8,128)(2,1)S(1)} %get-tuple-element.42), channel_id=1, source_target_pairs={{0,16},{16,32},{32,48},{48,64},{64,80},{80,96},{96,112},{112,128},... | collective-permute-start | bytes 245768 | tf_op jit(solution)/shard_map/ppermute | solution.py:611
  201.1 6.5 %copy-start.11 = (bf16[256,1408]{1,0:T(8,128)(2,1)S(1)}, bf16[256,1408]{1,0:T(8,128)(2,1)}, u32[]{:S(2)}) copy-start(bf16[256,1408]{1,0:T(8,128)(2,1)} %copy-done.10) | copy-start | bytes 2162692
  201.1 6.5 %collective-permute-start.1 = (bf16[4,80,128]{2,1,0:T(8,128)(2,1)S(1)}, bf16[4,80,128]{2,1,0:T(8,128)(2,1)S(1)}, u32[]{:S(2)}, u32[]{:S(2)}) collective-permute-start(bf16[4,80,128]{2,1,0:T(8,128)(2,1)S(1)} %get-tuple-element.41), channel_id=1, source_target_pairs={{16,0},{32,16},{48,32},{64,48},{80,64},{96,80},{112,96},{128,112},... | collective-permute-start | bytes 245768 | tf_op jit(solution)/shard_map/ppermute | solution.py:612

commit v7 on v6

--- a/solution.py
+++ b/solution.py
@@ -176,8 +176,7 @@
         ).astype(bf16)
 
 
-def dft_kernel(c_ref, x_ref, w_ref, s_ref, state_ref, *rest):
-    *part_refs, y_ref = rest
+def dft_kernel(c_ref, x_ref, w_ref, s_ref, state_ref, part_ref, y_ref):
     for q in range(16):
         cells = x_ref[q].astype(f32)
         first, last = cells[0:72], cells[72:144]
@@ -185,8 +184,7 @@
         state_ref[rows, 0:128] = first[:64].astype(bf16)
         state_ref[rows, 128:256] = reopen_cells(first, last).astype(bf16)
         state_ref[rows, 256:384] = last[:64].astype(bf16)
-        for part, ref in enumerate(part_refs):
-            ref[q] = cells[144 + 32 * part : min(176 + 32 * part, 200)].astype(bf16)
+        part_ref[q] = cells[144:200].astype(bf16)
     for t in range(3):
         for j in (6, 7):
             y_ref[t, mode_row(j), :] = jnp.zeros((128, 128), f32)
@@ -272,15 +270,16 @@
     close_modes(out_ref, s_ref)
 
 
-def mix_weight_kernel(w_ref, v_ref, o_ref, full_ref):
+def mix_weight_kernel(place_ref, a_ref, b_ref, c_ref, d_ref, o_ref, full_ref, w_ref):
+    for i, ref in enumerate((a_ref, b_ref, c_ref, d_ref)):
+        w_ref[(place_ref[0] + 4 - i) % 4] = ref[...].astype(f32)
     spread = widen()
     o_ref[...] = jnp.zeros(o_ref.shape, bf16)
     for r in range(3):
         for og in range(3):
             for it in range(3):
                 a, i = weight_tile(r, og, it)
-                part = (w_ref, v_ref)[i // 4][a].astype(f32)
-                full_ref[:, og, :, pl.ds(it * 128, 128)] = part[:, i % 4 * 8 : i % 4 * 8 + 8]
+                full_ref[:, og, :, pl.ds(it * 128, 128)] = w_ref[a, :, 8 * i : 8 * i + 8, :]
         part = full_ref[...].reshape(384, 384).astype(bf16)
         wide = dot(part, spread).astype(bf16)
         for b in range(4):
@@ -555,9 +554,9 @@
     )
     scale = (jnp.sin(colatitude) * (math.pi / 384) * (2.0 * math.pi / 1024))[None, :]
     scratch = [pltpu.VMEM((3, 1024, 128), f32)] * 2
-    spectra, state, *own = call(
+    spectra, state, own = call(
         dft_kernel,
-        (shape((1024, 256)), shape((1024, 384)), shape((16, 32, 128)), shape((16, 24, 128))),
+        (shape((1024, 256)), shape((1024, 384)), shape((16, 56, 128))),
         forward,
         arrived,
         scale,
@@ -579,15 +578,17 @@
         scratch=[pltpu.VMEM((9, 256, 128), f32)],
         flops=2 * 10**9,
     )
-    gathered = lax.all_gather(own[0], "qa", axis=0)
-    coeffs, gathered, rest = lax.optimization_barrier((coeffs, gathered, own[1]))
+    gathered = [own] + [
+        lax.ppermute(own, "qa", [(i, (i + turn) % 4) for i in range(4)]) for turn in (1, 2, 3)
+    ]
     degrees = exchange(coeffs, ("lat", "qb"))
     mixer = call(
         mix_weight_kernel,
         shape((3, 512, 512)),
-        gathered,
-        lax.all_gather(rest, "qa", axis=0),
-        scratch=[pltpu.VMEM((16, 3, 8, 384), f32)],
+        lax.axis_index("qa").reshape(1).astype(jnp.int32),
+        *gathered,
+        smem=(0,),
+        scratch=[pltpu.VMEM((16, 3, 8, 384), f32), pltpu.VMEM((4, 16, 56, 128), f32)],
         flops=10**9,
     )
     mixed = call(mix_kernel, shape((1024, 256)), degrees, mixer, scratch=scratch, flops=10**9)

time: 213 us -> 213 us (level)
  blocking collectives: 85.7 us -> 99.9 us
  starting transfers between devices: 54.2 us -> 44 us
  waiting for transfers between devices: 34 us -> 31.2 us
    all_to_all x2 -> x3, blocking collectives: 58.8 us -> 99.9 us  [exchange(): return lax.all_to_all(x, axes, 0, 0, tiled=True)]
    all_gather x2 -> x0, blocking collectives: 26.9 us -> none  [the longest x1 14.1 us: local(): gathered = lax.all_gather(own[0], 'qa', axis=0)]
    all_to_all x4 -> x3, starting transfers between devices: 45.5 us -> 25.7 us  [exchange(): return lax.all_to_all(x, axes, 0, 0, tiled=True)]
    ppermute x0 -> x3, starting transfers between devices: none -> 9.69 us  [local(): lax.ppermute(own, 'qa', [(i, (i + turn) % 4) for i in range(4)])]
    all_to_all x4 -> x3, waiting for transfers between devices: 33.7 us -> 25.3 us  [exchange(): return lax.all_to_all(x, axes, 0, 0, tiled=True)]
    ppermute x0 -> x3, waiting for transfers between devices: none -> 5.53 us  [local(): lax.ppermute(own, 'qa', [(i, (i + turn) % 4) for i in range(4)])]
    unnamed x30 -> x32, local copies, waits for them, and re-layouts: 4.63 us -> 3.69 us
  transfers between devices with their start and end apart: 6 -> 8, of which waited for: 5 -> 6; matrix products, arithmetic and copies ran while one was open for 3% -> 3% of each run, Pallas kernels for 5% -> 5%
where the time goes in v7:
time: 213 us
  blocking collectives  99.9 us (47%)
  starting transfers between devices  44 us (21%)
  waiting for transfers between devices  31.2 us (15%)
  Pallas kernels  27.5 us (13%)
  other arithmetic  5.37 us (3%)
  local copies, waits for them, and re-layouts  4.21 us (2%)
    all_to_all x3, blocking collectives, exchange(): return lax.all_to_all(x, axes, 0, 0, tiled=True)  99.9 us
    pallas_call x12, Pallas kernels, call(): pl.pallas_call(kernel, out_shape=out, in_specs=space, out_specs=jax.tree....  27.5 us
    all_to_all x3, starting transfers between devices, exchange(): return lax.all_to_all(x, axes, 0, 0, tiled=True)  25.7 us
    all_to_all x3, waiting for transfers between devices, exchange(): return lax.all_to_all(x, axes, 0, 0, tiled=True)  25.3 us
    ppermute x3, starting transfers between devices, local(): lax.ppermute(own, 'qa', [(i, (i + turn) % 4) for i in range(4)])  9.69 us
    ppermute x3, waiting for transfers between devices, local(): lax.ppermute(own, 'qa', [(i, (i + turn) % 4) for i in range(4)])  5.53 us
    ppermute x1, starting transfers between devices, local(): up = lax.ppermute(last_row, 'lat', [(i, i + 1) for i in range(count - 1)])  4.57 us
  transfers between devices with their start and end apart: 8, of which 6 were waited for; matrix products, arithmetic and copies ran while one was open for 3% of the time, Pallas kernels for 5%

profile of v7, /device:TPU:8, one launch (start us, length us, event | category | flops | bytes accessed | tf_op | source)
XLA Modules:
  0.0 212.6 jit_solution(10441499301371045964)
XLA Ops:
  0.0 3.3 %shard_map.74 = bf16[16,200,128]{2,1,0:T(8,128)(2,1)} custom-call(bf16[12,64,384]{2,1,0:T(8,128)(2,1)} %x_far.1, bf16[12,24,384]{2,1,0:T(8,128)(2,1)} %w_far.1), custom_call_target="tpu_custom_call" | custom-call | flops 1000000000 | bytes 1630208 | tf_op jit(solution)/shard_map/pallas_call | solution.py:26
  3.3 12.9 %all-to-all-start = ((bf16[16,200,128]{2,1,0:T(8,128)(2,1)}), bf16[16,200,128]{2,1,0:T(8,128)(2,1)S(1)}, u32[]{:S(2)}, u32[]{:S(2)}) async-start(bf16[16,200,128]{2,1,0:T(8,128)(2,1)} %shard_map.74), calls=%async_computation | async-start | bytes 1638400 | tf_op jit(solution)/shard_map/all_to_all | solution.py:526
  17.1 1.6 fusion.6
  18.7 1.6 sine_multiply_fusion
  20.3 1.4 multiply_sine_fusion
  21.8 4.0 %shard_map.75.l_ref = bf16[3,384,384]{2,1,0:T(8,128)(2,1)S(1)} custom-call(f32[8,128]{1,0:T(8,128)S(1)} %broadcast_in_dim.30.order_ref, f32[8,384]{1,0:T(8,128)S(1)} %broadcast_in_dim.31.cosine_ref, f32[8,384]{1,0:T(8,128)S(1)} %exponential_select_fusion.start_ref), custom_call_target="tpu_custom_call" | custom-call | flops 4000000000 | bytes 913408 | tf_op jit(solution)/shard_map/pallas_call | solution.py:26
  25.8 0.9 copy-done.6
  26.8 2.0 shard_map.73
  29.6 4.6 %all-to-all-done.x_ref = bf16[16,200,128]{2,1,0:T(8,128)(2,1)S(1)} async-done(((bf16[16,200,128]{2,1,0:T(8,128)(2,1)}), bf16[16,200,128]{2,1,0:T(8,128)(2,1)S(1)}, u32[]{:S(2)}, u32[]{:S(2)}) %all-to-all-start) | async-done | bytes 819232 | tf_op jit(solution)/shard_map/all_to_all | solution.py:526
  34.3 1.7 shard_map.76
  35.9 39.4 %all_to_all.54 = bf16[128,8,256]{2,1,0:T(8,128)(2,1)S(1)} all-to-all(bf16[128,8,256]{2,1,0:T(8,128)(2,1)S(1)} %bitcast.12), channel_id=1, replica_groups=mesh['lat'=32,'qa'=4,'qb'=4] {'lat','qa'}, dimensions={0} | all-to-all | bytes 1048576 | tf_op jit(solution)/shard_map/all_to_all | solution.py:526
  75.3 2.1 shard_map.77
  77.4 6.5 %all-to-all-start.2 = ((bf16[128,8,256]{2,1,0:T(8,128)(2,1)}), bf16[128,8,256]{2,1,0:T(8,128)(2,1)S(1)}, u32[]{:S(2)}, u32[]{:S(2)}) async-start(bf16[128,8,256]{2,1,0:T(8,128)(2,1)} %bitcast.4), calls=%async_computation.2 | async-start | bytes 1048576 | tf_op jit(solution)/shard_map/all_to_all | solution.py:526
  83.9 2.5 %collective-permute-start = (bf16[16,56,128]{2,1,0:T(8,128)(2,1)S(1)}, bf16[16,56,128]{2,1,0:T(8,128)(2,1)S(1)}, u32[]{:S(2)}, u32[]{:S(2)}) collective-permute-start(bf16[16,56,128]{2,1,0:T(8,128)(2,1)S(1)} %get-tuple-element.24.a_ref), channel_id=1, source_target_pairs={{0,4},{4,8},{8,12},{12,0},{1,5},{5,9},{9,13},{13,1},{2,6},{6,10},{... | collective-permute-start | bytes 688136 | tf_op jit(solution)/shard_map/ppermute | solution.py:582
  86.4 4.9 %collective-permute-start.1 = (bf16[16,56,128]{2,1,0:T(8,128)(2,1)S(1)}, bf16[16,56,128]{2,1,0:T(8,128)(2,1)S(1)}, u32[]{:S(2)}, u32[]{:S(2)}) collective-permute-start(bf16[16,56,128]{2,1,0:T(8,128)(2,1)S(1)} %get-tuple-element.24.a_ref), channel_id=1, source_target_pairs={{0,8},{4,12},{8,0},{12,4},{1,9},{5,13},{9,1},{13,5},{2,10},{6,14},... | collective-permute-start | bytes 688136 | tf_op jit(solution)/shard_map/ppermute | solution.py:582
  91.3 2.3 %collective-permute-start.2 = (bf16[16,56,128]{2,1,0:T(8,128)(2,1)S(1)}, bf16[16,56,128]{2,1,0:T(8,128)(2,1)S(1)}, u32[]{:S(2)}, u32[]{:S(2)}) collective-permute-start(bf16[16,56,128]{2,1,0:T(8,128)(2,1)S(1)} %get-tuple-element.24.a_ref), channel_id=1, source_target_pairs={{0,12},{4,0},{8,4},{12,8},{1,13},{5,1},{9,5},{13,9},{2,14},{6,2},{... | collective-permute-start | bytes 688136 | tf_op jit(solution)/shard_map/ppermute | solution.py:582
  93.6 1.1 shard_map.80
  94.8 1.0 copy-done.9
  96.6 3.3 %collective-permute-done.1.c_ref = bf16[16,56,128]{2,1,0:T(8,128)(2,1)S(1)} collective-permute-done((bf16[16,56,128]{2,1,0:T(8,128)(2,1)S(1)}, bf16[16,56,128]{2,1,0:T(8,128)(2,1)S(1)}, u32[]{:S(2)}, u32[]{:S(2)}) %collective-permute-start.1) | collective-permute-done | bytes 229408 | tf_op jit(solution)/shard_map/ppermute | solution.py:582
  99.9 2.2 %collective-permute-done.2.d_ref = bf16[16,56,128]{2,1,0:T(8,128)(2,1)S(1)} collective-permute-done((bf16[16,56,128]{2,1,0:T(8,128)(2,1)S(1)}, bf16[16,56,128]{2,1,0:T(8,128)(2,1)S(1)}, u32[]{:S(2)}, u32[]{:S(2)}) %collective-permute-start.2) | collective-permute-done | bytes 229408 | tf_op jit(solution)/shard_map/ppermute | solution.py:582
  102.1 0.9 shard_map.78.w_ref
  103.6 1.0 shard_map.79
  104.7 32.6 %all_to_all.55 = bf16[128,8,256]{2,1,0:T(8,128)(2,1)S(1)} all-to-all(bf16[128,8,256]{2,1,0:T(8,128)(2,1)S(1)} %bitcast.14), channel_id=1, replica_groups=mesh['lat'=32,'qa'=4,'qb'=4] {'lat','qb'}, dimensions={0} | all-to-all | bytes 1048576 | tf_op jit(solution)/shard_map/all_to_all | solution.py:526
  137.3 1.6 shard_map.81
  138.9 27.9 %all_to_all.56 = bf16[128,8,256]{2,1,0:T(8,128)(2,1)S(1)} all-to-all(bf16[128,8,256]{2,1,0:T(8,128)(2,1)S(1)} %bitcast.16), channel_id=1, replica_groups=mesh['lat'=32,'qa'=4,'qb'=4] {'lat','qa'}, dimensions={0} | all-to-all | bytes 1048576 | tf_op jit(solution)/shard_map/all_to_all | solution.py:526
  166.8 2.6 %shard_map.82 = bf16[16,80,256]{2,1,0:T(8,128)(2,1)} custom-call(bf16[512,768]{1,0:T(8,128)(2,1)S(1)} %copy-done.3, bf16[1024,256]{1,0:T(8,128)(2,1)S(1)} %bitcast.13, bf16[1024,384]{1,0:T(8,128)(2,1)S(1)} %copy-done.5), custom_call_target="tpu_custom_call" | custom-call | flops 1000000000 | bytes 2752512 | tf_op jit(solution)/shard_map/pallas_call | solution.py:26
  169.3 6.4 %all-to-all-start.5 = ((bf16[16,80,256]{2,1,0:T(8,128)(2,1)}), bf16[16,80,256]{2,1,0:T(8,128)(2,1)S(1)}, u32[]{:S(2)}, u32[]{:S(2)}) async-start(bf16[16,80,256]{2,1,0:T(8,128)(2,1)} %shard_map.82), calls=%async_computation.5 | async-start | bytes 1310720 | tf_op jit(solution)/shard_map/all_to_all | solution.py:526
  176.1 20.1 %all-to-all-done.5.x_ref = bf16[16,80,256]{2,1,0:T(8,128)(2,1)S(1)} async-done(((bf16[16,80,256]{2,1,0:T(8,128)(2,1)}), bf16[16,80,256]{2,1,0:T(8,128)(2,1)S(1)}, u32[]{:S(2)}, u32[]{:S(2)}) %all-to-all-start.5) | async-done | bytes 655392 | tf_op jit(solution)/shard_map/all_to_all | solution.py:526
  196.2 4.6 %collective-permute-start.3 = (bf16[4,80,128]{2,1,0:T(8,128)(2,1)S(1)}, bf16[4,80,128]{2,1,0:T(8,128)(2,1)S(1)}, u32[]{:S(2)}, u32[]{:S(2)}) collective-permute-start(bf16[4,80,128]{2,1,0:T(8,128)(2,1)S(1)} %get-tuple-element.34), channel_id=1, source_target_pairs={{0,16},{16,32},{32,48},{48,64},{64,80},{80,96},{96,112},{112,128},... | collective-permute-start | bytes 245768 | tf_op jit(solution)/shard_map/ppermute | solution.py:612
  200.8 4.1 %collective-permute-start.4 = (bf16[4,80,128]{2,1,0:T(8,128)(2,1)S(1)}, bf16[4,80,128]{2,1,0:T(8,128)(2,1)S(1)}, u32[]{:S(2)}, u32[]{:S(2)}) collective-permute-start(bf16[4,80,128]{2,1,0:T(8,128)(2,1)S(1)} %get-tuple-element.33), channel_id=1, source_target_pairs={{16,0},{32,16},{48,32},{64,48},{80,64},{96,80},{112,96},{128,112},... | collective-permute-start | bytes 245768 | tf_op jit(solution)/shard_map/ppermute | solution.py:613
  204.9 2.0 shard_map.83
  207.3 5.3 %shard_map.84 = bf16[64,48,256]{2,1,0:T(8,128)(2,1)} custom-call(s32[2]{0:T(128)S(1)} %add_convert_fusion.ends_ref, bf16[4,768,256]{2,1,0:T(8,128)(2,1)S(1)} %get-tuple-element.30.f_ref, bf16[4,192,256]{2,1,0:T(8,128)(2,1)S(1)} %get-tuple-element.31.side_ref, bf16[4,80,128]{2,1,0:T(8,128)(2,1)S(1)} %collective-permute-done.3.up_ref, ...), custom_call_target="tpu_custom_call" | custom-call | flops 10000000000 | bytes 5477384 | tf_op jit(solution)/shard_map/pallas_call | solution.py:26
  (54 shorter events, 4.0 us)
Async XLA Ops:
  3.3 13.3 %copy-start.13 = (f32[384]{0:T(512)S(1)}, f32[384]{0:T(512)}, u32[]{:S(2)}) copy-start(f32[384]{0:T(512)} %constant.216.clone) | copy-start | bytes 4612
  3.3 30.9 %all-to-all-start = ((bf16[16,200,128]{2,1,0:T(8,128)(2,1)}), bf16[16,200,128]{2,1,0:T(8,128)(2,1)S(1)}, u32[]{:S(2)}, u32[]{:S(2)}) async-start(bf16[16,200,128]{2,1,0:T(8,128)(2,1)} %shard_map.74), calls=%async_computation | async-start | bytes 1638400 | tf_op jit(solution)/shard_map/all_to_all | solution.py:526
  25.8 0.9 copy-start.6
  28.8 0.9 copy-start.2
  34.3 41.1 %copy-start.7 = (bf16[3,384,384]{2,1,0:T(8,128)(2,1)S(1)}, bf16[3,384,384]{2,1,0:T(8,128)(2,1)}, u32[]{:S(2)}) copy-start(bf16[3,384,384]{2,1,0:T(8,128)(2,1)} %copy-done.6) | copy-start | bytes 2654212
  35.9 39.4 %copy-start.4 = (bf16[1024,384]{1,0:T(8,128)(2,1)}, bf16[1024,384]{1,0:T(8,128)(2,1)S(1)}, u32[]{:S(2)}) copy-start(bf16[1024,384]{1,0:T(8,128)(2,1)S(1)} %get-tuple-element.28.state_ref) | copy-start | bytes 2359300
  75.3 18.3 %copy-start = (bf16[384,1024]{1,0:T(8,128)(2,1)S(1)}, bf16[384,1024]{1,0:T(8,128)(2,1)}, u32[]{:S(2)}) copy-start(bf16[384,1024]{1,0:T(8,128)(2,1)} %u_ref.1) | copy-start | bytes 2359300
  75.3 18.3 %copy-start.1 = (bf16[9,64,64]{2,1,0:T(8,128)(2,1)S(1)}, bf16[9,64,64]{2,1,0:T(8,128)(2,1)}, u32[]{:S(2)}) copy-start(bf16[9,64,64]{2,1,0:T(8,128)(2,1)} %w_ref.1) | copy-start | bytes 221188
  77.4 26.2 %all-to-all-start.2 = ((bf16[128,8,256]{2,1,0:T(8,128)(2,1)}), bf16[128,8,256]{2,1,0:T(8,128)(2,1)S(1)}, u32[]{:S(2)}, u32[]{:S(2)}) async-start(bf16[128,8,256]{2,1,0:T(8,128)(2,1)} %bitcast.4), calls=%async_computation.2 | async-start | bytes 1048576 | tf_op jit(solution)/shard_map/all_to_all | solution.py:526
  83.9 12.7 %collective-permute-start = (bf16[16,56,128]{2,1,0:T(8,128)(2,1)S(1)}, bf16[16,56,128]{2,1,0:T(8,128)(2,1)S(1)}, u32[]{:S(2)}, u32[]{:S(2)}) collective-permute-start(bf16[16,56,128]{2,1,0:T(8,128)(2,1)S(1)} %get-tuple-element.24.a_ref), channel_id=1, source_target_pairs={{0,4},{4,8},{8,12},{12,0},{1,5},{5,9},{9,13},{13,1},{2,6},{6,10},{... | collective-permute-start | bytes 688136 | tf_op jit(solution)/shard_map/ppermute | solution.py:582
  86.4 13.5 %collective-permute-start.1 = (bf16[16,56,128]{2,1,0:T(8,128)(2,1)S(1)}, bf16[16,56,128]{2,1,0:T(8,128)(2,1)S(1)}, u32[]{:S(2)}, u32[]{:S(2)}) collective-permute-start(bf16[16,56,128]{2,1,0:T(8,128)(2,1)S(1)} %get-tuple-element.24.a_ref), channel_id=1, source_target_pairs={{0,8},{4,12},{8,0},{12,4},{1,9},{5,13},{9,1},{13,5},{2,10},{6,14},... | collective-permute-start | bytes 688136 | tf_op jit(solution)/shard_map/ppermute | solution.py:582
  91.3 10.8 %collective-permute-start.2 = (bf16[16,56,128]{2,1,0:T(8,128)(2,1)S(1)}, bf16[16,56,128]{2,1,0:T(8,128)(2,1)S(1)}, u32[]{:S(2)}, u32[]{:S(2)}) collective-permute-start(bf16[16,56,128]{2,1,0:T(8,128)(2,1)S(1)} %get-tuple-element.24.a_ref), channel_id=1, source_target_pairs={{0,12},{4,0},{8,4},{12,8},{1,13},{5,1},{9,5},{13,9},{2,14},{6,2},{... | collective-permute-start | bytes 688136 | tf_op jit(solution)/shard_map/ppermute | solution.py:582
  94.7 1.0 copy-start.9
  95.7 0.9 copy-start.11
  103.6 33.7 %copy-start.8 = (bf16[3,384,384]{2,1,0:T(8,128)(2,1)S(1)}, bf16[3,384,384]{2,1,0:T(8,128)(2,1)}, u32[]{:S(2)}) copy-start(bf16[3,384,384]{2,1,0:T(8,128)(2,1)} %copy-done.6) | copy-start | bytes 2654212
  137.3 29.4 %copy-start.3 = (bf16[512,768]{1,0:T(8,128)(2,1)S(1)}, bf16[512,768]{1,0:T(8,128)(2,1)}, u32[]{:S(2)}) copy-start(bf16[512,768]{1,0:T(8,128)(2,1)} %copy-done.2) | copy-start | bytes 2359300
  137.3 29.4 %copy-start.5 = (bf16[1024,384]{1,0:T(8,128)(2,1)S(1)}, bf16[1024,384]{1,0:T(8,128)(2,1)}, u32[]{:S(2)}) copy-start(bf16[1024,384]{1,0:T(8,128)(2,1)} %copy-done.4) | copy-start | bytes 2359300
  166.7 9.0 %copy-start.15 = (f32[64]{0:T(128)S(1)}, f32[64]{0:T(128)}, u32[]{:S(2)}) copy-start(f32[64]{0:T(128)} %param.10) | copy-start | bytes 772
  166.7 9.1 %copy-start.14 = (f32[64]{0:T(128)S(1)}, f32[64]{0:T(128)}, u32[]{:S(2)}) copy-start(f32[64]{0:T(128)} %param.12) | copy-start | bytes 772
  169.3 35.6 %copy-start.10 = (bf16[512,1024]{1,0:T(8,128)(2,1)S(1)}, bf16[512,1024]{1,0:T(8,128)(2,1)}, u32[]{:S(2)}) copy-start(bf16[512,1024]{1,0:T(8,128)(2,1)} %copy-done.9) | copy-start | bytes 3145732
  169.3 26.9 %all-to-all-start.5 = ((bf16[16,80,256]{2,1,0:T(8,128)(2,1)}), bf16[16,80,256]{2,1,0:T(8,128)(2,1)S(1)}, u32[]{:S(2)}, u32[]{:S(2)}) async-start(bf16[16,80,256]{2,1,0:T(8,128)(2,1)} %shard_map.82), calls=%async_computation.5 | async-start | bytes 1310720 | tf_op jit(solution)/shard_map/all_to_all | solution.py:526
  196.2 10.7 %collective-permute-start.3 = (bf16[4,80,128]{2,1,0:T(8,128)(2,1)S(1)}, bf16[4,80,128]{2,1,0:T(8,128)(2,1)S(1)}, u32[]{:S(2)}, u32[]{:S(2)}) collective-permute-start(bf16[4,80,128]{2,1,0:T(8,128)(2,1)S(1)} %get-tuple-element.34), channel_id=1, source_target_pairs={{0,16},{16,32},{32,48},{48,64},{64,80},{80,96},{96,112},{112,128},... | collective-permute-start | bytes 245768 | tf_op jit(solution)/shard_map/ppermute | solution.py:612
  200.8 6.5 %copy-start.12 = (bf16[256,1408]{1,0:T(8,128)(2,1)S(1)}, bf16[256,1408]{1,0:T(8,128)(2,1)}, u32[]{:S(2)}) copy-start(bf16[256,1408]{1,0:T(8,128)(2,1)} %copy-done.11) | copy-start | bytes 2162692
  200.8 6.5 %collective-permute-start.4 = (bf16[4,80,128]{2,1,0:T(8,128)(2,1)S(1)}, bf16[4,80,128]{2,1,0:T(8,128)(2,1)S(1)}, u32[]{:S(2)}, u32[]{:S(2)}) collective-permute-start(bf16[4,80,128]{2,1,0:T(8,128)(2,1)S(1)} %get-tuple-element.33), channel_id=1, source_target_pairs={{16,0},{32,16},{48,32},{64,48},{80,64},{96,80},{112,96},{128,112},... | collective-permute-start | bytes 245768 | tf_op jit(solution)/shard_map/ppermute | solution.py:613
